TPU v7x, 32 devices: a whole 2x2x4 slice. The times are simulated.
32 devices in a mesh: orb: 4 (over z), space: 8 (over y, x, core).
Axes of the slice: x: 2, y: 2, z: 4, core: 2. Of those that a mesh axis runs over, the one named last changes fastest.
Arguments:
- orbitals: float32 [32, 128, 128], P('orb', 'space'), may hold values from 0 to 0.25
- points: float32 [3, 128, 128], P(None, 'space')
- quad_weight: float32 [128, 128], P('space'), may hold values from 0.5 to 2
- external: float32 [128, 128], P('space'), may hold values from -3 to 1
- screening: float32 [32], replicated, may hold values from 0.05 to 2
- level_index: int32 [32], P('orb'), may hold values from 0 to 31
- near_cells: int32 [128, 27], P('space'), may hold values from -1 to 127, as said below
- far_cells: int32 [128, 42], P('space'), may hold values from -1 to 127, as said below
Outputs:
- new_orbitals: float32 [32, 128, 128], P('orb', 'space')
- hartree: float32 [128, 128], P('space')
Inputs may be any that keep to these rules, and one draw needn't show every extreme that they name: `near_cells`: row t lists distinct cells in increasing order, then -1: every cell of its own plane whose first two box indices differ from those of t by at most one (t itself among them), the cells directly above and below t, and some of the other cells of the two adjacent planes whose first two box indices differ from those of t by at most one. Some row holds 27 cells. `far_cells`: row t lists in increasing order, then -1, all cells of the planes floor(t / 16) - 1 to floor(t / 16) + 1 that are not in row t of near_cells. Some row holds 42 cells.
All inputs are finite; a program needn't handle non-finite values.
Results may differ from a plain program's by a relative error of at most 0.0003.
Values sent between devices are 32-bit elements; how exact they have to be, the bound alone decides.
No kernel may reach another device: no remote copies, remote signals or barrier semaphores. Data moves between devices by JAX's collectives and lax.ppermute only.
A program may use at most 64 MiB of HBM per device.

v0:
```python
import functools
import math

import jax
import jax.numpy as jnp
import numpy as np
from jax import lax
from jax.experimental import pallas as pl
from jax.experimental.pallas import tpu as pltpu
from jax.sharding import PartitionSpec as P

NODES = 4
LANES = 128
PLANE = 16
ROWS = 8
HALF = NODES**3

cell_side = 0.25
soften = 6.25e-06
green_scale = -0.5 / math.pi
log2e = math.log2(math.e)
highest = lax.Precision.HIGHEST

node_set = np.cos((2.0 * np.arange(NODES) + 1.0) * (math.pi / (2.0 * NODES)))
roots = [[node_set[m] for m in range(NODES) if m != a] for a in range(NODES)]
scales = [1.0 / np.prod([node_set[a] - r for r in roots[a]]) for a in range(NODES)]


def basis_rows():
    row = np.arange(ROWS)
    out = []
    for pick in (row // 4, 2 + row // 4, row % 4):
        for k in range(NODES - 1):
            out.append([roots[a][k] for a in pick])
        out.append([scales[a] for a in pick])
    return np.broadcast_to(np.array(out, np.float32)[:, :, None], (12, ROWS, LANES)).copy()


def proxy_table(planes, window):
    offset = 0.5 * (node_set + 1.0)
    p = np.arange(LANES) % HALF
    offs = np.stack([offset[p // 16], offset[p // 4 % 4], offset[p % 4]])
    cells = np.arange(window)
    lows = np.stack([cells % 4, cells // 4 % 4, cells // 16]) * cell_side
    near = lows[:, :, None] + offs[:, None, :] * cell_side
    levels = np.arange(planes)
    lows = np.stack([0 * levels, 0 * levels, levels]) * cell_side
    far = lows[:, :, None] + offs[:, None, :] * np.array([1.0, 1.0, cell_side])[:, None, None]
    table = np.zeros((window + planes, ROWS, LANES), np.float32)
    table[:, :3] = np.moveaxis(np.concatenate([near, far], 1), 0, 1)
    return table


def poly(u, r0, r1, r2, scale):
    return ((u - r0) * (u - r1)) * ((u - r2) * scale)


def weights(cst, x, y, z, lows, sides):
    ux, uy, uz = (
        jnp.broadcast_to(2.0 * (c - lo) / e - 1.0, (ROWS, LANES)) for c, lo, e in zip((x, y, z), lows, sides)
    )
    pz = poly(uz, cst[8], cst[9], cst[10], cst[11])
    pyz = [poly(uy, cst[4 * k], cst[4 * k + 1], cst[4 * k + 2], cst[4 * k + 3]) * pz for k in range(2)]
    parts = []
    for a in range(NODES):
        px = poly(ux, *(float(r) for r in roots[a]), float(scales[a]))
        parts += [px * pyz[0], px * pyz[1]]
    return jnp.concatenate(parts, axis=0)


def twice(w):
    return jnp.concatenate([w, w], axis=0)


def cell_low(cell):
    return [(cell % 4).astype(jnp.float32) * cell_side, (cell // 4 % 4).astype(jnp.float32) * cell_side]


def dot_nt(a, b):
    return lax.dot_general(a, b, (((1,), (1,)), ((), ())), precision=highest, preferred_element_type=jnp.float32)


def gather_parts(block, axis, pairs):
    count = lax.axis_size(axis)
    parts = [block[None]]
    while sum(p.shape[0] for p in parts) < count:
        held = parts[0] if len(parts) == 1 else jnp.concatenate(parts, axis=0)
        have = held.shape[0]
        steps = range(1, 4 if (have > 1 or pairs) and have * 4 <= count else 2)
        parts = [held] + [lax.ppermute(held, axis, [(i, i ^ (have * j)) for i in range(count)]) for j in steps]
    return parts


def gather_list(block, axis):
    parts = gather_parts(block, axis, True)
    return [p[k] for p in parts for k in range(p.shape[0])]


def lay_out(parts, whole):
    at = 0
    for part in parts:
        for k in range(part.shape[0]):
            whole[at + k] = part[k]
        at += part.shape[0]


def target_cell(me, t, groups):
    return t * groups + lax.bitwise_xor(jnp.int32(t) if isinstance(t, int) else t, me)


def split(v):
    high = v.astype(jnp.bfloat16)
    return high, (v - high.astype(jnp.float32)).astype(jnp.bfloat16)


def dot_bf16(a, b):
    return lax.dot_general(a, b, (((1,), (1,)), ((), ())), preferred_element_type=jnp.float32)


def dot_split(v, w):
    vh, vl = split(v)
    wh, wl = split(w)
    rows = v.shape[0]
    both = dot_bf16(jnp.concatenate([vh, vl], axis=0), wh)
    return both[:rows] + both[rows:] + dot_bf16(vh, wl)


def charge_kernel(meta, cst, own, *refs):
    z_low = meta[0].astype(jnp.float32) * cell_side
    fields, out = refs[:-1], refs[-1]
    density = jnp.zeros((PLANE, LANES), jnp.float32)
    for phi in fields:
        for j in range(phi.shape[0]):
            v = phi[j]
            density = density + v * v
    out[:PLANE, :] = density
    acc = jnp.zeros((HALF, LANES), jnp.float32)
    ones = jnp.ones((ROWS, LANES), jnp.float32)
    for c in range(PLANE):
        charge = own[c, 4:5, :] * (2.0 * out[c : c + 1, :])
        out[c : c + 1, :] = charge
        x, y, z = own[c, 0:1, :], own[c, 1:2, :], own[c, 2:3, :]
        low = (cell_side * (c % 4), cell_side * (c // 4), z_low)
        acc = acc + weights(cst, x, y, z, (0.0, 0.0, z_low), (1.0, 1.0, cell_side)) * charge
        moments = dot_nt(ones, twice(weights(cst, x, y, z, low, (cell_side,) * 3) * charge))
        out[PLANE + c : PLANE + c + 1, :] = moments[0:1, :]
    out[2 * PLANE :, :] = dot_nt(ones, twice(acc))


def live_planes(me, planes):
    below = jnp.maximum(me - 1, 0)
    return below, below + jnp.maximum(planes - 2 - me, 0)


def list_sources(me, cell, counts, near, far, planes, table, pts, src, put_near, put_far, put_none, multiple):
    window = 3 * PLANE
    base = (me - 1) * PLANE
    below, n_planes = live_planes(me, planes)
    low_half = lax.broadcasted_iota(jnp.int32, (1, LANES), 1) < HALF
    n_near, n_far = counts[cell, 0], counts[cell, 1]
    n_items = n_far + n_planes
    n_pairs = (n_items + 1) // 2

    def near_step(j, c):
        slot = near[cell, j] - base
        src[j] = pts[slot]
        put_near(j, slot)
        return c

    lax.fori_loop(0, n_near, near_step, 0)

    def item(j):
        j = jnp.minimum(j, n_items - 1)
        p = j - n_far
        level = jnp.where(p < below, p, p + (me + 2 - below))
        slot = far[cell, jnp.minimum(j, far.shape[1] - 1)] - base
        return jnp.where(j < n_far, slot, window + level)

    def far_step(j, c):
        first, second = item(2 * j), item(2 * j + 1)
        src[n_near + j] = jnp.where(low_half, table[first], table[second])
        put_far(n_near + j, first, second, 2 * j + 1 < n_items, low_half)
        return c

    lax.fori_loop(0, n_pairs, far_step, 0)
    n_blocks = n_near + n_pairs
    for u in range(multiple - 1):
        src[n_blocks + u] = jnp.zeros(src.shape[1:], jnp.float32)
        put_none(n_blocks + u)
    return n_blocks


def put_targets(pts, cell, tgt):
    for d in range(3):
        tgt[d] = jnp.broadcast_to(pts[PLANE + cell, d : d + 1, :], (LANES, LANES)).T


def square(tgt, src, slot, rows):
    dx = tgt[0, rows, :] - src[slot, 0:1, :]
    dy = tgt[1, rows, :] - src[slot, 1:2, :]
    dz = tgt[2, rows, :] - src[slot, 2:3, :]
    return (dx * dx + dy * dy) + (dz * dz + soften)


def put_points(messages, pts):
    for k, message in enumerate(messages):
        top = message.shape[0] - PLANE * ROWS
        for c in range(PLANE):
            pts[k * PLANE + c] = message[top + c * ROWS : top + (c + 1) * ROWS, :]


def cell_fields(message, c, groups, kinds):
    rows = kinds * PLANE
    return jnp.concatenate(
        [message[pl.ds(g * rows + c, kinds, stride=PLANE), :] for g in range(groups)], axis=0
    )


def hartree_kernel(unroll, groups, kinds, meta, counts, near, far, cst, table, marks, before, mine, after, *refs):
    parts, (out, every, pts, val, mom, tgt, src, srcv) = refs[:-8], refs[-8:]
    lay_out(parts, every)
    put_points((before, mine, after), pts)
    planes = every.shape[0]
    cells = PLANE // groups
    me, group = meta[0], meta[1]
    for k in range(3):
        there = lax.bitwise_xor(me, jnp.clip(me - 1 + k, 0, planes - 1))
        val[k * PLANE : (k + 1) * PLANE, 0, :] = every[there, :PLANE, :]
        mom[k * PLANE : (k + 1) * PLANE, 0, :] = every[there, PLANE : 2 * PLANE, :]

    def put_plane(g, c):
        mom[3 * PLANE + g] = every[lax.bitwise_xor(me, g), 2 * PLANE : 2 * PLANE + 1, :]
        return c

    lax.fori_loop(0, planes, put_plane, 0)

    def put_near(j, slot):
        srcv[j] = val[slot]

    def put_far(j, first, second, live, low_half):
        srcv[j] = jnp.where(low_half, mom[first], mom[second] * live.astype(jnp.float32))

    def put_none(j):
        srcv[j] = jnp.zeros((1, LANES), jnp.float32)

    z_low = me.astype(jnp.float32) * cell_side
    total = jnp.zeros((groups * kinds, LANES), jnp.float32)
    out[0] = jnp.broadcast_to(marks[...], (ROWS, LANES))
    for t in range(cells):
        cell = target_cell(group, t, groups)
        n_blocks = list_sources(
            me, cell, counts, near, far, planes, table, pts, src, put_near, put_far, put_none, unroll
        )
        put_targets(pts, cell, tgt)

        def step(k, acc):
            for u in range(unroll):
                slot = k * unroll + u
                acc = acc + lax.rsqrt(square(tgt, src, slot, slice(None))) * srcv[slot]
            return acc

        acc = lax.fori_loop(0, (n_blocks + unroll - 1) // unroll, step, jnp.zeros((LANES, LANES), jnp.float32))
        row = dot_nt(jnp.ones((ROWS, LANES), jnp.float32), acc)[0:1, :]
        out[0, t : t + 1, :] = row
        there = PLANE + cell
        scaled = pts[there, 4:5, :] * (pts[there, 3:4, :] + row)
        v = cell_fields(mine, cell, groups, kinds) * scaled
        w = weights(
            cst, pts[there, 0:1, :], pts[there, 1:2, :], pts[there, 2:3, :], (0.0, 0.0, z_low), (1.0, 1.0, cell_side)
        )
        total = total + dot_split(v, twice(w))
    for k in range(groups):
        out[1 + lax.bitwise_xor(group, k), :kinds, :] = total[k * kinds : (k + 1) * kinds, :]


def combine_kernel(kinds, meta, *refs):
    shares, (hartree, out, total) = refs[:-3], refs[-3:]
    groups = len(shares)
    for k, share in enumerate(shares):
        for t in range(PLANE // groups):
            cell = target_cell(lax.bitwise_xor(meta[1], k), t, groups)
            out[pl.ds(cell, 1), :] = share[0, t : t + 1, :]
    hartree[...] = out[:PLANE, :]
    for g in range(groups):
        added = shares[0][1 + g, :kinds, :]
        for share in shares[1:]:
            added = added + share[1 + g, :kinds, :]
        total[g * kinds : (g + 1) * kinds, :] = added
    rows = groups * kinds // 2
    low_half = lax.broadcasted_iota(jnp.int32, (1, LANES), 1) < HALF
    out[PLANE:, :] = jnp.where(low_half, total[:rows, :], total[rows:, :])


def orbital_kernel(
    batch, unit, steps, meta, counts, near, far, levels, screening, cst, table, before, mine, after, *refs
):
    parts, refs = refs[:-14], refs[-14:]
    out, rate, slot_of, every, pts, val, mom, tgt, src, srcv, dist, inv, acc, total = refs
    lay_out(parts, every)
    put_points((before, mine, after), pts)
    planes = every.shape[0]
    groups, cells, kinds, _ = out.shape
    orbs = groups * kinds
    me, group = meta[0], meta[1]

    def clear(i, c):
        slot_of[i] = -1
        rate[i] = 0.0
        return c

    lax.fori_loop(0, screening.shape[0], clear, 0)
    for q in range(2 * batch):
        rate[screening.shape[0] + q] = 0.0
    lane = lax.broadcasted_iota(jnp.int32, (1, LANES), 1) % orbs

    def rank(i, carry):
        found, lane_slot = carry
        level = levels[i]
        known = slot_of[level]
        slot = jnp.where(known < 0, found, known)
        slot_of[level] = slot
        rate[slot] = screening[level] * (-log2e)
        return found + (known < 0).astype(jnp.int32), jnp.where(lane == i, slot, lane_slot)

    n_levels, lane_slot = lax.fori_loop(0, orbs, rank, (jnp.int32(0), jnp.zeros((1, LANES), jnp.int32)))
    n_batches = (n_levels + batch - 1) // batch

    first_half = lax.broadcasted_iota(jnp.int32, (1, 2 * orbs), 1) < orbs

    def flip(v):
        high = v.astype(jnp.bfloat16).astype(jnp.float32)
        square = jnp.concatenate([high, v - high, jnp.zeros((LANES - 2 * orbs, LANES), jnp.float32)], axis=0)
        return square.T[:, : 2 * orbs].astype(jnp.bfloat16)

    for k in range(3):
        there = lax.bitwise_xor(me, jnp.clip(me - 1 + k, 0, planes - 1))
        message = (before, mine, after)[k]

        def prepare(c, carry):
            at = k * PLANE + c
            scaled = pts[at, 4:5, :] * (pts[at, 3:4, :] + every[there, pl.ds(c, 1), :])
            v = cell_fields(message, c, groups, kinds) * scaled
            val[at] = flip(v)
            vh, vl = split(v)
            z_low = (me - 1 + k).astype(jnp.float32) * cell_side
            low = (*cell_low(c), z_low)
            wh, wl = split(weights(cst, pts[at, 0:1, :], pts[at, 1:2, :], pts[at, 2:3, :], low, (cell_side,) * 3))
            all_of = dot_bf16(jnp.concatenate([wh, wl], axis=0), jnp.concatenate([vh, vh, vl, vl], axis=0))
            m = all_of[:HALF] + all_of[HALF:]
            m = m[:, : 2 * orbs] + pltpu.roll(all_of[:HALF], 4 * orbs - 2 * orbs, 1)[:, : 2 * orbs]
            high = m.astype(jnp.bfloat16).astype(jnp.float32)
            mom[at] = jnp.where(first_half, high, m - high).astype(jnp.bfloat16)
            return carry

        lax.fori_loop(0, PLANE, prepare, 0, unroll=4)

    def put_plane(g, c):
        there = lax.bitwise_xor(me, g)
        rows = []
        for k in range(groups):
            row = lax.bitwise_xor(group, k) * kinds
            v = every[there, pl.ds(PLANE + lax.rem(row, orbs // 2), kinds), :]
            rows.append(jnp.where(row < orbs // 2, v, pltpu.roll(v, HALF, 1)))
        mom[3 * PLANE + g] = flip(jnp.concatenate(rows, axis=0))[:HALF]
        return c

    lax.fori_loop(0, planes, put_plane, 0)

    def put_near(j, slot):
        srcv[j] = val[slot]

    def put_far(j, first, second, live, low_half):
        srcv[j, :HALF, :] = mom[first]
        srcv[j, HALF:, :] = jnp.where(live, mom[second], jnp.zeros_like(mom[second]))

    def put_none(j):
        srcv[j] = jnp.zeros(srcv.shape[1:], srcv.dtype)

    def products(b, first):
        rates = [rate[b * batch + q] for q in range(batch)]
        rows = []
        for q in range(batch):
            tiles = [(jnp.exp2(dist[first + h] * rates[q]) * inv[first + h]).astype(jnp.bfloat16) for h in range(unit)]
            rows.append(jnp.concatenate(tiles, axis=1))
        v = jnp.concatenate([srcv[first + h] for h in range(unit)], axis=0)
        return jnp.dot(jnp.concatenate(rows, axis=0), v, preferred_element_type=jnp.float32)

    def per_cell(t, carry):
        cell = target_cell(group, t, groups)
        n_blocks = list_sources(me, cell, counts, near, far, planes, table, pts, src, put_near, put_far, put_none, unit)
        n_loops = (n_blocks + unit - 1) // unit
        put_targets(pts, cell, tgt)

        def measure(c, x):
            sq = square(tgt, src, c, slice(None))
            i = lax.rsqrt(sq)
            inv[c] = i
            dist[c] = sq * i
            return x

        lax.fori_loop(0, unit * n_loops, measure, 0)
        total[...] = jnp.zeros(total.shape, jnp.float32)

        def clear(b, x):
            acc[b] = jnp.zeros(acc.shape[1:], jnp.float32)
            return x

        lax.fori_loop(0, n_batches, clear, 0)

        def step(i, at):
            b, u = at
            for _ in range(steps):
                acc[b] = acc[b] + products(b, unit * u)
                wrap = u + 1 == n_loops
                b, u = jnp.where(wrap, b + 1, b), jnp.where(wrap, 0, u + 1)
            return b, u

        lax.fori_loop(0, (n_batches * n_loops + steps - 1) // steps, step, (jnp.int32(0), jnp.int32(0)))

        def choose(b, x):
            add = total[...]
            for q in range(batch):
                mine = lane_slot[:, : 2 * orbs] == b * batch + q
                add = add + jnp.where(mine, acc[b, q * LANES : (q + 1) * LANES, :], 0.0)
            total[...] = add
            return x

        lax.fori_loop(0, n_batches, choose, 0)
        flipped = jnp.concatenate([total[...], jnp.zeros((LANES, LANES - 2 * orbs), jnp.float32)], axis=1).T
        rows = (flipped[:orbs] + flipped[orbs : 2 * orbs]) * green_scale
        for k in range(groups):
            out[k, t] = rows[k * kinds : (k + 1) * kinds]
        return carry

    lax.fori_loop(0, cells, per_cell, 0)


def place_kernel(meta, *refs):
    parts, out, ordered = refs[:-2], refs[-2], refs[-1]
    for k, part in enumerate(parts):
        for t in range(part.shape[0]):
            ordered[target_cell(lax.bitwise_xor(meta[1], k), t, len(parts))] = part[t]
    for c in range(PLANE):
        out[:, c, :] = ordered[c]


def smem():
    return pl.BlockSpec(memory_space=pltpu.SMEM)


def vmem():
    return pl.BlockSpec(memory_space=pltpu.VMEM)


def call(kernel, name, out_shape, smems, args, scratch=()):
    return pl.pallas_call(
        kernel,
        out_shape=out_shape,
        in_specs=[smem()] * smems + [vmem()] * (len(args) - smems),
        out_specs=jax.tree.map(lambda _: vmem(), out_shape),
        scratch_shapes=scratch,
        compiler_params=pltpu.CompilerParams(vmem_limit_bytes=52 * 1024 * 1024),
        name=name,
    )(*args)


def body(orbitals, points, quad_weight, external, screening, level_index, near_cells, far_cells):
    kinds, cells, point_count = orbitals.shape
    planes, groups = lax.axis_size("space"), lax.axis_size("orb")
    orbs = kinds * groups
    window = 3 * PLANE
    share = cells // groups
    me, group = lax.axis_index("space"), lax.axis_index("orb")
    meta = jnp.stack([me, group]).astype(jnp.int32)
    f32, bf16 = jnp.float32, jnp.bfloat16

    fields = gather_list(orbitals, "orb")
    weight = quad_weight * (cell_side**3 / point_count)
    own = jnp.concatenate(
        [jnp.transpose(points, (1, 0, 2)), external[:, None], weight[:, None], jnp.zeros((cells, 3, LANES), f32)], axis=1
    )
    marks = jnp.pad(level_index.astype(f32), (0, LANES - kinds))[None]
    ends = planes - 1
    up = [(i, i + 1) for i in range(ends)]
    down = [(i + 1, i) for i in range(ends)]
    message = jnp.concatenate([f.reshape(kinds * cells, LANES) for f in fields] + [own.reshape(cells * ROWS, LANES)], axis=0)
    windows = (lax.ppermute(message, "space", up), message, lax.ppermute(message, "space", down))
    cst = jnp.asarray(basis_rows())
    base_table = proxy_table(planes, window)
    shift = np.zeros(base_table.shape, np.float32)
    shift[:window, 2] = cell_side
    table = jnp.asarray(base_table) + jnp.asarray(shift) * (me - 1).astype(f32)
    counts = jnp.stack(
        [jnp.sum((near_cells >= 0).astype(jnp.int32), 1), jnp.sum((far_cells >= 0).astype(jnp.int32), 1)], axis=1
    )
    charges = call(
        charge_kernel, "charge", jax.ShapeDtypeStruct((2 * cells + ROWS, LANES), f32), 1, (meta, cst, own, *fields)
    )
    charges = gather_parts(charges, "space", False)

    unroll = 2
    blocks = near_cells.shape[1] + (far_cells.shape[1] + planes + 1) // 2 + 8
    shares = call(
        functools.partial(hartree_kernel, unroll, groups, kinds),
        "hartree",
        jax.ShapeDtypeStruct((1 + groups, ROWS, LANES), f32),
        4,
        (meta, counts, near_cells, far_cells, cst, table, marks, *windows, *charges),
        [
            pltpu.VMEM((planes, 2 * cells + ROWS, LANES), f32),
            pltpu.VMEM((window, ROWS, LANES), f32),
            pltpu.VMEM((window, 1, LANES), f32),
            pltpu.VMEM((window + planes, 1, LANES), f32),
            pltpu.VMEM((3, LANES, LANES), f32),
            pltpu.VMEM((blocks, ROWS, LANES), f32),
            pltpu.VMEM((blocks, 1, LANES), f32),
        ],
    )
    shares = gather_list(shares, "orb")
    levels = jnp.concatenate([share[0, ROWS - 1, :kinds] for share in shares]).astype(jnp.int32)
    hartree, combined = call(
        functools.partial(combine_kernel, kinds),
        "combine",
        (jax.ShapeDtypeStruct((cells, LANES), f32), jax.ShapeDtypeStruct((cells + orbs // 2, LANES), f32)),
        1,
        (meta, *shares),
        [pltpu.VMEM((orbs, LANES), f32)],
    )
    gathered = gather_parts(combined, "space", False)

    batch, unit, steps = 4, 4, 9
    levels_at_most = -(-screening.shape[0] // batch) + 1
    sent = call(
        functools.partial(orbital_kernel, batch, unit, steps),
        "orbitals",
        jax.ShapeDtypeStruct((groups, share, kinds, LANES), f32),
        6,
        (meta, counts, near_cells, far_cells, levels, screening, cst, table, *windows, *gathered),
        [
            pltpu.SMEM((screening.shape[0] + 2 * batch,), f32),
            pltpu.SMEM((screening.shape[0],), jnp.int32),
            pltpu.VMEM((planes, cells + orbs // 2, LANES), f32),
            pltpu.VMEM((window, ROWS, LANES), f32),
            pltpu.VMEM((window, LANES, 2 * orbs), bf16),
            pltpu.VMEM((window + planes, HALF, 2 * orbs), bf16),
            pltpu.VMEM((3, LANES, LANES), f32),
            pltpu.VMEM((blocks, ROWS, LANES), f32),
            pltpu.VMEM((blocks, LANES, 2 * orbs), bf16),
            pltpu.VMEM((blocks, LANES, LANES), f32),
            pltpu.VMEM((blocks, LANES, LANES), f32),
            pltpu.VMEM((levels_at_most, batch * LANES, 2 * orbs), f32),
            pltpu.VMEM((LANES, 2 * orbs), f32),
        ],
    )
    parts = [sent[0]]
    for k in range(1, groups):
        parts.append(lax.ppermute(sent[k], "orb", [(i, i ^ k) for i in range(groups)]))
    updated = call(
        place_kernel,
        "place",
        jax.ShapeDtypeStruct((kinds, cells, LANES), f32),
        1,
        (meta, *parts),
        [pltpu.VMEM((cells, kinds, LANES), f32)],
    )
    return updated, hartree


def solution(mesh):
    in_specs = (
        P("orb", "space", None),
        P(None, "space", None),
        P("space", None),
        P("space", None),
        P(),
        P("orb"),
        P("space", None),
        P("space", None),
    )
    out_specs = (P("orb", "space", None), P("space", None))
    return jax.shard_map(body, mesh=mesh, in_specs=in_specs, out_specs=out_specs, check_vma=False)
```

profile of v0, /device:TPU:4, one launch (start us, length us, event | category | flops | bytes accessed | tf_op | source)
XLA Modules:
  0.0 111.8 jit_solution(6092605809939854538)
XLA Ops:
  0.6 0.0 copy-start.1
  0.6 3.7 %collective-permute-start.2 = (f32[1,8,16,128]{3,2,1,0:T(8,128)}, f32[1,8,16,128]{3,2,1,0:T(8,128)S(1)}, u32[]{:S(2)}, u32[]{:S(2)}) collective-permute-start(f32[1,8,16,128]{3,2,1,0:T(8,128)} %bitcast.43), channel_id=1, source_target_pairs={{0,24},{8,16},{16,8},{24,0},{1,25},{9,17},{17,9},{25,1},{2,26},{10... | collective-permute-start | bytes 196616 | tf_op jit(solution)/shard_map/ppermute | solution.py:90
  4.3 0.0 collective-permute-start.1
  4.3 0.8 collective-permute-start
  5.1 0.8 convert_reduce_fusion.1
  5.9 0.8 convert_reduce_fusion
  6.7 0.7 broadcast_multiply_fusion
  7.4 0.8 copy.20
  8.2 0.0 copy-done.1
  8.2 0.1 pad.16.clone
  8.3 0.0 copy-start.5
  8.3 1.1 multiply_add_fusion.table
  9.4 0.0 copy-done.5
  9.4 0.1 maximum_maximum_fusion.own
  9.5 0.1 pad_add_fusion.1.meta
  9.5 0.0 collective-permute-done
  9.5 0.6 collective-permute-done.1
  10.1 0.0 collective-permute-done.2
  10.1 0.0 copy-start
  10.2 0.1 bitcast_dynamic-update-slice_fusion.mine
  10.2 2.8 %collective-permute-start.4 = (f32[640,128]{1,0:T(8,128)S(1)}, f32[640,128]{1,0:T(8,128)S(1)}, u32[]{:S(2)}, u32[]{:S(2)}) collective-permute-start(f32[640,128]{1,0:T(8,128)S(1)} %bitcast_dynamic-update-slice_fusion.mine), channel_id=1, source_target_pairs={{1,0},{2,1},{3,2},{4,3},{5,4},{6,5},{7,6},{9,8},{10,9},{11,10},{12... | collective-permute-start | bytes 983048 | tf_op jit(solution)/shard_map/ppermute | solution.py:487
  13.0 1.9 %collective-permute-start.3 = (f32[640,128]{1,0:T(8,128)S(1)}, f32[640,128]{1,0:T(8,128)S(1)}, u32[]{:S(2)}, u32[]{:S(2)}) collective-permute-start(f32[640,128]{1,0:T(8,128)S(1)} %bitcast_dynamic-update-slice_fusion.mine), channel_id=1, source_target_pairs={{0,1},{1,2},{2,3},{3,4},{4,5},{5,6},{6,7},{8,9},{9,10},{10,11},{11... | collective-permute-start | bytes 983048 | tf_op jit(solution)/shard_map/ppermute | solution.py:487
  15.0 0.0 copy-done
  15.0 2.4 %charge.1 = f32[40,128]{1,0:T(8,128)S(1)} custom-call(s32[2]{0:T(128)S(1)} %pad_add_fusion.1.meta, f32[12,8,128]{2,1,0:T(8,128)S(1)} %copy-done, f32[16,8,128]{2,1,0:T(8,128)S(1)} %maximum_maximum_fusion.own, f32[8,16,128]{2,1,0:T(8,128)S(1)} %copy-done.1, f32[8,16,128]{2,1,0:T(8,128)S(1)} %bitcast.52, f32[8,16,128]{2,1,0:T(8,128)S(1)} %bitcast.50, ...), custom_call_target="tpu_custom_call" | custom-call | tf_op jit(solution)/shard_map/charge/pallas_call | solution.py:456
  17.4 0.7 collective-permute-start.5
  18.1 0.6 copy-done.6
  18.8 0.2 collective-permute-done.5
  19.0 2.4 %collective-permute-start.8 = (f32[2,40,128]{2,1,0:T(8,128)S(1)}, f32[2,40,128]{2,1,0:T(8,128)S(1)}, u32[]{:S(2)}, u32[]{:S(2)}) collective-permute-start(f32[2,40,128]{2,1,0:T(8,128)S(1)} %pad_maximum_fusion.refs_0_), channel_id=1, source_target_pairs={{0,6},{1,7},{2,4},{3,5},{4,2},{5,3},{6,0},{7,1},{8,14},{9,15},{10,... | collective-permute-start | bytes 122888 | tf_op jit(solution)/shard_map/ppermute | solution.py:90
  21.3 0.0 collective-permute-start.7
  21.4 1.2 %collective-permute-start.6 = (f32[2,40,128]{2,1,0:T(8,128)S(1)}, f32[2,40,128]{2,1,0:T(8,128)S(1)}, u32[]{:S(2)}, u32[]{:S(2)}) collective-permute-start(f32[2,40,128]{2,1,0:T(8,128)S(1)} %pad_maximum_fusion.refs_0_), channel_id=1, source_target_pairs={{0,2},{1,3},{2,0},{3,1},{4,6},{5,7},{6,4},{7,5},{8,10},{9,11},{10,... | collective-permute-start | bytes 122888 | tf_op jit(solution)/shard_map/ppermute | solution.py:90
  22.5 0.1 copy.18.counts
  22.6 1.3 %collective-permute-done.8.refs_3_ = f32[2,40,128]{2,1,0:T(8,128)S(1)} collective-permute-done((f32[2,40,128]{2,1,0:T(8,128)S(1)}, f32[2,40,128]{2,1,0:T(8,128)S(1)}, u32[]{:S(2)}, u32[]{:S(2)}) %collective-permute-start.8) | collective-permute-done | bytes 40992 | tf_op jit(solution)/shard_map/ppermute | solution.py:90
  23.9 1.4 %collective-permute-done.7.refs_2_ = f32[2,40,128]{2,1,0:T(8,128)S(1)} collective-permute-done((f32[2,40,128]{2,1,0:T(8,128)S(1)}, f32[2,40,128]{2,1,0:T(8,128)S(1)}, u32[]{:S(2)}, u32[]{:S(2)}) %collective-permute-start.7) | collective-permute-done | bytes 40992 | tf_op jit(solution)/shard_map/ppermute | solution.py:90
  25.4 0.0 collective-permute-done.6.refs_1_
  25.4 0.0 collective-permute-done.4.after
  25.4 0.0 collective-permute-done.3.before
  25.4 0.0 copy-done.3
  25.4 0.0 copy-done.2
  25.4 9.3 %hartree.1.refs_0_ = f32[5,8,128]{2,1,0:T(8,128)S(1)} custom-call(s32[2]{0:T(128)S(1)} %pad_add_fusion.1.meta, s32[16,2]{1,0:T(8,128)S(1)} %copy.18.counts, s32[16,27]{1,0:T(8,128)S(1)} %copy-done.3, s32[16,42]{1,0:T(8,128)S(1)} %copy-done.2, f32[12,8,128]{2,1,0:T(8,128)S(1)} %copy-done, f32[56,8,128]{2,1,0:T(8,128)S(1)} %multiply_add_fusion.table, ...), custom_call_target="tpu_custom_call" | custom-call | tf_op jit(solution)/shard_map/hartree/pallas_call | solution.py:456
  34.7 2.9 %collective-permute-start.11 = (f32[1,5,8,128]{3,2,1,0:T(8,128)S(1)}, f32[1,5,8,128]{3,2,1,0:T(8,128)S(1)}, u32[]{:S(2)}, u32[]{:S(2)}) collective-permute-start(f32[1,5,8,128]{3,2,1,0:T(8,128)S(1)} %bitcast.55), channel_id=1, source_target_pairs={{0,24},{8,16},{16,8},{24,0},{1,25},{9,17},{17,9},{25,1},{2,26},{10... | collective-permute-start | bytes 61448 | tf_op jit(solution)/shard_map/ppermute | solution.py:90
  37.6 0.0 collective-permute-start.10
  37.6 1.5 %collective-permute-start.9 = (f32[1,5,8,128]{3,2,1,0:T(8,128)S(1)}, f32[1,5,8,128]{3,2,1,0:T(8,128)S(1)}, u32[]{:S(2)}, u32[]{:S(2)}) collective-permute-start(f32[1,5,8,128]{3,2,1,0:T(8,128)S(1)} %bitcast.57), channel_id=1, source_target_pairs={{0,8},{8,0},{16,24},{24,16},{1,9},{9,1},{17,25},{25,17},{2,10},{10... | collective-permute-start | bytes 61448 | tf_op jit(solution)/shard_map/ppermute | solution.py:90
  39.1 1.3 %collective-permute-done.11 = f32[1,5,8,128]{3,2,1,0:T(8,128)S(1)} collective-permute-done((f32[1,5,8,128]{3,2,1,0:T(8,128)S(1)}, f32[1,5,8,128]{3,2,1,0:T(8,128)S(1)}, u32[]{:S(2)}, u32[]{:S(2)}) %collective-permute-start.11) | collective-permute-done | bytes 20512 | tf_op jit(solution)/shard_map/ppermute | solution.py:90
  40.4 1.9 %collective-permute-done.10 = f32[1,5,8,128]{3,2,1,0:T(8,128)S(1)} collective-permute-done((f32[1,5,8,128]{3,2,1,0:T(8,128)S(1)}, f32[1,5,8,128]{3,2,1,0:T(8,128)S(1)}, u32[]{:S(2)}, u32[]{:S(2)}) %collective-permute-start.10) | collective-permute-done | bytes 20512 | tf_op jit(solution)/shard_map/ppermute | solution.py:90
  42.3 0.0 collective-permute-done.9
  42.3 1.2 %combine.1 = (f32[16,128]{1,0:T(8,128)}, f32[32,128]{1,0:T(8,128)S(1)}) custom-call(s32[2]{0:T(128)S(1)} %pad_add_fusion.1.meta, f32[5,8,128]{2,1,0:T(8,128)S(1)} %hartree.1.refs_0_, f32[5,8,128]{2,1,0:T(8,128)S(1)} %bitcast.60, f32[5,8,128]{2,1,0:T(8,128)S(1)} %bitcast.63, f32[5,8,128]{2,1,0:T(8,128)S(1)} %bitcast.59), custom_call_target="tpu_custom_call" | custom-call | tf_op jit(solution)/shard_map/combine/pallas_call | solution.py:456
  43.5 0.0 collective-permute-start.12
  43.5 1.2 %collective-permute-done.12 = f32[1,32,128]{2,1,0:T(8,128)S(1)} collective-permute-done((f32[1,32,128]{2,1,0:T(8,128)S(1)}, f32[1,32,128]{2,1,0:T(8,128)S(1)}, u32[]{:S(2)}, u32[]{:S(2)}) %collective-permute-start.12) | collective-permute-done | bytes 16416 | tf_op jit(solution)/shard_map/ppermute | solution.py:90
  44.7 1.3 %collective-permute-start.15 = (f32[2,32,128]{2,1,0:T(8,128)S(1)}, f32[2,32,128]{2,1,0:T(8,128)S(1)}, u32[]{:S(2)}, u32[]{:S(2)}) collective-permute-start(f32[2,32,128]{2,1,0:T(8,128)S(1)} %pad_maximum_fusion.1.refs_0_), channel_id=1, source_target_pairs={{0,6},{1,7},{2,4},{3,5},{4,2},{5,3},{6,0},{7,1},{8,14},{9,15},{10,... | collective-permute-start | bytes 98312 | tf_op jit(solution)/shard_map/ppermute | solution.py:90
  46.0 1.4 %collective-permute-start.14 = (f32[2,32,128]{2,1,0:T(8,128)S(1)}, f32[2,32,128]{2,1,0:T(8,128)S(1)}, u32[]{:S(2)}, u32[]{:S(2)}) collective-permute-start(f32[2,32,128]{2,1,0:T(8,128)S(1)} %pad_maximum_fusion.1.refs_0_), channel_id=1, source_target_pairs={{0,4},{1,5},{2,6},{3,7},{4,0},{5,1},{6,2},{7,3},{8,12},{9,13},{10,... | collective-permute-start | bytes 98312 | tf_op jit(solution)/shard_map/ppermute | solution.py:90
  47.4 0.8 collective-permute-start.13
  48.2 0.1 maximum_convert_fusion.levels
  48.2 1.2 %collective-permute-done.15.refs_3_ = f32[2,32,128]{2,1,0:T(8,128)S(1)} collective-permute-done((f32[2,32,128]{2,1,0:T(8,128)S(1)}, f32[2,32,128]{2,1,0:T(8,128)S(1)}, u32[]{:S(2)}, u32[]{:S(2)}) %collective-permute-start.15) | collective-permute-done | bytes 32800 | tf_op jit(solution)/shard_map/ppermute | solution.py:90
  49.5 0.4 collective-permute-done.14.refs_2_
  49.9 1.4 %collective-permute-done.13.refs_1_ = f32[2,32,128]{2,1,0:T(8,128)S(1)} collective-permute-done((f32[2,32,128]{2,1,0:T(8,128)S(1)}, f32[2,32,128]{2,1,0:T(8,128)S(1)}, u32[]{:S(2)}, u32[]{:S(2)}) %collective-permute-start.13) | collective-permute-done | bytes 32800 | tf_op jit(solution)/shard_map/ppermute | solution.py:90
  51.3 0.0 copy-done.4
  51.3 52.9 %orbitals.1 = f32[4,4,8,128]{3,2,1,0:T(8,128)S(1)} custom-call(s32[2]{0:T(128)S(1)} %pad_add_fusion.1.meta, s32[16,2]{1,0:T(8,128)S(1)} %copy.18.counts, s32[16,27]{1,0:T(8,128)S(1)} %copy-done.3, s32[16,42]{1,0:T(8,128)S(1)} %copy-done.2, s32[32]{0:T(128)S(1)} %maximum_convert_fusion.levels, f32[32]{0:T(128)S(1)} %copy-done.4, f32[12,8,128]{2,1,0:T(8,128)S(1)} %copy-done, ...), custom_call_target="tpu_custom_call" | custom-call | tf_op jit(solution)/shard_map/orbitals/pallas_call | solution.py:456
  104.3 1.5 %collective-permute-start.18 = (f32[4,8,128]{2,1,0:T(8,128)S(1)}, f32[4,8,128]{2,1,0:T(8,128)S(1)}, u32[]{:S(2)}, u32[]{:S(2)}) collective-permute-start(f32[4,8,128]{2,1,0:T(8,128)S(1)} %get-tuple-element.6), channel_id=1, source_target_pairs={{0,24},{8,16},{16,8},{24,0},{1,25},{9,17},{17,9},{25,1},{2,26},{10... | collective-permute-start | bytes 49160 | tf_op jit(solution)/shard_map/ppermute | solution.py:557
  105.8 0.0 collective-permute-start.17
  105.8 2.9 %collective-permute-start.16 = (f32[4,8,128]{2,1,0:T(8,128)S(1)}, f32[4,8,128]{2,1,0:T(8,128)S(1)}, u32[]{:S(2)}, u32[]{:S(2)}) collective-permute-start(f32[4,8,128]{2,1,0:T(8,128)S(1)} %get-tuple-element.8), channel_id=1, source_target_pairs={{0,8},{8,0},{16,24},{24,16},{1,9},{9,1},{17,25},{25,17},{2,10},{10... | collective-permute-start | bytes 49160 | tf_op jit(solution)/shard_map/ppermute | solution.py:557
  108.7 1.1 %collective-permute-done.18.refs_3_ = f32[4,8,128]{2,1,0:T(8,128)S(1)} collective-permute-done((f32[4,8,128]{2,1,0:T(8,128)S(1)}, f32[4,8,128]{2,1,0:T(8,128)S(1)}, u32[]{:S(2)}, u32[]{:S(2)}) %collective-permute-start.18) | collective-permute-done | bytes 16416 | tf_op jit(solution)/shard_map/ppermute | solution.py:557
  109.9 0.6 collective-permute-done.17.refs_2_
  110.4 0.2 collective-permute-done.16.refs_1_
  110.6 1.2 %place.1 = f32[8,16,128]{2,1,0:T(8,128)} custom-call(s32[2]{0:T(128)S(1)} %pad_add_fusion.1.meta, f32[4,8,128]{2,1,0:T(8,128)S(1)} %get-tuple-element.9.refs_0_, f32[4,8,128]{2,1,0:T(8,128)S(1)} %collective-permute-done.16.refs_1_, f32[4,8,128]{2,1,0:T(8,128)S(1)} %collective-permute-done.17.refs_2_, f32[4,8,128]{2,1,0:T(8,128)S(1)} %collective-permute-done.18.refs_3_), custom_call_target="tpu_custom_call" | custom-call | tf_op jit(solution)/shard_map/place/pallas_call | solution.py:456
  (19 shorter events, 0.1 us)
Async XLA Ops:
  0.6 7.5 %copy-start.1 = (f32[8,16,128]{2,1,0:T(8,128)S(1)}, f32[8,16,128]{2,1,0:T(8,128)}, u32[]{:S(2)}) copy-start(f32[8,16,128]{2,1,0:T(8,128)} %refs_0_.1) | copy-start | bytes 196612
  0.6 9.5 %collective-permute-start.2 = (f32[1,8,16,128]{3,2,1,0:T(8,128)}, f32[1,8,16,128]{3,2,1,0:T(8,128)S(1)}, u32[]{:S(2)}, u32[]{:S(2)}) collective-permute-start(f32[1,8,16,128]{3,2,1,0:T(8,128)} %bitcast.43), channel_id=1, source_target_pairs={{0,24},{8,16},{16,8},{24,0},{1,25},{9,17},{17,9},{25,1},{2,26},{10... | collective-permute-start | bytes 196616 | tf_op jit(solution)/shard_map/ppermute | solution.py:90
  4.3 5.8 %collective-permute-start.1 = (f32[1,8,16,128]{3,2,1,0:T(8,128)}, f32[1,8,16,128]{3,2,1,0:T(8,128)S(1)}, u32[]{:S(2)}, u32[]{:S(2)}) collective-permute-start(f32[1,8,16,128]{3,2,1,0:T(8,128)} %bitcast.44), channel_id=1, source_target_pairs={{0,16},{8,24},{16,0},{24,8},{1,17},{9,25},{17,1},{25,9},{2,18},{10... | collective-permute-start | bytes 196616 | tf_op jit(solution)/shard_map/ppermute | solution.py:90
  4.3 5.2 %collective-permute-start = (f32[1,8,16,128]{3,2,1,0:T(8,128)}, f32[1,8,16,128]{3,2,1,0:T(8,128)S(1)}, u32[]{:S(2)}, u32[]{:S(2)}) collective-permute-start(f32[1,8,16,128]{3,2,1,0:T(8,128)} %bitcast.45), channel_id=1, source_target_pairs={{0,8},{8,0},{16,24},{24,16},{1,9},{9,1},{17,25},{25,17},{2,10},{10... | collective-permute-start | bytes 196616 | tf_op jit(solution)/shard_map/ppermute | solution.py:90
  8.3 1.1 copy-start.5
  10.1 4.8 %copy-start = (f32[12,8,128]{2,1,0:T(8,128)S(1)}, f32[12,8,128]{2,1,0:T(8,128)}, u32[]{:S(2)}) copy-start(f32[12,8,128]{2,1,0:T(8,128)} %constant.26.clone.cst) | copy-start | bytes 147460
  10.2 15.1 %collective-permute-start.4 = (f32[640,128]{1,0:T(8,128)S(1)}, f32[640,128]{1,0:T(8,128)S(1)}, u32[]{:S(2)}, u32[]{:S(2)}) collective-permute-start(f32[640,128]{1,0:T(8,128)S(1)} %bitcast_dynamic-update-slice_fusion.mine), channel_id=1, source_target_pairs={{1,0},{2,1},{3,2},{4,3},{5,4},{6,5},{7,6},{9,8},{10,9},{11,10},{12... | collective-permute-start | bytes 983048 | tf_op jit(solution)/shard_map/ppermute | solution.py:487
  13.0 12.3 %collective-permute-start.3 = (f32[640,128]{1,0:T(8,128)S(1)}, f32[640,128]{1,0:T(8,128)S(1)}, u32[]{:S(2)}, u32[]{:S(2)}) collective-permute-start(f32[640,128]{1,0:T(8,128)S(1)} %bitcast_dynamic-update-slice_fusion.mine), channel_id=1, source_target_pairs={{0,1},{1,2},{2,3},{3,4},{4,5},{5,6},{6,7},{8,9},{9,10},{10,11},{11... | collective-permute-start | bytes 983048 | tf_op jit(solution)/shard_map/ppermute | solution.py:487
  17.4 1.6 %collective-permute-start.5 = (f32[1,40,128]{2,1,0:T(8,128)S(1)}, f32[1,40,128]{2,1,0:T(8,128)S(1)}, u32[]{:S(2)}, u32[]{:S(2)}) collective-permute-start(f32[1,40,128]{2,1,0:T(8,128)S(1)} %bitcast.53), channel_id=1, source_target_pairs={{0,1},{1,0},{2,3},{3,2},{4,5},{5,4},{6,7},{7,6},{8,9},{9,8},{10,11... | collective-permute-start | bytes 61448 | tf_op jit(solution)/shard_map/ppermute | solution.py:90
  18.1 0.7 copy-start.6
  19.0 6.4 %copy-start.3 = (s32[16,27]{1,0:T(8,128)S(1)}, s32[16,27]{1,0:T(8,128)}, u32[]{:S(2)}) copy-start(s32[16,27]{1,0:T(8,128)} %near.3) | copy-start | bytes 5188
  19.0 6.4 %copy-start.2 = (s32[16,42]{1,0:T(8,128)S(1)}, s32[16,42]{1,0:T(8,128)}, u32[]{:S(2)}) copy-start(s32[16,42]{1,0:T(8,128)} %far.3) | copy-start | bytes 8068
  19.0 5.0 %collective-permute-start.8 = (f32[2,40,128]{2,1,0:T(8,128)S(1)}, f32[2,40,128]{2,1,0:T(8,128)S(1)}, u32[]{:S(2)}, u32[]{:S(2)}) collective-permute-start(f32[2,40,128]{2,1,0:T(8,128)S(1)} %pad_maximum_fusion.refs_0_), channel_id=1, source_target_pairs={{0,6},{1,7},{2,4},{3,5},{4,2},{5,3},{6,0},{7,1},{8,14},{9,15},{10,... | collective-permute-start | bytes 122888 | tf_op jit(solution)/shard_map/ppermute | solution.py:90
  21.3 4.0 %collective-permute-start.7 = (f32[2,40,128]{2,1,0:T(8,128)S(1)}, f32[2,40,128]{2,1,0:T(8,128)S(1)}, u32[]{:S(2)}, u32[]{:S(2)}) collective-permute-start(f32[2,40,128]{2,1,0:T(8,128)S(1)} %pad_maximum_fusion.refs_0_), channel_id=1, source_target_pairs={{0,4},{1,5},{2,6},{3,7},{4,0},{5,1},{6,2},{7,3},{8,12},{9,13},{10,... | collective-permute-start | bytes 122888 | tf_op jit(solution)/shard_map/ppermute | solution.py:90
  21.4 4.0 %collective-permute-start.6 = (f32[2,40,128]{2,1,0:T(8,128)S(1)}, f32[2,40,128]{2,1,0:T(8,128)S(1)}, u32[]{:S(2)}, u32[]{:S(2)}) collective-permute-start(f32[2,40,128]{2,1,0:T(8,128)S(1)} %pad_maximum_fusion.refs_0_), channel_id=1, source_target_pairs={{0,2},{1,3},{2,0},{3,1},{4,6},{5,7},{6,4},{7,5},{8,10},{9,11},{10,... | collective-permute-start | bytes 122888 | tf_op jit(solution)/shard_map/ppermute | solution.py:90
  34.7 5.7 %collective-permute-start.11 = (f32[1,5,8,128]{3,2,1,0:T(8,128)S(1)}, f32[1,5,8,128]{3,2,1,0:T(8,128)S(1)}, u32[]{:S(2)}, u32[]{:S(2)}) collective-permute-start(f32[1,5,8,128]{3,2,1,0:T(8,128)S(1)} %bitcast.55), channel_id=1, source_target_pairs={{0,24},{8,16},{16,8},{24,0},{1,25},{9,17},{17,9},{25,1},{2,26},{10... | collective-permute-start | bytes 61448 | tf_op jit(solution)/shard_map/ppermute | solution.py:90
  37.6 4.7 %collective-permute-start.10 = (f32[1,5,8,128]{3,2,1,0:T(8,128)S(1)}, f32[1,5,8,128]{3,2,1,0:T(8,128)S(1)}, u32[]{:S(2)}, u32[]{:S(2)}) collective-permute-start(f32[1,5,8,128]{3,2,1,0:T(8,128)S(1)} %bitcast.56), channel_id=1, source_target_pairs={{0,16},{8,24},{16,0},{24,8},{1,17},{9,25},{17,1},{25,9},{2,18},{10... | collective-permute-start | bytes 61448 | tf_op jit(solution)/shard_map/ppermute | solution.py:90
  37.6 4.7 %collective-permute-start.9 = (f32[1,5,8,128]{3,2,1,0:T(8,128)S(1)}, f32[1,5,8,128]{3,2,1,0:T(8,128)S(1)}, u32[]{:S(2)}, u32[]{:S(2)}) collective-permute-start(f32[1,5,8,128]{3,2,1,0:T(8,128)S(1)} %bitcast.57), channel_id=1, source_target_pairs={{0,8},{8,0},{16,24},{24,16},{1,9},{9,1},{17,25},{25,17},{2,10},{10... | collective-permute-start | bytes 61448 | tf_op jit(solution)/shard_map/ppermute | solution.py:90
  43.5 1.2 %collective-permute-start.12 = (f32[1,32,128]{2,1,0:T(8,128)S(1)}, f32[1,32,128]{2,1,0:T(8,128)S(1)}, u32[]{:S(2)}, u32[]{:S(2)}) collective-permute-start(f32[1,32,128]{2,1,0:T(8,128)S(1)} %bitcast.64), channel_id=1, source_target_pairs={{0,1},{1,0},{2,3},{3,2},{4,5},{5,4},{6,7},{7,6},{8,9},{9,8},{10,11... | collective-permute-start | bytes 49160 | tf_op jit(solution)/shard_map/ppermute | solution.py:90
  44.7 6.6 %copy-start.4 = (f32[32]{0:T(128)S(1)}, f32[32]{0:T(128)}, u32[]{:S(2)}) copy-start(f32[32]{0:T(128)} %screening.1) | copy-start | bytes 388
  44.7 4.8 %collective-permute-start.15 = (f32[2,32,128]{2,1,0:T(8,128)S(1)}, f32[2,32,128]{2,1,0:T(8,128)S(1)}, u32[]{:S(2)}, u32[]{:S(2)}) collective-permute-start(f32[2,32,128]{2,1,0:T(8,128)S(1)} %pad_maximum_fusion.1.refs_0_), channel_id=1, source_target_pairs={{0,6},{1,7},{2,4},{3,5},{4,2},{5,3},{6,0},{7,1},{8,14},{9,15},{10,... | collective-permute-start | bytes 98312 | tf_op jit(solution)/shard_map/ppermute | solution.py:90
  46.0 3.9 %collective-permute-start.14 = (f32[2,32,128]{2,1,0:T(8,128)S(1)}, f32[2,32,128]{2,1,0:T(8,128)S(1)}, u32[]{:S(2)}, u32[]{:S(2)}) collective-permute-start(f32[2,32,128]{2,1,0:T(8,128)S(1)} %pad_maximum_fusion.1.refs_0_), channel_id=1, source_target_pairs={{0,4},{1,5},{2,6},{3,7},{4,0},{5,1},{6,2},{7,3},{8,12},{9,13},{10,... | collective-permute-start | bytes 98312 | tf_op jit(solution)/shard_map/ppermute | solution.py:90
  47.4 3.9 %collective-permute-start.13 = (f32[2,32,128]{2,1,0:T(8,128)S(1)}, f32[2,32,128]{2,1,0:T(8,128)S(1)}, u32[]{:S(2)}, u32[]{:S(2)}) collective-permute-start(f32[2,32,128]{2,1,0:T(8,128)S(1)} %pad_maximum_fusion.1.refs_0_), channel_id=1, source_target_pairs={{0,2},{1,3},{2,0},{3,1},{4,6},{5,7},{6,4},{7,5},{8,10},{9,11},{10,... | collective-permute-start | bytes 98312 | tf_op jit(solution)/shard_map/ppermute | solution.py:90
  104.3 5.6 %collective-permute-start.18 = (f32[4,8,128]{2,1,0:T(8,128)S(1)}, f32[4,8,128]{2,1,0:T(8,128)S(1)}, u32[]{:S(2)}, u32[]{:S(2)}) collective-permute-start(f32[4,8,128]{2,1,0:T(8,128)S(1)} %get-tuple-element.6), channel_id=1, source_target_pairs={{0,24},{8,16},{16,8},{24,0},{1,25},{9,17},{17,9},{25,1},{2,26},{10... | collective-permute-start | bytes 49160 | tf_op jit(solution)/shard_map/ppermute | solution.py:557
  105.8 4.7 %collective-permute-start.17 = (f32[4,8,128]{2,1,0:T(8,128)S(1)}, f32[4,8,128]{2,1,0:T(8,128)S(1)}, u32[]{:S(2)}, u32[]{:S(2)}) collective-permute-start(f32[4,8,128]{2,1,0:T(8,128)S(1)} %get-tuple-element.7), channel_id=1, source_target_pairs={{0,16},{8,24},{16,0},{24,8},{1,17},{9,25},{17,1},{25,9},{2,18},{10... | collective-permute-start | bytes 49160 | tf_op jit(solution)/shard_map/ppermute | solution.py:557
  105.8 4.8 %collective-permute-start.16 = (f32[4,8,128]{2,1,0:T(8,128)S(1)}, f32[4,8,128]{2,1,0:T(8,128)S(1)}, u32[]{:S(2)}, u32[]{:S(2)}) collective-permute-start(f32[4,8,128]{2,1,0:T(8,128)S(1)} %get-tuple-element.8), channel_id=1, source_target_pairs={{0,8},{8,0},{16,24},{24,16},{1,9},{9,1},{17,25},{25,17},{2,10},{10... | collective-permute-start | bytes 49160 | tf_op jit(solution)/shard_map/ppermute | solution.py:557
where the time goes:
time: 113 us; the launch traced here: 112 us
  Pallas kernels  67 us (59%)
  starting transfers between devices  25.8 us (23%)
  waiting for transfers between devices  12.8 us (11%)
  other arithmetic  3.74 us (3%)
  local copies, waits for them, and re-layouts  1.63 us (1%)
    pallas_call x5, Pallas kernels, call(): pl.pallas_call(kernel, out_shape=out_shape, in_specs=[smem()] * smems + [...  67 us
    ppermute x14, starting transfers between devices, gather_parts(): lax.ppermute(held, axis, [(i, i ^ have * j) for i in range(count)])  16.6 us
    ppermute x14, waiting for transfers between devices, gather_parts(): lax.ppermute(held, axis, [(i, i ^ have * j) for i in range(count)])  10.9 us
    ppermute x3, starting transfers between devices, body(): lax.ppermute(sent[k], 'orb', [(i, i ^ k) for i in range(groups)])  4.45 us
    ppermute x1, starting transfers between devices, body(): lax.ppermute(message, 'space', down)  2.78 us
  transfers between devices with their start and end apart: 19, of which 13 were waited for; matrix products, arithmetic and copies ran while one was open for 4% of the time, Pallas kernels for 2%

commit v1 on v0

--- a/solution.py
+++ b/solution.py
@@ -152,42 +152,48 @@
     return below, below + jnp.maximum(planes - 2 - me, 0)
 
 
-def list_sources(me, cell, counts, near, far, planes, table, pts, src, put_near, put_far, put_none, multiple):
+def list_blocks(own, start, me, cell, counts, near, far, planes, put_near, put_far, put_none):
     window = 3 * PLANE
     base = (me - 1) * PLANE
-    below, n_planes = live_planes(me, planes)
-    low_half = lax.broadcasted_iota(jnp.int32, (1, LANES), 1) < HALF
-    n_near, n_far = counts[cell, 0], counts[cell, 1]
+    near_low, near_own, near_all, far_low, far_own, far_all = (counts[cell, k] for k in range(6))
+    if own:
+        n_near, n_far, n_planes = near_own, far_own, 0
+    else:
+        below, n_planes = live_planes(me, planes)
+        n_near, n_far = near_all - near_own, far_all - far_own
     n_items = n_far + n_planes
     n_pairs = (n_items + 1) // 2
 
+    def place(j, low, mid):
+        return j + low if own else jnp.where(j < low, j, j + mid)
+
     def near_step(j, c):
-        slot = near[cell, j] - base
-        src[j] = pts[slot]
-        put_near(j, slot)
+        put_near(start + j, near[cell, place(j, near_low, near_own)] - base)
         return c
 
     lax.fori_loop(0, n_near, near_step, 0)
 
     def item(j):
         j = jnp.minimum(j, n_items - 1)
+        slot = far[cell, jnp.clip(place(j, far_low, far_own), 0, far.shape[1] - 1)] - base
+        if own:
+            return slot
         p = j - n_far
         level = jnp.where(p < below, p, p + (me + 2 - below))
-        slot = far[cell, jnp.minimum(j, far.shape[1] - 1)] - base
         return jnp.where(j < n_far, slot, window + level)
 
     def far_step(j, c):
-        first, second = item(2 * j), item(2 * j + 1)
-        src[n_near + j] = jnp.where(low_half, table[first], table[second])
-        put_far(n_near + j, first, second, 2 * j + 1 < n_items, low_half)
+        put_far(start + n_near + j, item(2 * j), item(2 * j + 1), 2 * j + 1 < n_items)
         return c
 
     lax.fori_loop(0, n_pairs, far_step, 0)
-    n_blocks = n_near + n_pairs
-    for u in range(multiple - 1):
-        src[n_blocks + u] = jnp.zeros(src.shape[1:], jnp.float32)
-        put_none(n_blocks + u)
-    return n_blocks
+    last = start + n_near + n_pairs
+    put_none(last)
+    return start + (n_near + n_pairs + 1) // 2 * 2
+
+
+def in_low_half():
+    return lax.broadcasted_iota(jnp.int32, (1, LANES), 1) < HALF
 
 
 def put_targets(pts, cell, tgt):
@@ -216,10 +222,44 @@
     )
 
 
-def hartree_kernel(unroll, groups, kinds, meta, counts, near, far, cst, table, marks, before, mine, after, *refs):
-    parts, (out, every, pts, val, mom, tgt, src, srcv) = refs[:-8], refs[-8:]
+def pairs_kernel(groups, planes, meta, counts, near, far, table, before, mine, after, inv, dist, pts, tgt, src):
+    put_points((before, mine, after), pts)
+    me, group = meta[0], meta[1]
+    low_half = in_low_half()
+
+    def put_near(j, slot):
+        src[j] = pts[slot]
+
+    def put_far(j, first, second, live):
+        src[j] = jnp.where(low_half, table[first], table[second])
+
+    def put_none(j):
+        src[j] = jnp.zeros(src.shape[1:], jnp.float32)
+
+    def per_cell(t, carry):
+        cell = target_cell(group, t, groups)
+        end = jnp.int32(0)
+        for own in (True, False):
+            end = list_blocks(own, end, me, cell, counts, near, far, planes, put_near, put_far, put_none)
+        put_targets(pts, cell, tgt)
+
+        def measure(i, x):
+            for u in range(2):
+                sq = square(tgt, src, 2 * i + u, slice(None))
+                r = lax.rsqrt(sq)
+                inv[t, 2 * i + u] = r
+                dist[t, 2 * i + u] = sq * r
+            return x
+
+        lax.fori_loop(0, end // 2, measure, 0)
+        return carry
+
+    lax.fori_loop(0, PLANE // groups, per_cell, 0)
+
+
+def hartree_kernel(groups, kinds, meta, counts, near, far, cst, marks, mine, inv, *refs):
+    parts, (out, every, val, mom, srcv) = refs[:-5], refs[-5:]
     lay_out(parts, every)
-    put_points((before, mine, after), pts)
     planes = every.shape[0]
     cells = PLANE // groups
     me, group = meta[0], meta[1]
@@ -233,41 +273,37 @@
         return c
 
     lax.fori_loop(0, planes, put_plane, 0)
+    low_half = in_low_half()
 
     def put_near(j, slot):
         srcv[j] = val[slot]
 
-    def put_far(j, first, second, live, low_half):
+    def put_far(j, first, second, live):
         srcv[j] = jnp.where(low_half, mom[first], mom[second] * live.astype(jnp.float32))
 
     def put_none(j):
         srcv[j] = jnp.zeros((1, LANES), jnp.float32)
 
     z_low = me.astype(jnp.float32) * cell_side
+    top = mine.shape[0] - PLANE * ROWS
     total = jnp.zeros((groups * kinds, LANES), jnp.float32)
     out[0] = jnp.broadcast_to(marks[...], (ROWS, LANES))
     for t in range(cells):
         cell = target_cell(group, t, groups)
-        n_blocks = list_sources(
-            me, cell, counts, near, far, planes, table, pts, src, put_near, put_far, put_none, unroll
-        )
-        put_targets(pts, cell, tgt)
-
-        def step(k, acc):
-            for u in range(unroll):
-                slot = k * unroll + u
-                acc = acc + lax.rsqrt(square(tgt, src, slot, slice(None))) * srcv[slot]
-            return acc
-
-        acc = lax.fori_loop(0, (n_blocks + unroll - 1) // unroll, step, jnp.zeros((LANES, LANES), jnp.float32))
+        end = jnp.int32(0)
+        for own in (True, False):
+            end = list_blocks(own, end, me, cell, counts, near, far, planes, put_near, put_far, put_none)
+
+        def step(i, acc):
+            return acc + (inv[t, 2 * i] * srcv[2 * i] + inv[t, 2 * i + 1] * srcv[2 * i + 1])
+
+        acc = lax.fori_loop(0, end // 2, step, jnp.zeros((LANES, LANES), jnp.float32))
         row = dot_nt(jnp.ones((ROWS, LANES), jnp.float32), acc)[0:1, :]
         out[0, t : t + 1, :] = row
-        there = PLANE + cell
-        scaled = pts[there, 4:5, :] * (pts[there, 3:4, :] + row)
+        point = mine[pl.ds(pl.multiple_of(top + cell * ROWS, ROWS), ROWS), :]
+        scaled = point[4:5] * (point[3:4] + row)
         v = cell_fields(mine, cell, groups, kinds) * scaled
-        w = weights(
-            cst, pts[there, 0:1, :], pts[there, 1:2, :], pts[there, 2:3, :], (0.0, 0.0, z_low), (1.0, 1.0, cell_side)
-        )
+        w = weights(cst, point[0:1], point[1:2], point[2:3], (0.0, 0.0, z_low), (1.0, 1.0, cell_side))
         total = total + dot_split(v, twice(w))
     for k in range(groups):
         out[1 + lax.bitwise_xor(group, k), :kinds, :] = total[k * kinds : (k + 1) * kinds, :]
@@ -291,14 +327,13 @@
     out[PLANE:, :] = jnp.where(low_half, total[:rows, :], total[rows:, :])
 
 
-def orbital_kernel(
-    batch, unit, steps, meta, counts, near, far, levels, screening, cst, table, before, mine, after, *refs
-):
-    parts, refs = refs[:-14], refs[-14:]
-    out, rate, slot_of, every, pts, val, mom, tgt, src, srcv, dist, inv, acc, total = refs
-    lay_out(parts, every)
-    put_points((before, mine, after), pts)
-    planes = every.shape[0]
+def orbital_kernel(own, planes, batch, steps, meta, counts, near, far, levels, screening, cst, inv, dist, *refs):
+    if own:
+        mine, hartree, out, rate, slot_of, units, val, mom, srcv, acc = refs
+    else:
+        before, after, partial, *parts = refs[:-9]
+        out, rate, slot_of, units, val, mom, srcv, acc, every = refs[-9:]
+        lay_out(parts, every)
     groups, cells, kinds, _ = out.shape
     orbs = groups * kinds
     me, group = meta[0], meta[1]
@@ -324,7 +359,6 @@
 
     n_levels, lane_slot = lax.fori_loop(0, orbs, rank, (jnp.int32(0), jnp.zeros((1, LANES), jnp.int32)))
     n_batches = (n_levels + batch - 1) // batch
-
     first_half = lax.broadcasted_iota(jnp.int32, (1, 2 * orbs), 1) < orbs
 
     def flip(v):
@@ -332,22 +366,24 @@
         square = jnp.concatenate([high, v - high, jnp.zeros((LANES - 2 * orbs, LANES), jnp.float32)], axis=0)
         return square.T[:, : 2 * orbs].astype(jnp.bfloat16)
 
-    for k in range(3):
+    for k in (1,) if own else (0, 2):
+        message = mine if own else (before if k == 0 else after)
         there = lax.bitwise_xor(me, jnp.clip(me - 1 + k, 0, planes - 1))
-        message = (before, mine, after)[k]
+        top = message.shape[0] - PLANE * ROWS
 
         def prepare(c, carry):
             at = k * PLANE + c
-            scaled = pts[at, 4:5, :] * (pts[at, 3:4, :] + every[there, pl.ds(c, 1), :])
-            v = cell_fields(message, c, groups, kinds) * scaled
+            point = message[pl.ds(pl.multiple_of(top + c * ROWS, ROWS), ROWS), :]
+            potential = point[3:4] + (hartree[pl.ds(c, 1), :] if own else every[there, pl.ds(c, 1), :])
+            v = cell_fields(message, c, groups, kinds) * (point[4:5] * potential)
             val[at] = flip(v)
             vh, vl = split(v)
             z_low = (me - 1 + k).astype(jnp.float32) * cell_side
             low = (*cell_low(c), z_low)
-            wh, wl = split(weights(cst, pts[at, 0:1, :], pts[at, 1:2, :], pts[at, 2:3, :], low, (cell_side,) * 3))
+            wh, wl = split(weights(cst, point[0:1], point[1:2], point[2:3], low, (cell_side,) * 3))
             all_of = dot_bf16(jnp.concatenate([wh, wl], axis=0), jnp.concatenate([vh, vh, vl, vl], axis=0))
             m = all_of[:HALF] + all_of[HALF:]
-            m = m[:, : 2 * orbs] + pltpu.roll(all_of[:HALF], 4 * orbs - 2 * orbs, 1)[:, : 2 * orbs]
+            m = m[:, : 2 * orbs] + pltpu.roll(all_of[:HALF], 2 * orbs, 1)[:, : 2 * orbs]
             high = m.astype(jnp.bfloat16).astype(jnp.float32)
             mom[at] = jnp.where(first_half, high, m - high).astype(jnp.bfloat16)
             return carry
@@ -364,75 +400,76 @@
         mom[3 * PLANE + g] = flip(jnp.concatenate(rows, axis=0))[:HALF]
         return c
 
-    lax.fori_loop(0, planes, put_plane, 0)
-
-    def put_near(j, slot):
-        srcv[j] = val[slot]
-
-    def put_far(j, first, second, live, low_half):
-        srcv[j, :HALF, :] = mom[first]
-        srcv[j, HALF:, :] = jnp.where(live, mom[second], jnp.zeros_like(mom[second]))
-
-    def put_none(j):
-        srcv[j] = jnp.zeros(srcv.shape[1:], srcv.dtype)
-
-    def products(b, first):
-        rates = [rate[b * batch + q] for q in range(batch)]
-        rows = []
-        for q in range(batch):
-            tiles = [(jnp.exp2(dist[first + h] * rates[q]) * inv[first + h]).astype(jnp.bfloat16) for h in range(unit)]
-            rows.append(jnp.concatenate(tiles, axis=1))
-        v = jnp.concatenate([srcv[first + h] for h in range(unit)], axis=0)
-        return jnp.dot(jnp.concatenate(rows, axis=0), v, preferred_element_type=jnp.float32)
-
-    def per_cell(t, carry):
+    if not own:
+        lax.fori_loop(0, planes, put_plane, 0)
+
+    def list_cell(t, carry):
+        def put_near(j, slot):
+            srcv[t, j] = val[slot]
+
+        def put_far(j, first, second, live):
+            srcv[t, j, :HALF, :] = mom[first]
+            srcv[t, j, HALF:, :] = jnp.where(live, mom[second], jnp.zeros_like(mom[second]))
+
+        def put_none(j):
+            srcv[t, j] = jnp.zeros(srcv.shape[2:], srcv.dtype)
+
         cell = target_cell(group, t, groups)
-        n_blocks = list_sources(me, cell, counts, near, far, planes, table, pts, src, put_near, put_far, put_none, unit)
-        n_loops = (n_blocks + unit - 1) // unit
-        put_targets(pts, cell, tgt)
-
-        def measure(c, x):
-            sq = square(tgt, src, c, slice(None))
-            i = lax.rsqrt(sq)
-            inv[c] = i
-            dist[c] = sq * i
+        begin = jnp.int32(0)
+        if not own:
+            begin = counts[cell, 1] + (counts[cell, 4] + 1) // 2
+            begin = (begin + 1) // 2 * 2
+        end = list_blocks(own, begin, me, cell, counts, near, far, planes, put_near, put_far, put_none)
+        units[0, t] = begin // 2
+        units[1, t] = end // 2
+
+        def clear_acc(b, x):
+            acc[t, b] = jnp.zeros(acc.shape[2:], jnp.float32)
             return x
 
-        lax.fori_loop(0, unit * n_loops, measure, 0)
-        total[...] = jnp.zeros(total.shape, jnp.float32)
-
-        def clear(b, x):
-            acc[b] = jnp.zeros(acc.shape[1:], jnp.float32)
-            return x
-
-        lax.fori_loop(0, n_batches, clear, 0)
-
-        def step(i, at):
-            b, u = at
-            for _ in range(steps):
-                acc[b] = acc[b] + products(b, unit * u)
-                wrap = u + 1 == n_loops
-                b, u = jnp.where(wrap, b + 1, b), jnp.where(wrap, 0, u + 1)
-            return b, u
-
-        lax.fori_loop(0, (n_batches * n_loops + steps - 1) // steps, step, (jnp.int32(0), jnp.int32(0)))
-
-        def choose(b, x):
-            add = total[...]
+        lax.fori_loop(0, n_batches, clear_acc, 0)
+        return carry
+
+    lax.fori_loop(0, cells, list_cell, 0)
+    work = sum(units[1, t] - units[0, t] for t in range(cells)) * n_batches
+
+    def step(i, at):
+        t, b, u = at
+        for _ in range(steps):
+            rows = []
+            for q in range(batch):
+                r = rate[b * batch + q]
+                tiles = [(jnp.exp2(dist[t, 2 * u + h] * r) * inv[t, 2 * u + h]).astype(jnp.bfloat16) for h in range(2)]
+                rows.append(jnp.concatenate(tiles, axis=1))
+            v = jnp.concatenate([srcv[t, 2 * u], srcv[t, 2 * u + 1]], axis=0)
+            acc[t, b] = acc[t, b] + jnp.dot(jnp.concatenate(rows, axis=0), v, preferred_element_type=jnp.float32)
+            wrap = u + 1 >= units[1, t]
+            b = jnp.where(wrap, b + 1, b)
+            over = b >= n_batches
+            done = over & (t + 1 >= cells)
+            t = jnp.where(over & (t + 1 < cells), t + 1, t)
+            b = jnp.where(done, n_batches, jnp.where(over, 0, b))
+            u = jnp.where(wrap, units[0, t], u + 1)
+        return t, b, u
+
+    lax.fori_loop(0, (work + steps - 1) // steps, step, (jnp.int32(0), jnp.int32(0), units[0, 0]))
+
+    def finish(t, carry):
+        def choose(b, add):
             for q in range(batch):
                 mine = lane_slot[:, : 2 * orbs] == b * batch + q
-                add = add + jnp.where(mine, acc[b, q * LANES : (q + 1) * LANES, :], 0.0)
-            total[...] = add
-            return x
-
-        lax.fori_loop(0, n_batches, choose, 0)
-        flipped = jnp.concatenate([total[...], jnp.zeros((LANES, LANES - 2 * orbs), jnp.float32)], axis=1).T
+                add = add + jnp.where(mine, acc[t, b, q * LANES : (q + 1) * LANES, :], 0.0)
+            return add
+
+        total = lax.fori_loop(0, n_batches, choose, jnp.zeros((LANES, 2 * orbs), jnp.float32))
+        flipped = jnp.concatenate([total, jnp.zeros((LANES, LANES - 2 * orbs), jnp.float32)], axis=1).T
         rows = (flipped[:orbs] + flipped[orbs : 2 * orbs]) * green_scale
         for k in range(groups):
-            out[k, t] = rows[k * kinds : (k + 1) * kinds]
+            mine = rows[k * kinds : (k + 1) * kinds]
+            out[k, t] = mine if own else mine + partial[k, t]
         return carry
 
-    lax.fori_loop(0, cells, per_cell, 0)
+    lax.fori_loop(0, cells, finish, 0)
 
 
 def place_kernel(meta, *refs):
@@ -459,7 +496,7 @@
         in_specs=[smem()] * smems + [vmem()] * (len(args) - smems),
         out_specs=jax.tree.map(lambda _: vmem(), out_shape),
         scratch_shapes=scratch,
-        compiler_params=pltpu.CompilerParams(vmem_limit_bytes=52 * 1024 * 1024),
+        compiler_params=pltpu.CompilerParams(vmem_limit_bytes=28 * 1024 * 1024),
         name=name,
     )(*args)
 
@@ -483,36 +520,53 @@
     ends = planes - 1
     up = [(i, i + 1) for i in range(ends)]
     down = [(i + 1, i) for i in range(ends)]
-    message = jnp.concatenate([f.reshape(kinds * cells, LANES) for f in fields] + [own.reshape(cells * ROWS, LANES)], axis=0)
-    windows = (lax.ppermute(message, "space", up), message, lax.ppermute(message, "space", down))
     cst = jnp.asarray(basis_rows())
     base_table = proxy_table(planes, window)
     shift = np.zeros(base_table.shape, np.float32)
     shift[:window, 2] = cell_side
     table = jnp.asarray(base_table) + jnp.asarray(shift) * (me - 1).astype(f32)
-    counts = jnp.stack(
-        [jnp.sum((near_cells >= 0).astype(jnp.int32), 1), jnp.sum((far_cells >= 0).astype(jnp.int32), 1)], axis=1
-    )
+    counts = []
+    for cells_of in (near_cells, far_cells):
+        slot = cells_of - me * cells
+        listed = cells_of >= 0
+        inside = (slot >= 0) & (slot < cells)
+        for chosen in (listed & (slot < 0), listed & inside, listed):
+            counts.append(jnp.sum(chosen.astype(jnp.int32), axis=1))
+    counts = jnp.stack(counts, axis=1)
+
     charges = call(
         charge_kernel, "charge", jax.ShapeDtypeStruct((2 * cells + ROWS, LANES), f32), 1, (meta, cst, own, *fields)
     )
+    message = jnp.concatenate([f.reshape(kinds * cells, LANES) for f in fields] + [own.reshape(cells * ROWS, LANES)], axis=0)
+    charges, message = lax.optimization_barrier((charges, message))
     charges = gather_parts(charges, "space", False)
-
-    unroll = 2
-    blocks = near_cells.shape[1] + (far_cells.shape[1] + planes + 1) // 2 + 8
+    before, mine, after = lax.ppermute(message, "space", up), message, lax.ppermute(message, "space", down)
+
+    most = near_cells.shape[1]
+    blocks = most + (window - most + planes + 1) // 2 + 4
+    pairs = pltpu.VMEM((share, blocks, LANES, LANES), f32)
+    inv, dist = call(
+        functools.partial(pairs_kernel, groups, planes),
+        "pairs",
+        (pairs, pairs),
+        4,
+        (meta, counts, near_cells, far_cells, table, before, mine, after),
+        [
+            pltpu.VMEM((window, ROWS, LANES), f32),
+            pltpu.VMEM((3, LANES, LANES), f32),
+            pltpu.VMEM((blocks, ROWS, LANES), f32),
+        ],
+    )
     shares = call(
-        functools.partial(hartree_kernel, unroll, groups, kinds),
+        functools.partial(hartree_kernel, groups, kinds),
         "hartree",
         jax.ShapeDtypeStruct((1 + groups, ROWS, LANES), f32),
         4,
-        (meta, counts, near_cells, far_cells, cst, table, marks, *windows, *charges),
+        (meta, counts, near_cells, far_cells, cst, marks, mine, inv, *charges),
         [
             pltpu.VMEM((planes, 2 * cells + ROWS, LANES), f32),
-            pltpu.VMEM((window, ROWS, LANES), f32),
             pltpu.VMEM((window, 1, LANES), f32),
             pltpu.VMEM((window + planes, 1, LANES), f32),
-            pltpu.VMEM((3, LANES, LANES), f32),
-            pltpu.VMEM((blocks, ROWS, LANES), f32),
             pltpu.VMEM((blocks, 1, LANES), f32),
         ],
     )
@@ -528,30 +582,32 @@
     )
     gathered = gather_parts(combined, "space", False)
 
-    batch, unit, steps = 4, 4, 9
+    batch, steps = 4, 16
     levels_at_most = -(-screening.shape[0] // batch) + 1
-    sent = call(
-        functools.partial(orbital_kernel, batch, unit, steps),
-        "orbitals",
-        jax.ShapeDtypeStruct((groups, share, kinds, LANES), f32),
-        6,
-        (meta, counts, near_cells, far_cells, levels, screening, cst, table, *windows, *gathered),
-        [
+
+    def orbital_part(own_plane, *args):
+        scratch = [
             pltpu.SMEM((screening.shape[0] + 2 * batch,), f32),
             pltpu.SMEM((screening.shape[0],), jnp.int32),
-            pltpu.VMEM((planes, cells + orbs // 2, LANES), f32),
-            pltpu.VMEM((window, ROWS, LANES), f32),
+            pltpu.SMEM((2, share), jnp.int32),
             pltpu.VMEM((window, LANES, 2 * orbs), bf16),
             pltpu.VMEM((window + planes, HALF, 2 * orbs), bf16),
-            pltpu.VMEM((3, LANES, LANES), f32),
-            pltpu.VMEM((blocks, ROWS, LANES), f32),
-            pltpu.VMEM((blocks, LANES, 2 * orbs), bf16),
-            pltpu.VMEM((blocks, LANES, LANES), f32),
-            pltpu.VMEM((blocks, LANES, LANES), f32),
-            pltpu.VMEM((levels_at_most, batch * LANES, 2 * orbs), f32),
-            pltpu.VMEM((LANES, 2 * orbs), f32),
-        ],
-    )
+            pltpu.VMEM((share, blocks, LANES, 2 * orbs), bf16),
+            pltpu.VMEM((share, levels_at_most, batch * LANES, 2 * orbs), f32),
+        ]
+        if not own_plane:
+            scratch.append(pltpu.VMEM((planes, cells + orbs // 2, LANES), f32))
+        return call(
+            functools.partial(orbital_kernel, own_plane, planes, batch, steps),
+            "own_orbitals" if own_plane else "orbitals",
+            jax.ShapeDtypeStruct((groups, share, kinds, LANES), f32),
+            6,
+            (meta, counts, near_cells, far_cells, levels, screening, cst, inv, dist, *args),
+            scratch,
+        )
+
+    partial = orbital_part(True, mine, hartree)
+    sent = orbital_part(False, before, after, partial, *gathered)
     parts = [sent[0]]
     for k in range(1, groups):
         parts.append(lax.ppermute(sent[k], "orb", [(i, i ^ k) for i in range(groups)]))

time: 113 us -> 141 us (1.25)
  local copies, waits for them, and re-layouts: 1.63 us -> 18 us
  Pallas kernels: 67 us -> 76 us
  other arithmetic: 3.74 us -> 6.46 us
  waiting for transfers between devices: 12.8 us -> 11 us
    unnamed x19 -> x55, local copies, waits for them, and re-layouts: 1.45 us -> 17.3 us
    pallas_call x5 -> x7, Pallas kernels: 67 us -> 76 us  [call(): pl.pallas_call(kernel, out_shape=out_shape, in_specs=[smem()] * smems + [...]
    ppermute x14, waiting for transfers between devices: 10.9 us -> 6.64 us  [gather_parts(): lax.ppermute(held, axis, [(i, i ^ have * j) for i in range(count)])]
    ppermute x3, waiting for transfers between devices: 1.88 us -> 4.38 us  [body(): lax.ppermute(sent[k], 'orb', [(i, i ^ k) for i in range(groups)])]
    ppermute x1, starting transfers between devices: 2.78 us -> 4.54 us  [body(): lax.ppermute(message, 'space', down)]
  transfers between devices with their start and end apart: 19 -> 19, of which waited for: 13 -> 5; matrix products, arithmetic and copies ran while one was open for 4% -> 6% of each run, Pallas kernels for 2% -> 20%
where the time goes in v1:
time: 141 us; the launch traced here: 139 us
  Pallas kernels  76 us (54%)
  starting transfers between devices  26.8 us (19%)
  local copies, waits for them, and re-layouts  18 us (13%)
  waiting for transfers between devices  11 us (8%)
  other arithmetic  6.46 us (5%)
    pallas_call x7, Pallas kernels, call(): pl.pallas_call(kernel, out_shape=out_shape, in_specs=[smem()] * smems + [...  76 us
    unnamed x55, local copies, waits for them, and re-layouts  17.3 us
    ppermute x14, starting transfers between devices, gather_parts(): lax.ppermute(held, axis, [(i, i ^ have * j) for i in range(count)])  15.9 us
    ppermute x14, waiting for transfers between devices, gather_parts(): lax.ppermute(held, axis, [(i, i ^ have * j) for i in range(count)])  6.64 us
    ppermute x1, starting transfers between devices, body(): lax.ppermute(message, 'space', down)  4.54 us
    ppermute x3, starting transfers between devices, body(): lax.ppermute(sent[k], 'orb', [(i, i ^ k) for i in range(groups)])  4.44 us
    ppermute x3, waiting for transfers between devices, body(): lax.ppermute(sent[k], 'orb', [(i, i ^ k) for i in range(groups)])  4.38 us
  transfers between devices with their start and end apart: 19, of which 5 were waited for; matrix products, arithmetic and copies ran while one was open for 6% of the time, Pallas kernels for 20%

profile of v1, /device:TPU:4, one launch (start us, length us, event | category | flops | bytes accessed | tf_op | source)
XLA Modules:
  0.0 139.3 jit_solution(6946730392886236540)
XLA Ops:
  0.7 1.6 %collective-permute-start = (f32[1,8,16,128]{3,2,1,0:T(8,128)}, f32[1,8,16,128]{3,2,1,0:T(8,128)S(1)}, u32[]{:S(2)}, u32[]{:S(2)}) collective-permute-start(f32[1,8,16,128]{3,2,1,0:T(8,128)} %bitcast.49), channel_id=1, source_target_pairs={{0,8},{8,0},{16,24},{24,16},{1,9},{9,1},{17,25},{25,17},{2,10},{10... | collective-permute-start | bytes 196616 | tf_op jit(solution)/shard_map/ppermute | solution.py:90
  2.3 2.6 %collective-permute-start.1 = (f32[1,8,16,128]{3,2,1,0:T(8,128)}, f32[1,8,16,128]{3,2,1,0:T(8,128)S(1)}, u32[]{:S(2)}, u32[]{:S(2)}) collective-permute-start(f32[1,8,16,128]{3,2,1,0:T(8,128)} %bitcast.50), channel_id=1, source_target_pairs={{0,16},{8,24},{16,0},{24,8},{1,17},{9,25},{17,1},{25,9},{2,18},{10... | collective-permute-start | bytes 196616 | tf_op jit(solution)/shard_map/ppermute | solution.py:90
  4.9 0.2 collective-permute-start.2
  5.1 0.8 copy.21
  5.9 0.7 broadcast_multiply_fusion
  6.6 0.8 constant_dynamic-update-slice_fusion.3
  7.4 0.1 pad.16.clone
  7.5 0.8 convert_reduce_fusion.3
  8.3 1.1 multiply_add_fusion.table
  9.4 0.8 maximum_maximum_fusion.own
  10.2 0.1 pad_add_fusion.meta
  10.3 0.9 collective-permute-done.2
  11.2 0.8 bitcast_dynamic-update-slice_fusion.mine.refs_0_
  12.0 0.8 copy-done.12
  12.8 0.8 copy-done.15
  13.6 2.4 %charge.1 = f32[40,128]{1,0:T(8,128)S(1)} custom-call(s32[2]{0:T(128)S(1)} %pad_add_fusion.meta, f32[12,8,128]{2,1,0:T(8,128)S(1)} %copy-done.12, f32[16,8,128]{2,1,0:T(8,128)S(1)} %maximum_maximum_fusion.own, f32[8,16,128]{2,1,0:T(8,128)S(1)} %copy-done.15, f32[8,16,128]{2,1,0:T(8,128)S(1)} %bitcast.54, f32[8,16,128]{2,1,0:T(8,128)S(1)} %bitcast.56, ...), custom_call_target="tpu_custom_call" | custom-call | tf_op jit(solution)/shard_map/charge/pallas_call | solution.py:493
  16.1 1.9 %collective-permute-start.3 = (f32[640,128]{1,0:T(8,128)S(1)}, f32[640,128]{1,0:T(8,128)S(1)}, u32[]{:S(2)}, u32[]{:S(2)}) collective-permute-start(f32[640,128]{1,0:T(8,128)S(1)} %bitcast_dynamic-update-slice_fusion.mine.refs_0_), channel_id=1, source_target_pairs={{0,1},{1,2},{2,3},{3,4},{4,5},{5,6},{6,7},{8,9},{9,10},{10,11},{11... | collective-permute-start | bytes 983048 | tf_op jit(solution)/shard_map/ppermute | solution.py:543
  18.0 4.5 %collective-permute-start.4 = (f32[640,128]{1,0:T(8,128)S(1)}, f32[640,128]{1,0:T(8,128)S(1)}, u32[]{:S(2)}, u32[]{:S(2)}) collective-permute-start(f32[640,128]{1,0:T(8,128)S(1)} %bitcast_dynamic-update-slice_fusion.mine.refs_0_), channel_id=1, source_target_pairs={{1,0},{2,1},{3,2},{4,3},{5,4},{6,5},{7,6},{9,8},{10,9},{11,10},{12... | collective-permute-start | bytes 983048 | tf_op jit(solution)/shard_map/ppermute | solution.py:543
  22.5 0.1 collective-permute-start.5
  22.6 0.8 convert_reduce_fusion
  23.5 0.7 convert_element_type.35
  24.1 0.6 pad_maximum_fusion.refs_0_
  24.8 0.6 collective-permute-start.6
  25.3 0.5 collective-permute-start.7
  25.9 2.4 %collective-permute-start.8 = (f32[2,40,128]{2,1,0:T(8,128)}, f32[2,40,128]{2,1,0:T(8,128)}, u32[]{:S(2)}, u32[]{:S(2)}) collective-permute-start(f32[2,40,128]{2,1,0:T(8,128)} %pad_maximum_fusion.refs_0_), channel_id=1, source_target_pairs={{0,6},{1,7},{2,4},{3,5},{4,2},{5,3},{6,0},{7,1},{8,14},{9,15},{10,... | collective-permute-start | bytes 122888 | tf_op jit(solution)/shard_map/ppermute | solution.py:90
  28.2 0.1 copy.13
  28.3 0.1 copy.14
  28.4 0.1 copy.15
  28.5 0.1 copy.16
  28.6 0.1 copy.17
  28.7 0.1 copy.18
  28.7 0.1 stack.39.counts
  28.9 0.7 copy-done.6
  29.6 0.8 copy-done.9
  30.4 1.0 copy-done.3
  31.3 1.0 copy-done.7
  32.3 1.0 copy-done.10
  33.3 0.7 copy-done.16
  34.0 0.7 copy-done.18
  34.7 7.9 %pairs.1 = (f32[4,46,128,128]{3,2,1,0:T(8,128)S(1)}, f32[4,46,128,128]{3,2,1,0:T(8,128)S(1)}) custom-call(s32[2]{0:T(128)S(1)} %pad_add_fusion.meta, s32[16,6]{1,0:T(8,128)S(1)} %stack.39.counts, s32[16,27]{1,0:T(8,128)S(1)} %copy-done.16, s32[16,42]{1,0:T(8,128)S(1)} %copy-done.18, f32[56,8,128]{2,1,0:T(8,128)S(1)} %multiply_add_fusion.table, ...), custom_call_target="tpu_custom_call" | custom-call | tf_op jit(solution)/shard_map/pairs/pallas_call | solution.py:493
  42.6 4.4 %copy-done = f32[4,46,128,128]{3,2,1,0:T(8,128)} copy-done((f32[4,46,128,128]{3,2,1,0:T(8,128)}, f32[4,46,128,128]{3,2,1,0:T(8,128)S(1)}, u32[]{:S(2)}) %copy-start) | copy-done | bytes 12058648
  47.1 1.1 copy-done.4
  48.2 1.0 copy-done.13
  49.2 6.7 %hartree.1.refs_0_ = f32[5,8,128]{2,1,0:T(8,128)S(1)} custom-call(s32[2]{0:T(128)S(1)} %pad_add_fusion.meta, s32[16,6]{1,0:T(8,128)S(1)} %stack.39.counts, s32[16,27]{1,0:T(8,128)S(1)} %copy-done.16, s32[16,42]{1,0:T(8,128)S(1)} %copy-done.18, f32[12,8,128]{2,1,0:T(8,128)S(1)} %copy-done.13, f32[1,128]{1,0:T(1,128)S(1)} %pad_bitcast_fusion.marks, ...), custom_call_target="tpu_custom_call" | custom-call | tf_op jit(solution)/shard_map/hartree/pallas_call | solution.py:493
  55.9 0.0 collective-permute-start.9
  55.9 3.4 %collective-permute-start.10 = (f32[1,5,8,128]{3,2,1,0:T(8,128)S(1)}, f32[1,5,8,128]{3,2,1,0:T(8,128)S(1)}, u32[]{:S(2)}, u32[]{:S(2)}) collective-permute-start(f32[1,5,8,128]{3,2,1,0:T(8,128)S(1)} %bitcast.60), channel_id=1, source_target_pairs={{0,16},{8,24},{16,0},{24,8},{1,17},{9,25},{17,1},{25,9},{2,18},{10... | collective-permute-start | bytes 61448 | tf_op jit(solution)/shard_map/ppermute | solution.py:90
  59.3 1.0 collective-permute-start.11
  60.3 4.6 %collective-permute-done.11 = f32[1,5,8,128]{3,2,1,0:T(8,128)S(1)} collective-permute-done((f32[1,5,8,128]{3,2,1,0:T(8,128)S(1)}, f32[1,5,8,128]{3,2,1,0:T(8,128)S(1)}, u32[]{:S(2)}, u32[]{:S(2)}) %collective-permute-start.11) | collective-permute-done | bytes 20512 | tf_op jit(solution)/shard_map/ppermute | solution.py:90
  64.9 1.2 combine.1
  66.1 1.2 collective-permute-done.12
  67.2 0.8 collective-permute-start.13
  68.0 0.3 collective-permute-start.14
  68.3 2.4 %collective-permute-start.15 = (f32[2,32,128]{2,1,0:T(8,128)S(1)}, f32[2,32,128]{2,1,0:T(8,128)S(1)}, u32[]{:S(2)}, u32[]{:S(2)}) collective-permute-start(f32[2,32,128]{2,1,0:T(8,128)S(1)} %pad_maximum_fusion.1.refs_3_), channel_id=1, source_target_pairs={{0,6},{1,7},{2,4},{3,5},{4,2},{5,3},{6,0},{7,1},{8,14},{9,15},{10,... | collective-permute-start | bytes 98312 | tf_op jit(solution)/shard_map/ppermute | solution.py:90
  70.7 0.1 maximum_convert_fusion.levels
  70.8 0.7 copy-done.20
  71.5 19.8 %own_orbitals.1.refs_2_ = f32[4,4,8,128]{3,2,1,0:T(8,128)S(1)} custom-call(s32[2]{0:T(128)S(1)} %pad_add_fusion.meta, s32[16,6]{1,0:T(8,128)S(1)} %stack.39.counts, s32[16,27]{1,0:T(8,128)S(1)} %copy-done.17, s32[16,42]{1,0:T(8,128)S(1)} %copy-done.18, s32[32]{0:T(128)S(1)} %maximum_convert_fusion.levels, f32[32]{0:T(128)S(1)} %copy-done.21, ...), custom_call_target="tpu_custom_call" | custom-call | tf_op jit(solution)/shard_map/own_orbitals/pallas_call | solution.py:493
  91.4 1.0 copy-done.11
  92.4 36.9 %orbitals.1 = f32[4,4,8,128]{3,2,1,0:T(8,128)S(1)} custom-call(s32[2]{0:T(128)S(1)} %pad_add_fusion.meta, s32[16,6]{1,0:T(8,128)S(1)} %stack.39.counts, s32[16,27]{1,0:T(8,128)S(1)} %copy-done.17, s32[16,42]{1,0:T(8,128)S(1)} %copy-done.19, s32[32]{0:T(128)S(1)} %maximum_convert_fusion.levels, f32[32]{0:T(128)S(1)} %copy-done.21, ...), custom_call_target="tpu_custom_call" | custom-call | tf_op jit(solution)/shard_map/orbitals/pallas_call | solution.py:493
  129.2 0.1 collective-permute-start.16
  129.3 3.2 %collective-permute-start.17 = (f32[4,8,128]{2,1,0:T(8,128)S(1)}, f32[4,8,128]{2,1,0:T(8,128)S(1)}, u32[]{:S(2)}, u32[]{:S(2)}) collective-permute-start(f32[4,8,128]{2,1,0:T(8,128)S(1)} %get-tuple-element.21), channel_id=1, source_target_pairs={{0,16},{8,24},{16,0},{24,8},{1,17},{9,25},{17,1},{25,9},{2,18},{10... | collective-permute-start | bytes 49160 | tf_op jit(solution)/shard_map/ppermute | solution.py:613
  132.5 1.2 collective-permute-start.18
  133.7 0.6 collective-permute-done.17.refs_2_
  134.3 3.8 %collective-permute-done.18.refs_3_ = f32[4,8,128]{2,1,0:T(8,128)S(1)} collective-permute-done((f32[4,8,128]{2,1,0:T(8,128)S(1)}, f32[4,8,128]{2,1,0:T(8,128)S(1)}, u32[]{:S(2)}, u32[]{:S(2)}) %collective-permute-start.18) | collective-permute-done | bytes 16416 | tf_op jit(solution)/shard_map/ppermute | solution.py:613
  138.1 1.2 place.1
  (63 shorter events, 0.2 us)
Async XLA Ops:
  0.6 70.2 %copy-start.17 = (s32[16,27]{1,0:T(8,128)S(1)}, s32[16,27]{1,0:T(8,128)}, u32[]{:S(2)}) copy-start(s32[16,27]{1,0:T(8,128)} %near.7) | copy-start | bytes 5188
  0.6 70.2 %copy-start.21 = (f32[32]{0:T(128)S(1)}, f32[32]{0:T(128)}, u32[]{:S(2)}) copy-start(f32[32]{0:T(128)} %screening.3) | copy-start | bytes 388
  0.7 9.6 %collective-permute-start = (f32[1,8,16,128]{3,2,1,0:T(8,128)}, f32[1,8,16,128]{3,2,1,0:T(8,128)S(1)}, u32[]{:S(2)}, u32[]{:S(2)}) collective-permute-start(f32[1,8,16,128]{3,2,1,0:T(8,128)} %bitcast.49), channel_id=1, source_target_pairs={{0,8},{8,0},{16,24},{24,16},{1,9},{9,1},{17,25},{25,17},{2,10},{10... | collective-permute-start | bytes 196616 | tf_op jit(solution)/shard_map/ppermute | solution.py:90
  2.3 8.0 %collective-permute-start.1 = (f32[1,8,16,128]{3,2,1,0:T(8,128)}, f32[1,8,16,128]{3,2,1,0:T(8,128)S(1)}, u32[]{:S(2)}, u32[]{:S(2)}) collective-permute-start(f32[1,8,16,128]{3,2,1,0:T(8,128)} %bitcast.50), channel_id=1, source_target_pairs={{0,16},{8,24},{16,0},{24,8},{1,17},{9,25},{17,1},{25,9},{2,18},{10... | collective-permute-start | bytes 196616 | tf_op jit(solution)/shard_map/ppermute | solution.py:90
  4.9 6.3 %collective-permute-start.2 = (f32[1,8,16,128]{3,2,1,0:T(8,128)}, f32[1,8,16,128]{3,2,1,0:T(8,128)S(1)}, u32[]{:S(2)}, u32[]{:S(2)}) collective-permute-start(f32[1,8,16,128]{3,2,1,0:T(8,128)} %bitcast.51), channel_id=1, source_target_pairs={{0,24},{8,16},{16,8},{24,0},{1,25},{9,17},{17,9},{25,1},{2,26},{10... | collective-permute-start | bytes 196616 | tf_op jit(solution)/shard_map/ppermute | solution.py:90
  12.0 16.9 %copy-start.2 = (f32[640,128]{1,0:T(8,128)}, f32[640,128]{1,0:T(8,128)S(1)}, u32[]{:S(2)}) copy-start(f32[640,128]{1,0:T(8,128)S(1)} %bitcast_dynamic-update-slice_fusion.mine.refs_0_) | copy-start | bytes 983044
  12.0 0.8 copy-start.12
  12.8 0.8 copy-start.15
  16.1 12.8 %collective-permute-start.3 = (f32[640,128]{1,0:T(8,128)S(1)}, f32[640,128]{1,0:T(8,128)S(1)}, u32[]{:S(2)}, u32[]{:S(2)}) collective-permute-start(f32[640,128]{1,0:T(8,128)S(1)} %bitcast_dynamic-update-slice_fusion.mine.refs_0_), channel_id=1, source_target_pairs={{0,1},{1,2},{2,3},{3,4},{4,5},{5,6},{6,7},{8,9},{9,10},{10,11},{11... | collective-permute-start | bytes 983048 | tf_op jit(solution)/shard_map/ppermute | solution.py:543
  18.0 11.6 %collective-permute-start.4 = (f32[640,128]{1,0:T(8,128)S(1)}, f32[640,128]{1,0:T(8,128)S(1)}, u32[]{:S(2)}, u32[]{:S(2)}) collective-permute-start(f32[640,128]{1,0:T(8,128)S(1)} %bitcast_dynamic-update-slice_fusion.mine.refs_0_), channel_id=1, source_target_pairs={{1,0},{2,1},{3,2},{4,3},{5,4},{6,5},{7,6},{9,8},{10,9},{11,10},{12... | collective-permute-start | bytes 983048 | tf_op jit(solution)/shard_map/ppermute | solution.py:543
  22.5 1.6 %collective-permute-start.5 = (f32[1,40,128]{2,1,0:T(8,128)S(1)}, f32[1,40,128]{2,1,0:T(8,128)S(1)}, u32[]{:S(2)}, u32[]{:S(2)}) collective-permute-start(f32[1,40,128]{2,1,0:T(8,128)S(1)} %bitcast.62), channel_id=1, source_target_pairs={{0,1},{1,0},{2,3},{3,2},{4,5},{5,4},{6,7},{7,6},{8,9},{9,8},{10,11... | collective-permute-start | bytes 61448 | tf_op jit(solution)/shard_map/ppermute | solution.py:90
  24.8 22.3 %collective-permute-start.6 = (f32[2,40,128]{2,1,0:T(8,128)}, f32[2,40,128]{2,1,0:T(8,128)}, u32[]{:S(2)}, u32[]{:S(2)}) collective-permute-start(f32[2,40,128]{2,1,0:T(8,128)} %pad_maximum_fusion.refs_0_), channel_id=1, source_target_pairs={{0,2},{1,3},{2,0},{3,1},{4,6},{5,7},{6,4},{7,5},{8,10},{9,11},{10,... | collective-permute-start | bytes 122888 | tf_op jit(solution)/shard_map/ppermute | solution.py:90
  25.3 21.7 %collective-permute-start.7 = (f32[2,40,128]{2,1,0:T(8,128)}, f32[2,40,128]{2,1,0:T(8,128)}, u32[]{:S(2)}, u32[]{:S(2)}) collective-permute-start(f32[2,40,128]{2,1,0:T(8,128)} %pad_maximum_fusion.refs_0_), channel_id=1, source_target_pairs={{0,4},{1,5},{2,6},{3,7},{4,0},{5,1},{6,2},{7,3},{8,12},{9,13},{10,... | collective-permute-start | bytes 122888 | tf_op jit(solution)/shard_map/ppermute | solution.py:90
  25.9 21.2 %collective-permute-start.8 = (f32[2,40,128]{2,1,0:T(8,128)}, f32[2,40,128]{2,1,0:T(8,128)}, u32[]{:S(2)}, u32[]{:S(2)}) collective-permute-start(f32[2,40,128]{2,1,0:T(8,128)} %pad_maximum_fusion.refs_0_), channel_id=1, source_target_pairs={{0,6},{1,7},{2,4},{3,5},{4,2},{5,3},{6,0},{7,1},{8,14},{9,15},{10,... | collective-permute-start | bytes 122888 | tf_op jit(solution)/shard_map/ppermute | solution.py:90
  28.8 0.8 copy-start.6
  29.6 0.8 copy-start.9
  30.4 1.0 copy-start.3
  31.3 1.0 copy-start.7
  32.3 1.0 copy-start.10
  33.3 0.7 copy-start.16
  34.0 0.7 copy-start.18
  34.7 36.1 %copy-start.5 = (f32[640,128]{1,0:T(8,128)S(1)}, f32[640,128]{1,0:T(8,128)}, u32[]{:S(2)}) copy-start(f32[640,128]{1,0:T(8,128)} %copy-done.2) | copy-start | bytes 983044
  34.7 36.1 %copy-start.14 = (f32[12,8,128]{2,1,0:T(8,128)S(1)}, f32[12,8,128]{2,1,0:T(8,128)}, u32[]{:S(2)}) copy-start(f32[12,8,128]{2,1,0:T(8,128)} %constant.30.clone.cst) | copy-start | bytes 147460
  42.6 4.4 %copy-start = (f32[4,46,128,128]{3,2,1,0:T(8,128)}, f32[4,46,128,128]{3,2,1,0:T(8,128)S(1)}, u32[]{:S(2)}) copy-start(f32[4,46,128,128]{3,2,1,0:T(8,128)S(1)} %get-tuple-element.11.dist) | copy-start | bytes 36175876
  47.0 23.8 %copy-start.1 = (f32[4,46,128,128]{3,2,1,0:T(8,128)S(1)}, f32[4,46,128,128]{3,2,1,0:T(8,128)}, u32[]{:S(2)}) copy-start(f32[4,46,128,128]{3,2,1,0:T(8,128)} %copy-done) | copy-start | bytes 36175876
  47.1 1.1 copy-start.4
  48.2 1.0 copy-start.13
  49.2 42.1 %slice-start = ((s8[12058624]{0:T(1024)(128)(4,1)}), s8[3670016]{0:T(1024)(128)(4,1)S(1)}, s32[]{:S(2)}) async-start(s8[12058624]{0:T(1024)(128)(4,1)} %bitcast.47), calls=%async_computation | async-start | bytes 7340032
  49.2 42.2 %slice-start.1 = ((s8[12058624]{0:T(1024)(128)(4,1)}), s8[4194304]{0:T(1024)(128)(4,1)S(1)}, s32[]{:S(2)}) async-start(s8[12058624]{0:T(1024)(128)(4,1)} %bitcast.47), calls=%async_computation.1 | async-start | bytes 8388608
  55.9 9.0 %collective-permute-start.9 = (f32[1,5,8,128]{3,2,1,0:T(8,128)S(1)}, f32[1,5,8,128]{3,2,1,0:T(8,128)S(1)}, u32[]{:S(2)}, u32[]{:S(2)}) collective-permute-start(f32[1,5,8,128]{3,2,1,0:T(8,128)S(1)} %bitcast.59), channel_id=1, source_target_pairs={{0,8},{8,0},{16,24},{24,16},{1,9},{9,1},{17,25},{25,17},{2,10},{10... | collective-permute-start | bytes 61448 | tf_op jit(solution)/shard_map/ppermute | solution.py:90
  55.9 8.9 %collective-permute-start.10 = (f32[1,5,8,128]{3,2,1,0:T(8,128)S(1)}, f32[1,5,8,128]{3,2,1,0:T(8,128)S(1)}, u32[]{:S(2)}, u32[]{:S(2)}) collective-permute-start(f32[1,5,8,128]{3,2,1,0:T(8,128)S(1)} %bitcast.60), channel_id=1, source_target_pairs={{0,16},{8,24},{16,0},{24,8},{1,17},{9,25},{17,1},{25,9},{2,18},{10... | collective-permute-start | bytes 61448 | tf_op jit(solution)/shard_map/ppermute | solution.py:90
  59.3 5.6 %collective-permute-start.11 = (f32[1,5,8,128]{3,2,1,0:T(8,128)S(1)}, f32[1,5,8,128]{3,2,1,0:T(8,128)S(1)}, u32[]{:S(2)}, u32[]{:S(2)}) collective-permute-start(f32[1,5,8,128]{3,2,1,0:T(8,128)S(1)} %bitcast.61), channel_id=1, source_target_pairs={{0,24},{8,16},{16,8},{24,0},{1,25},{9,17},{17,9},{25,1},{2,26},{10... | collective-permute-start | bytes 61448 | tf_op jit(solution)/shard_map/ppermute | solution.py:90
  66.0 1.2 collective-permute-start.12
  67.2 24.1 %collective-permute-start.13 = (f32[2,32,128]{2,1,0:T(8,128)S(1)}, f32[2,32,128]{2,1,0:T(8,128)S(1)}, u32[]{:S(2)}, u32[]{:S(2)}) collective-permute-start(f32[2,32,128]{2,1,0:T(8,128)S(1)} %pad_maximum_fusion.1.refs_3_), channel_id=1, source_target_pairs={{0,2},{1,3},{2,0},{3,1},{4,6},{5,7},{6,4},{7,5},{8,10},{9,11},{10,... | collective-permute-start | bytes 98312 | tf_op jit(solution)/shard_map/ppermute | solution.py:90
  68.0 23.3 %collective-permute-start.14 = (f32[2,32,128]{2,1,0:T(8,128)S(1)}, f32[2,32,128]{2,1,0:T(8,128)S(1)}, u32[]{:S(2)}, u32[]{:S(2)}) collective-permute-start(f32[2,32,128]{2,1,0:T(8,128)S(1)} %pad_maximum_fusion.1.refs_3_), channel_id=1, source_target_pairs={{0,4},{1,5},{2,6},{3,7},{4,0},{5,1},{6,2},{7,3},{8,12},{9,13},{10,... | collective-permute-start | bytes 98312 | tf_op jit(solution)/shard_map/ppermute | solution.py:90
  68.3 23.0 %collective-permute-start.15 = (f32[2,32,128]{2,1,0:T(8,128)S(1)}, f32[2,32,128]{2,1,0:T(8,128)S(1)}, u32[]{:S(2)}, u32[]{:S(2)}) collective-permute-start(f32[2,32,128]{2,1,0:T(8,128)S(1)} %pad_maximum_fusion.1.refs_3_), channel_id=1, source_target_pairs={{0,6},{1,7},{2,4},{3,5},{4,2},{5,3},{6,0},{7,1},{8,14},{9,15},{10,... | collective-permute-start | bytes 98312 | tf_op jit(solution)/shard_map/ppermute | solution.py:90
  70.8 0.7 copy-start.20
  71.5 19.8 %slice-start.2 = ((s8[12058624]{0:T(1024)(128)(4,1)}), s8[4194304]{0:T(1024)(128)(4,1)S(1)}, s32[]{:S(2)}) async-start(s8[12058624]{0:T(1024)(128)(4,1)} %bitcast.47), calls=%async_computation.2 | async-start | bytes 8388608
  71.5 19.8 %copy-start.8 = (f32[640,128]{1,0:T(8,128)S(1)}, f32[640,128]{1,0:T(8,128)}, u32[]{:S(2)}) copy-start(f32[640,128]{1,0:T(8,128)} %copy-done.6) | copy-start | bytes 983044
  71.5 19.8 %copy-start.19 = (s32[16,42]{1,0:T(8,128)S(1)}, s32[16,42]{1,0:T(8,128)}, u32[]{:S(2)}) copy-start(s32[16,42]{1,0:T(8,128)} %far.7) | copy-start | bytes 8068
  91.4 1.0 copy-start.11
  129.2 4.5 %collective-permute-start.16 = (f32[4,8,128]{2,1,0:T(8,128)S(1)}, f32[4,8,128]{2,1,0:T(8,128)S(1)}, u32[]{:S(2)}, u32[]{:S(2)}) collective-permute-start(f32[4,8,128]{2,1,0:T(8,128)S(1)} %get-tuple-element.22), channel_id=1, source_target_pairs={{0,8},{8,0},{16,24},{24,16},{1,9},{9,1},{17,25},{25,17},{2,10},{10... | collective-permute-start | bytes 49160 | tf_op jit(solution)/shard_map/ppermute | solution.py:613
  129.3 4.9 %collective-permute-start.17 = (f32[4,8,128]{2,1,0:T(8,128)S(1)}, f32[4,8,128]{2,1,0:T(8,128)S(1)}, u32[]{:S(2)}, u32[]{:S(2)}) collective-permute-start(f32[4,8,128]{2,1,0:T(8,128)S(1)} %get-tuple-element.21), channel_id=1, source_target_pairs={{0,16},{8,24},{16,0},{24,8},{1,17},{9,25},{17,1},{25,9},{2,18},{10... | collective-permute-start | bytes 49160 | tf_op jit(solution)/shard_map/ppermute | solution.py:613
  132.5 5.5 %collective-permute-start.18 = (f32[4,8,128]{2,1,0:T(8,128)S(1)}, f32[4,8,128]{2,1,0:T(8,128)S(1)}, u32[]{:S(2)}, u32[]{:S(2)}) collective-permute-start(f32[4,8,128]{2,1,0:T(8,128)S(1)} %get-tuple-element.20), channel_id=1, source_target_pairs={{0,24},{8,16},{16,8},{24,0},{1,25},{9,17},{17,9},{25,1},{2,26},{10... | collective-permute-start | bytes 49160 | tf_op jit(solution)/shard_map/ppermute | solution.py:613

commit v2 on v0

--- a/solution.py
+++ b/solution.py
@@ -80,7 +80,7 @@
     return lax.dot_general(a, b, (((1,), (1,)), ((), ())), precision=highest, preferred_element_type=jnp.float32)
 
 
-def gather_parts(block, axis, pairs):
+def gather_parts(block, axis, pairs, later=()):
     count = lax.axis_size(axis)
     parts = [block[None]]
     while sum(p.shape[0] for p in parts) < count:
@@ -88,11 +88,13 @@
         have = held.shape[0]
         steps = range(1, 4 if (have > 1 or pairs) and have * 4 <= count else 2)
         parts = [held] + [lax.ppermute(held, axis, [(i, i ^ (have * j)) for i in range(count)]) for j in steps]
-    return parts
+        if later and have == 1:
+            parts[1], later = lax.optimization_barrier((parts[1], later))
+    return parts, later
 
 
 def gather_list(block, axis):
-    parts = gather_parts(block, axis, True)
+    parts, _ = gather_parts(block, axis, True)
     return [p[k] for p in parts for k in range(p.shape[0])]
 
 
@@ -152,19 +154,16 @@
     return below, below + jnp.maximum(planes - 2 - me, 0)
 
 
-def list_sources(me, cell, counts, near, far, planes, table, pts, src, put_near, put_far, put_none, multiple):
+def list_blocks(me, cell, counts, near, far, planes, put_near, put_far, put_none, multiple):
     window = 3 * PLANE
     base = (me - 1) * PLANE
     below, n_planes = live_planes(me, planes)
-    low_half = lax.broadcasted_iota(jnp.int32, (1, LANES), 1) < HALF
     n_near, n_far = counts[cell, 0], counts[cell, 1]
     n_items = n_far + n_planes
     n_pairs = (n_items + 1) // 2
 
     def near_step(j, c):
-        slot = near[cell, j] - base
-        src[j] = pts[slot]
-        put_near(j, slot)
+        put_near(j, near[cell, j] - base)
         return c
 
     lax.fori_loop(0, n_near, near_step, 0)
@@ -177,17 +176,17 @@
         return jnp.where(j < n_far, slot, window + level)
 
     def far_step(j, c):
-        first, second = item(2 * j), item(2 * j + 1)
-        src[n_near + j] = jnp.where(low_half, table[first], table[second])
-        put_far(n_near + j, first, second, 2 * j + 1 < n_items, low_half)
+        put_far(n_near + j, item(2 * j), item(2 * j + 1), 2 * j + 1 < n_items)
         return c
 
     lax.fori_loop(0, n_pairs, far_step, 0)
-    n_blocks = n_near + n_pairs
     for u in range(multiple - 1):
-        src[n_blocks + u] = jnp.zeros(src.shape[1:], jnp.float32)
-        put_none(n_blocks + u)
-    return n_blocks
+        put_none(n_near + n_pairs + u)
+    return n_near + n_pairs
+
+
+def in_low_half():
+    return lax.broadcasted_iota(jnp.int32, (1, LANES), 1) < HALF
 
 
 def put_targets(pts, cell, tgt):
@@ -202,24 +201,45 @@
     return (dx * dx + dy * dy) + (dz * dz + soften)
 
 
-def put_points(messages, pts):
-    for k, message in enumerate(messages):
-        top = message.shape[0] - PLANE * ROWS
-        for c in range(PLANE):
-            pts[k * PLANE + c] = message[top + c * ROWS : top + (c + 1) * ROWS, :]
-
-
 def cell_fields(message, c, groups, kinds):
     rows = kinds * PLANE
-    return jnp.concatenate(
-        [message[pl.ds(g * rows + c, kinds, stride=PLANE), :] for g in range(groups)], axis=0
-    )
-
-
-def hartree_kernel(unroll, groups, kinds, meta, counts, near, far, cst, table, marks, before, mine, after, *refs):
-    parts, (out, every, pts, val, mom, tgt, src, srcv) = refs[:-8], refs[-8:]
+    return jnp.concatenate([message[pl.ds(g * rows + c, kinds, stride=PLANE), :] for g in range(groups)], axis=0)
+
+
+def pairs_kernel(groups, planes, unit, meta, counts, near, far, table, before, mine, after, out, pts, tgt, src):
+    for k, points in enumerate((before, mine, after)):
+        pts[k * PLANE : (k + 1) * PLANE] = points[...]
+    me, group = meta[0], meta[1]
+    low_half = in_low_half()
+
+    def put_near(j, slot):
+        src[j] = pts[slot]
+
+    def put_far(j, first, second, live):
+        src[j] = jnp.where(low_half, table[first], table[second])
+
+    def put_none(j):
+        src[j] = jnp.zeros(src.shape[1:], jnp.float32)
+
+    def per_cell(t, carry):
+        cell = target_cell(group, t, groups)
+        n_blocks = list_blocks(me, cell, counts, near, far, planes, put_near, put_far, put_none, unit)
+        put_targets(pts, cell, tgt)
+
+        def measure(i, x):
+            for u in range(unit):
+                out[t, unit * i + u] = square(tgt, src, unit * i + u, slice(None))
+            return x
+
+        lax.fori_loop(0, (n_blocks + unit - 1) // unit, measure, 0)
+        return carry
+
+    lax.fori_loop(0, PLANE // groups, per_cell, 0)
+
+
+def hartree_kernel(groups, kinds, meta, counts, near, far, cst, marks, own, mine, squares, *refs):
+    parts, (out, every, val, mom, srcv) = refs[:-5], refs[-5:]
     lay_out(parts, every)
-    put_points((before, mine, after), pts)
     planes = every.shape[0]
     cells = PLANE // groups
     me, group = meta[0], meta[1]
@@ -233,11 +253,12 @@
         return c
 
     lax.fori_loop(0, planes, put_plane, 0)
+    low_half = in_low_half()
 
     def put_near(j, slot):
         srcv[j] = val[slot]
 
-    def put_far(j, first, second, live, low_half):
+    def put_far(j, first, second, live):
         srcv[j] = jnp.where(low_half, mom[first], mom[second] * live.astype(jnp.float32))
 
     def put_none(j):
@@ -248,26 +269,19 @@
     out[0] = jnp.broadcast_to(marks[...], (ROWS, LANES))
     for t in range(cells):
         cell = target_cell(group, t, groups)
-        n_blocks = list_sources(
-            me, cell, counts, near, far, planes, table, pts, src, put_near, put_far, put_none, unroll
-        )
-        put_targets(pts, cell, tgt)
-
-        def step(k, acc):
-            for u in range(unroll):
-                slot = k * unroll + u
-                acc = acc + lax.rsqrt(square(tgt, src, slot, slice(None))) * srcv[slot]
-            return acc
-
-        acc = lax.fori_loop(0, (n_blocks + unroll - 1) // unroll, step, jnp.zeros((LANES, LANES), jnp.float32))
+        n_blocks = list_blocks(me, cell, counts, near, far, planes, put_near, put_far, put_none, 2)
+
+        def step(i, acc):
+            parts = [lax.rsqrt(squares[t, 2 * i + u]) * srcv[2 * i + u] for u in range(2)]
+            return acc + (parts[0] + parts[1])
+
+        acc = lax.fori_loop(0, (n_blocks + 1) // 2, step, jnp.zeros((LANES, LANES), jnp.float32))
         row = dot_nt(jnp.ones((ROWS, LANES), jnp.float32), acc)[0:1, :]
         out[0, t : t + 1, :] = row
-        there = PLANE + cell
-        scaled = pts[there, 4:5, :] * (pts[there, 3:4, :] + row)
+        point = own[cell]
+        scaled = point[4:5] * (point[3:4] + row)
         v = cell_fields(mine, cell, groups, kinds) * scaled
-        w = weights(
-            cst, pts[there, 0:1, :], pts[there, 1:2, :], pts[there, 2:3, :], (0.0, 0.0, z_low), (1.0, 1.0, cell_side)
-        )
+        w = weights(cst, point[0:1], point[1:2], point[2:3], (0.0, 0.0, z_low), (1.0, 1.0, cell_side))
         total = total + dot_split(v, twice(w))
     for k in range(groups):
         out[1 + lax.bitwise_xor(group, k), :kinds, :] = total[k * kinds : (k + 1) * kinds, :]
@@ -292,13 +306,11 @@
 
 
 def orbital_kernel(
-    batch, unit, steps, meta, counts, near, far, levels, screening, cst, table, before, mine, after, *refs
+    planes, batch, unit, steps, meta, counts, near, far, levels, screening, cst,
+    points_before, own, points_after, before, mine, after, squares, *refs,
 ):
-    parts, refs = refs[:-14], refs[-14:]
-    out, rate, slot_of, every, pts, val, mom, tgt, src, srcv, dist, inv, acc, total = refs
+    parts, (out, rate, slot_of, every, val, mom, srcv, dist, inv, acc) = refs[:-10], refs[-10:]
     lay_out(parts, every)
-    put_points((before, mine, after), pts)
-    planes = every.shape[0]
     groups, cells, kinds, _ = out.shape
     orbs = groups * kinds
     me, group = meta[0], meta[1]
@@ -324,7 +336,6 @@
 
     n_levels, lane_slot = lax.fori_loop(0, orbs, rank, (jnp.int32(0), jnp.zeros((1, LANES), jnp.int32)))
     n_batches = (n_levels + batch - 1) // batch
-
     first_half = lax.broadcasted_iota(jnp.int32, (1, 2 * orbs), 1) < orbs
 
     def flip(v):
@@ -333,21 +344,22 @@
         return square.T[:, : 2 * orbs].astype(jnp.bfloat16)
 
     for k in range(3):
+        points, message = (points_before, own, points_after)[k], (before, mine, after)[k]
         there = lax.bitwise_xor(me, jnp.clip(me - 1 + k, 0, planes - 1))
-        message = (before, mine, after)[k]
 
         def prepare(c, carry):
             at = k * PLANE + c
-            scaled = pts[at, 4:5, :] * (pts[at, 3:4, :] + every[there, pl.ds(c, 1), :])
-            v = cell_fields(message, c, groups, kinds) * scaled
+            point = points[c]
+            potential = point[3:4] + every[there, pl.ds(c, 1), :]
+            v = cell_fields(message, c, groups, kinds) * (point[4:5] * potential)
             val[at] = flip(v)
             vh, vl = split(v)
             z_low = (me - 1 + k).astype(jnp.float32) * cell_side
             low = (*cell_low(c), z_low)
-            wh, wl = split(weights(cst, pts[at, 0:1, :], pts[at, 1:2, :], pts[at, 2:3, :], low, (cell_side,) * 3))
+            wh, wl = split(weights(cst, point[0:1], point[1:2], point[2:3], low, (cell_side,) * 3))
             all_of = dot_bf16(jnp.concatenate([wh, wl], axis=0), jnp.concatenate([vh, vh, vl, vl], axis=0))
             m = all_of[:HALF] + all_of[HALF:]
-            m = m[:, : 2 * orbs] + pltpu.roll(all_of[:HALF], 4 * orbs - 2 * orbs, 1)[:, : 2 * orbs]
+            m = m[:, : 2 * orbs] + pltpu.roll(all_of[:HALF], 2 * orbs, 1)[:, : 2 * orbs]
             high = m.astype(jnp.bfloat16).astype(jnp.float32)
             mom[at] = jnp.where(first_half, high, m - high).astype(jnp.bfloat16)
             return carry
@@ -369,7 +381,7 @@
     def put_near(j, slot):
         srcv[j] = val[slot]
 
-    def put_far(j, first, second, live, low_half):
+    def put_far(j, first, second, live):
         srcv[j, :HALF, :] = mom[first]
         srcv[j, HALF:, :] = jnp.where(live, mom[second], jnp.zeros_like(mom[second]))
 
@@ -387,46 +399,43 @@
 
     def per_cell(t, carry):
         cell = target_cell(group, t, groups)
-        n_blocks = list_sources(me, cell, counts, near, far, planes, table, pts, src, put_near, put_far, put_none, unit)
-        n_loops = (n_blocks + unit - 1) // unit
-        put_targets(pts, cell, tgt)
-
-        def measure(c, x):
-            sq = square(tgt, src, c, slice(None))
-            i = lax.rsqrt(sq)
-            inv[c] = i
-            dist[c] = sq * i
+        n_blocks = list_blocks(me, cell, counts, near, far, planes, put_near, put_far, put_none, unit)
+        n_units = (n_blocks + unit - 1) // unit
+
+        def measure(i, x):
+            for u in range(unit):
+                sq = squares[t, unit * i + u]
+                r = lax.rsqrt(sq)
+                inv[unit * i + u] = r
+                dist[unit * i + u] = sq * r
             return x
 
-        lax.fori_loop(0, unit * n_loops, measure, 0)
-        total[...] = jnp.zeros(total.shape, jnp.float32)
-
-        def clear(b, x):
+        lax.fori_loop(0, n_units, measure, 0)
+
+        def clear_acc(b, x):
             acc[b] = jnp.zeros(acc.shape[1:], jnp.float32)
             return x
 
-        lax.fori_loop(0, n_batches, clear, 0)
+        lax.fori_loop(0, n_batches, clear_acc, 0)
 
         def step(i, at):
             b, u = at
             for _ in range(steps):
                 acc[b] = acc[b] + products(b, unit * u)
-                wrap = u + 1 == n_loops
+                wrap = u + 1 == n_units
                 b, u = jnp.where(wrap, b + 1, b), jnp.where(wrap, 0, u + 1)
             return b, u
 
-        lax.fori_loop(0, (n_batches * n_loops + steps - 1) // steps, step, (jnp.int32(0), jnp.int32(0)))
-
-        def choose(b, x):
-            add = total[...]
+        lax.fori_loop(0, (n_batches * n_units + steps - 1) // steps, step, (jnp.int32(0), jnp.int32(0)))
+
+        def choose(b, add):
             for q in range(batch):
                 mine = lane_slot[:, : 2 * orbs] == b * batch + q
                 add = add + jnp.where(mine, acc[b, q * LANES : (q + 1) * LANES, :], 0.0)
-            total[...] = add
-            return x
-
-        lax.fori_loop(0, n_batches, choose, 0)
-        flipped = jnp.concatenate([total[...], jnp.zeros((LANES, LANES - 2 * orbs), jnp.float32)], axis=1).T
+            return add
+
+        total = lax.fori_loop(0, n_batches, choose, jnp.zeros((LANES, 2 * orbs), jnp.float32))
+        flipped = jnp.concatenate([total, jnp.zeros((LANES, LANES - 2 * orbs), jnp.float32)], axis=1).T
         rows = (flipped[:orbs] + flipped[orbs : 2 * orbs]) * green_scale
         for k in range(groups):
             out[k, t] = rows[k * kinds : (k + 1) * kinds]
@@ -452,14 +461,14 @@
     return pl.BlockSpec(memory_space=pltpu.VMEM)
 
 
-def call(kernel, name, out_shape, smems, args, scratch=()):
+def call(kernel, name, out_shape, smems, args, scratch=(), mib=8):
     return pl.pallas_call(
         kernel,
         out_shape=out_shape,
         in_specs=[smem()] * smems + [vmem()] * (len(args) - smems),
         out_specs=jax.tree.map(lambda _: vmem(), out_shape),
         scratch_shapes=scratch,
-        compiler_params=pltpu.CompilerParams(vmem_limit_bytes=52 * 1024 * 1024),
+        compiler_params=pltpu.CompilerParams(vmem_limit_bytes=mib * 1024 * 1024),
         name=name,
     )(*args)
 
@@ -483,8 +492,6 @@
     ends = planes - 1
     up = [(i, i + 1) for i in range(ends)]
     down = [(i + 1, i) for i in range(ends)]
-    message = jnp.concatenate([f.reshape(kinds * cells, LANES) for f in fields] + [own.reshape(cells * ROWS, LANES)], axis=0)
-    windows = (lax.ppermute(message, "space", up), message, lax.ppermute(message, "space", down))
     cst = jnp.asarray(basis_rows())
     base_table = proxy_table(planes, window)
     shift = np.zeros(base_table.shape, np.float32)
@@ -493,26 +500,41 @@
     counts = jnp.stack(
         [jnp.sum((near_cells >= 0).astype(jnp.int32), 1), jnp.sum((far_cells >= 0).astype(jnp.int32), 1)], axis=1
     )
+    points_before, points_after = lax.ppermute(own, "space", up), lax.ppermute(own, "space", down)
+
     charges = call(
         charge_kernel, "charge", jax.ShapeDtypeStruct((2 * cells + ROWS, LANES), f32), 1, (meta, cst, own, *fields)
     )
-    charges = gather_parts(charges, "space", False)
-
-    unroll = 2
-    blocks = near_cells.shape[1] + (far_cells.shape[1] + planes + 1) // 2 + 8
+    charges, (points_before, points_after) = gather_parts(charges, "space", False, (points_before, points_after))
+
+    batch, unit, steps = 4, 4, 9
+    most = near_cells.shape[1]
+    blocks = most + (window - most + planes + 1) // 2 + 2 * unit
+    squares = call(
+        functools.partial(pairs_kernel, groups, planes, unit),
+        "pairs",
+        jax.ShapeDtypeStruct((share, blocks, LANES, LANES), f32),
+        4,
+        (meta, counts, near_cells, far_cells, table, points_before, own, points_after),
+        [
+            pltpu.VMEM((window, ROWS, LANES), f32),
+            pltpu.VMEM((3, LANES, LANES), f32),
+            pltpu.VMEM((blocks, ROWS, LANES), f32),
+        ],
+    )
+    mine = jnp.concatenate([f.reshape(kinds * cells, LANES) for f in fields], axis=0)
+    mine, squares = lax.optimization_barrier((mine, squares))
+    before, after = lax.ppermute(mine, "space", up), lax.ppermute(mine, "space", down)
     shares = call(
-        functools.partial(hartree_kernel, unroll, groups, kinds),
+        functools.partial(hartree_kernel, groups, kinds),
         "hartree",
         jax.ShapeDtypeStruct((1 + groups, ROWS, LANES), f32),
         4,
-        (meta, counts, near_cells, far_cells, cst, table, marks, *windows, *charges),
+        (meta, counts, near_cells, far_cells, cst, marks, own, mine, squares, *charges),
         [
             pltpu.VMEM((planes, 2 * cells + ROWS, LANES), f32),
-            pltpu.VMEM((window, ROWS, LANES), f32),
             pltpu.VMEM((window, 1, LANES), f32),
             pltpu.VMEM((window + planes, 1, LANES), f32),
-            pltpu.VMEM((3, LANES, LANES), f32),
-            pltpu.VMEM((blocks, ROWS, LANES), f32),
             pltpu.VMEM((blocks, 1, LANES), f32),
         ],
     )
@@ -526,31 +548,28 @@
         (meta, *shares),
         [pltpu.VMEM((orbs, LANES), f32)],
     )
-    gathered = gather_parts(combined, "space", False)
-
-    batch, unit, steps = 4, 4, 9
+    gathered, _ = gather_parts(combined, "space", False)
+
     levels_at_most = -(-screening.shape[0] // batch) + 1
     sent = call(
-        functools.partial(orbital_kernel, batch, unit, steps),
+        functools.partial(orbital_kernel, planes, batch, unit, steps),
         "orbitals",
         jax.ShapeDtypeStruct((groups, share, kinds, LANES), f32),
         6,
-        (meta, counts, near_cells, far_cells, levels, screening, cst, table, *windows, *gathered),
+        (meta, counts, near_cells, far_cells, levels, screening, cst)
+        + (points_before, own, points_after, before, mine, after, squares, *gathered),
         [
             pltpu.SMEM((screening.shape[0] + 2 * batch,), f32),
             pltpu.SMEM((screening.shape[0],), jnp.int32),
             pltpu.VMEM((planes, cells + orbs // 2, LANES), f32),
-            pltpu.VMEM((window, ROWS, LANES), f32),
             pltpu.VMEM((window, LANES, 2 * orbs), bf16),
             pltpu.VMEM((window + planes, HALF, 2 * orbs), bf16),
-            pltpu.VMEM((3, LANES, LANES), f32),
-            pltpu.VMEM((blocks, ROWS, LANES), f32),
             pltpu.VMEM((blocks, LANES, 2 * orbs), bf16),
             pltpu.VMEM((blocks, LANES, LANES), f32),
             pltpu.VMEM((blocks, LANES, LANES), f32),
             pltpu.VMEM((levels_at_most, batch * LANES, 2 * orbs), f32),
-            pltpu.VMEM((LANES, 2 * orbs), f32),
         ],
+        24,
     )
     parts = [sent[0]]
     for k in range(1, groups):

time: 113 us -> 121 us (1.071)
  the two profiles are of different devices: /device:TPU:4 before, /device:TPU:14 now
where the time goes in v2:
time: 121 us; the launch traced here: 120 us
  Pallas kernels  65.1 us (54%)
  starting transfers between devices  30.5 us (25%)
  waiting for transfers between devices  13.8 us (11%)
  other arithmetic  5.87 us (5%)
  local copies, waits for them, and re-layouts  3.98 us (3%)
    pallas_call x6, Pallas kernels, call(): pl.pallas_call(kernel, out_shape=out_shape, in_specs=[smem()] * smems + [...  65.1 us
    ppermute x14, starting transfers between devices, gather_parts(): lax.ppermute(held, axis, [(i, i ^ have * j) for i in range(count)])  14.9 us
    ppermute x14, waiting for transfers between devices, gather_parts(): lax.ppermute(held, axis, [(i, i ^ have * j) for i in range(count)])  10.1 us
    ppermute x3, starting transfers between devices, body(): lax.ppermute(sent[k], 'orb', [(i, i ^ k) for i in range(groups)])  6.58 us
    unnamed x17, local copies, waits for them, and re-layouts  3.79 us
    ppermute x3, waiting for transfers between devices, body(): lax.ppermute(sent[k], 'orb', [(i, i ^ k) for i in range(groups)])  3.73 us
    ppermute x1, starting transfers between devices, body(): lax.ppermute(mine, 'space', down)  2.79 us
  transfers between devices with their start and end apart: 21, of which 11 were waited for; matrix products, arithmetic and copies ran while one was open for 4% of the time, Pallas kernels for 14%

profile of v2, /device:TPU:14, one launch (start us, length us, event | category | flops | bytes accessed | tf_op | source)
XLA Modules:
  0.0 120.1 jit_solution(14774693121616401090)
XLA Ops:
  0.6 0.0 copy-start.1
  0.6 0.7 broadcast_multiply_fusion
  1.4 0.8 copy.21
  2.1 0.1 pad.20.clone
  2.2 0.8 maximum_maximum_fusion.own.mine
  3.0 1.9 %collective-permute-start.5 = (f32[16,8,128]{2,1,0:T(8,128)S(1)}, f32[16,8,128]{2,1,0:T(8,128)S(1)}, u32[]{:S(2)}, u32[]{:S(2)}) collective-permute-start(f32[16,8,128]{2,1,0:T(8,128)S(1)} %maximum_maximum_fusion.own.mine), channel_id=1, source_target_pairs={{1,0},{2,1},{3,2},{4,3},{5,4},{6,5},{7,6},{9,8},{10,9},{11,10},{12... | collective-permute-start | bytes 196616 | tf_op jit(solution)/shard_map/ppermute | solution.py:503
  4.9 2.4 %collective-permute-start.4 = (f32[16,8,128]{2,1,0:T(8,128)S(1)}, f32[16,8,128]{2,1,0:T(8,128)S(1)}, u32[]{:S(2)}, u32[]{:S(2)}) collective-permute-start(f32[16,8,128]{2,1,0:T(8,128)S(1)} %maximum_maximum_fusion.own.mine), channel_id=1, source_target_pairs={{0,1},{1,2},{2,3},{3,4},{4,5},{5,6},{6,7},{8,9},{9,10},{10,11},{11... | collective-permute-start | bytes 196616 | tf_op jit(solution)/shard_map/ppermute | solution.py:503
  7.3 1.6 %collective-permute-start.2 = (f32[1,8,16,128]{3,2,1,0:T(8,128)}, f32[1,8,16,128]{3,2,1,0:T(8,128)S(1)}, u32[]{:S(2)}, u32[]{:S(2)}) collective-permute-start(f32[1,8,16,128]{3,2,1,0:T(8,128)} %bitcast.41), channel_id=1, source_target_pairs={{0,24},{8,16},{16,8},{24,0},{1,25},{9,17},{17,9},{25,1},{2,26},{10... | collective-permute-start | bytes 196616 | tf_op jit(solution)/shard_map/ppermute | solution.py:90
  8.9 1.2 %collective-permute-start.1 = (f32[1,8,16,128]{3,2,1,0:T(8,128)}, f32[1,8,16,128]{3,2,1,0:T(8,128)S(1)}, u32[]{:S(2)}, u32[]{:S(2)}) collective-permute-start(f32[1,8,16,128]{3,2,1,0:T(8,128)} %bitcast.42), channel_id=1, source_target_pairs={{0,16},{8,24},{16,0},{24,8},{1,17},{9,25},{17,1},{25,9},{2,18},{10... | collective-permute-start | bytes 196616 | tf_op jit(solution)/shard_map/ppermute | solution.py:90
  10.2 1.2 %collective-permute-start = (f32[1,8,16,128]{3,2,1,0:T(8,128)}, f32[1,8,16,128]{3,2,1,0:T(8,128)S(1)}, u32[]{:S(2)}, u32[]{:S(2)}) collective-permute-start(f32[1,8,16,128]{3,2,1,0:T(8,128)} %bitcast.43), channel_id=1, source_target_pairs={{0,8},{8,0},{16,24},{24,16},{1,9},{9,1},{17,25},{25,17},{2,10},{10... | collective-permute-start | bytes 196616 | tf_op jit(solution)/shard_map/ppermute | solution.py:90
  11.4 0.7 convert_element_type.19
  12.1 0.8 convert_reduce_fusion.1
  12.9 0.8 convert_reduce_fusion
  13.7 1.1 multiply_add_fusion.table
  14.8 0.1 pad_add_fusion.1.meta
  14.9 0.0 collective-permute-done.2
  14.9 0.0 collective-permute-done.1
  14.9 1.0 collective-permute-done
  15.8 0.8 copy-done
  16.6 0.8 copy-done.2
  17.5 2.4 %charge.1 = f32[40,128]{1,0:T(8,128)S(1)} custom-call(s32[2]{0:T(128)S(1)} %pad_add_fusion.1.meta, f32[12,8,128]{2,1,0:T(8,128)S(1)} %copy-done, f32[16,8,128]{2,1,0:T(8,128)S(1)} %maximum_maximum_fusion.own.mine, f32[8,16,128]{2,1,0:T(8,128)S(1)} %copy-done.2, f32[8,16,128]{2,1,0:T(8,128)S(1)} %bitcast.49, f32[8,16,128]{2,1,0:T(8,128)S(1)} %bitcast.47, ...), custom_call_target="tpu_custom_call" | custom-call | tf_op jit(solution)/shard_map/charge/pallas_call | solution.py:465
  19.9 0.0 collective-permute-start.3
  19.9 0.1 copy.19.counts
  20.0 0.0 collective-permute-done.5.after.points_after
  20.0 0.0 collective-permute-done.4.before.points_before
  20.0 1.1 collective-permute-done.3
  21.1 1.9 %collective-permute-start.8 = (f32[2,40,128]{2,1,0:T(8,128)S(1)}, f32[2,40,128]{2,1,0:T(8,128)S(1)}, u32[]{:S(2)}, u32[]{:S(2)}) collective-permute-start(f32[2,40,128]{2,1,0:T(8,128)S(1)} %pad_maximum_fusion.1.refs_0_), channel_id=1, source_target_pairs={{0,6},{1,7},{2,4},{3,5},{4,2},{5,3},{6,0},{7,1},{8,14},{9,15},{10,... | collective-permute-start | bytes 122888 | tf_op jit(solution)/shard_map/ppermute | solution.py:90
  23.0 1.8 %collective-permute-start.7 = (f32[2,40,128]{2,1,0:T(8,128)S(1)}, f32[2,40,128]{2,1,0:T(8,128)S(1)}, u32[]{:S(2)}, u32[]{:S(2)}) collective-permute-start(f32[2,40,128]{2,1,0:T(8,128)S(1)} %pad_maximum_fusion.1.refs_0_), channel_id=1, source_target_pairs={{0,4},{1,5},{2,6},{3,7},{4,0},{5,1},{6,2},{7,3},{8,12},{9,13},{10,... | collective-permute-start | bytes 122888 | tf_op jit(solution)/shard_map/ppermute | solution.py:90
  24.8 0.0 collective-permute-start.6
  24.8 0.9 pad_maximum_fusion.mine
  25.7 0.0 copy-start.3
  25.7 0.7 copy-done.3
  26.4 0.7 copy-done.5
  27.1 6.3 %pairs.1.squares = f32[4,50,128,128]{3,2,1,0:T(8,128)S(1)} custom-call(s32[2]{0:T(128)S(1)} %pad_add_fusion.1.meta, s32[16,2]{1,0:T(8,128)S(1)} %copy.19.counts, s32[16,27]{1,0:T(8,128)S(1)} %copy-done.5, s32[16,42]{1,0:T(8,128)S(1)} %copy-done.3, f32[56,8,128]{2,1,0:T(8,128)S(1)} %multiply_add_fusion.table, ...), custom_call_target="tpu_custom_call" | custom-call | tf_op jit(solution)/shard_map/pairs/pallas_call | solution.py:465
  33.4 2.8 %collective-permute-start.13 = (f32[512,128]{1,0:T(8,128)S(1)}, f32[512,128]{1,0:T(8,128)S(1)}, u32[]{:S(2)}, u32[]{:S(2)}) collective-permute-start(f32[512,128]{1,0:T(8,128)S(1)} %pad_maximum_fusion.mine), channel_id=1, source_target_pairs={{1,0},{2,1},{3,2},{4,3},{5,4},{6,5},{7,6},{9,8},{10,9},{11,10},{12... | collective-permute-start | bytes 786440 | tf_op jit(solution)/shard_map/ppermute | solution.py:527
  36.2 1.9 %collective-permute-start.12 = (f32[512,128]{1,0:T(8,128)S(1)}, f32[512,128]{1,0:T(8,128)S(1)}, u32[]{:S(2)}, u32[]{:S(2)}) collective-permute-start(f32[512,128]{1,0:T(8,128)S(1)} %pad_maximum_fusion.mine), channel_id=1, source_target_pairs={{0,1},{1,2},{2,3},{3,4},{4,5},{5,6},{6,7},{8,9},{9,10},{10,11},{11... | collective-permute-start | bytes 786440 | tf_op jit(solution)/shard_map/ppermute | solution.py:527
  38.2 0.0 collective-permute-done.8.refs_3_
  38.2 0.0 collective-permute-done.6.refs_1_
  38.2 6.4 %hartree.1.refs_0_ = f32[5,8,128]{2,1,0:T(8,128)S(1)} custom-call(s32[2]{0:T(128)S(1)} %pad_add_fusion.1.meta, s32[16,2]{1,0:T(8,128)S(1)} %copy.19.counts, s32[16,27]{1,0:T(8,128)S(1)} %copy-done.5, s32[16,42]{1,0:T(8,128)S(1)} %copy-done.3, f32[12,8,128]{2,1,0:T(8,128)S(1)} %copy-done.1, f32[1,128]{1,0:T(1,128)S(1)} %pad_bitcast_fusion.marks, ...), custom_call_target="tpu_custom_call" | custom-call | tf_op jit(solution)/shard_map/hartree/pallas_call | solution.py:465
  44.6 1.0 collective-permute-start.11
  45.6 2.4 %collective-permute-start.10 = (f32[1,5,8,128]{3,2,1,0:T(8,128)S(1)}, f32[1,5,8,128]{3,2,1,0:T(8,128)S(1)}, u32[]{:S(2)}, u32[]{:S(2)}) collective-permute-start(f32[1,5,8,128]{3,2,1,0:T(8,128)S(1)} %bitcast.52), channel_id=1, source_target_pairs={{0,16},{8,24},{16,0},{24,8},{1,17},{9,25},{17,1},{25,9},{2,18},{10... | collective-permute-start | bytes 61448 | tf_op jit(solution)/shard_map/ppermute | solution.py:90
  47.9 0.2 collective-permute-start.9
  48.1 0.3 collective-permute-done.11
  48.4 1.8 %collective-permute-done.10 = f32[1,5,8,128]{3,2,1,0:T(8,128)S(1)} collective-permute-done((f32[1,5,8,128]{3,2,1,0:T(8,128)S(1)}, f32[1,5,8,128]{3,2,1,0:T(8,128)S(1)}, u32[]{:S(2)}, u32[]{:S(2)}) %collective-permute-start.10) | collective-permute-done | bytes 20512 | tf_op jit(solution)/shard_map/ppermute | solution.py:90
  50.3 1.5 %collective-permute-done.9 = f32[1,5,8,128]{3,2,1,0:T(8,128)S(1)} collective-permute-done((f32[1,5,8,128]{3,2,1,0:T(8,128)S(1)}, f32[1,5,8,128]{3,2,1,0:T(8,128)S(1)}, u32[]{:S(2)}, u32[]{:S(2)}) %collective-permute-start.9) | collective-permute-done | bytes 20512 | tf_op jit(solution)/shard_map/ppermute | solution.py:90
  51.7 1.2 combine.1
  52.9 0.0 collective-permute-start.14
  52.9 1.2 collective-permute-done.14
  54.1 0.2 collective-permute-start.17
  54.3 2.7 %collective-permute-start.16 = (f32[2,32,128]{2,1,0:T(8,128)S(1)}, f32[2,32,128]{2,1,0:T(8,128)S(1)}, u32[]{:S(2)}, u32[]{:S(2)}) collective-permute-start(f32[2,32,128]{2,1,0:T(8,128)S(1)} %pad_maximum_fusion.2.refs_0_), channel_id=1, source_target_pairs={{0,4},{1,5},{2,6},{3,7},{4,0},{5,1},{6,2},{7,3},{8,12},{9,13},{10,... | collective-permute-start | bytes 98312 | tf_op jit(solution)/shard_map/ppermute | solution.py:90
  57.0 0.6 collective-permute-start.15
  57.6 0.1 maximum_convert_fusion.levels
  57.6 1.3 %collective-permute-done.17.refs_3_ = f32[2,32,128]{2,1,0:T(8,128)S(1)} collective-permute-done((f32[2,32,128]{2,1,0:T(8,128)S(1)}, f32[2,32,128]{2,1,0:T(8,128)S(1)}, u32[]{:S(2)}, u32[]{:S(2)}) %collective-permute-start.17) | collective-permute-done | bytes 32800 | tf_op jit(solution)/shard_map/ppermute | solution.py:90
  58.9 0.3 collective-permute-done.16.refs_2_
  59.2 1.7 %collective-permute-done.15.refs_1_ = f32[2,32,128]{2,1,0:T(8,128)S(1)} collective-permute-done((f32[2,32,128]{2,1,0:T(8,128)S(1)}, f32[2,32,128]{2,1,0:T(8,128)S(1)}, u32[]{:S(2)}, u32[]{:S(2)}) %collective-permute-start.15) | collective-permute-done | bytes 32800 | tf_op jit(solution)/shard_map/ppermute | solution.py:90
  60.9 0.0 collective-permute-done.13.after
  60.9 0.0 collective-permute-done.12.before
  60.9 47.6 %orbitals.1 = f32[4,4,8,128]{3,2,1,0:T(8,128)S(1)} custom-call(s32[2]{0:T(128)S(1)} %pad_add_fusion.1.meta, s32[16,2]{1,0:T(8,128)S(1)} %copy.19.counts, s32[16,27]{1,0:T(8,128)S(1)} %copy-done.6, s32[16,42]{1,0:T(8,128)S(1)} %copy-done.4, s32[32]{0:T(128)S(1)} %maximum_convert_fusion.levels, f32[32]{0:T(128)S(1)} %copy-done.7, f32[12,8,128]{2,1,0:T(8,128)S(1)} %copy-done.1, ...), custom_call_target="tpu_custom_call" | custom-call | tf_op jit(solution)/shard_map/orbitals/pallas_call | solution.py:465
  108.5 1.7 %collective-permute-start.20 = (f32[4,8,128]{2,1,0:T(8,128)S(1)}, f32[4,8,128]{2,1,0:T(8,128)S(1)}, u32[]{:S(2)}, u32[]{:S(2)}) collective-permute-start(f32[4,8,128]{2,1,0:T(8,128)S(1)} %get-tuple-element.16), channel_id=1, source_target_pairs={{0,24},{8,16},{16,8},{24,0},{1,25},{9,17},{17,9},{25,1},{2,26},{10... | collective-permute-start | bytes 49160 | tf_op jit(solution)/shard_map/ppermute | solution.py:576
  110.2 4.9 %collective-permute-start.19 = (f32[4,8,128]{2,1,0:T(8,128)S(1)}, f32[4,8,128]{2,1,0:T(8,128)S(1)}, u32[]{:S(2)}, u32[]{:S(2)}) collective-permute-start(f32[4,8,128]{2,1,0:T(8,128)S(1)} %get-tuple-element.17), channel_id=1, source_target_pairs={{0,16},{8,24},{16,0},{24,8},{1,17},{9,25},{17,1},{25,9},{2,18},{10... | collective-permute-start | bytes 49160 | tf_op jit(solution)/shard_map/ppermute | solution.py:576
  115.1 0.0 collective-permute-start.18
  115.1 1.9 %collective-permute-done.19.refs_2_ = f32[4,8,128]{2,1,0:T(8,128)S(1)} collective-permute-done((f32[4,8,128]{2,1,0:T(8,128)S(1)}, f32[4,8,128]{2,1,0:T(8,128)S(1)}, u32[]{:S(2)}, u32[]{:S(2)}) %collective-permute-start.19) | collective-permute-done | bytes 16416 | tf_op jit(solution)/shard_map/ppermute | solution.py:576
  117.0 1.9 %collective-permute-done.18.refs_1_ = f32[4,8,128]{2,1,0:T(8,128)S(1)} collective-permute-done((f32[4,8,128]{2,1,0:T(8,128)S(1)}, f32[4,8,128]{2,1,0:T(8,128)S(1)}, u32[]{:S(2)}, u32[]{:S(2)}) %collective-permute-start.18) | collective-permute-done | bytes 16416 | tf_op jit(solution)/shard_map/ppermute | solution.py:576
  118.8 1.2 %place.1 = f32[8,16,128]{2,1,0:T(8,128)} custom-call(s32[2]{0:T(128)S(1)} %pad_add_fusion.1.meta, f32[4,8,128]{2,1,0:T(8,128)S(1)} %get-tuple-element.19.refs_0_, f32[4,8,128]{2,1,0:T(8,128)S(1)} %collective-permute-done.18.refs_1_, f32[4,8,128]{2,1,0:T(8,128)S(1)} %collective-permute-done.19.refs_2_, f32[4,8,128]{2,1,0:T(8,128)S(1)} %collective-permute-done.20.refs_3_), custom_call_target="tpu_custom_call" | custom-call | tf_op jit(solution)/shard_map/place/pallas_call | solution.py:465
  (22 shorter events, 0.1 us)
Async XLA Ops:
  0.6 37.6 %copy-start.1 = (f32[12,8,128]{2,1,0:T(8,128)S(1)}, f32[12,8,128]{2,1,0:T(8,128)}, u32[]{:S(2)}) copy-start(f32[12,8,128]{2,1,0:T(8,128)} %constant.26.clone.cst) | copy-start | bytes 147460
  3.0 17.0 %collective-permute-start.5 = (f32[16,8,128]{2,1,0:T(8,128)S(1)}, f32[16,8,128]{2,1,0:T(8,128)S(1)}, u32[]{:S(2)}, u32[]{:S(2)}) collective-permute-start(f32[16,8,128]{2,1,0:T(8,128)S(1)} %maximum_maximum_fusion.own.mine), channel_id=1, source_target_pairs={{1,0},{2,1},{3,2},{4,3},{5,4},{6,5},{7,6},{9,8},{10,9},{11,10},{12... | collective-permute-start | bytes 196616 | tf_op jit(solution)/shard_map/ppermute | solution.py:503
  4.9 15.1 %collective-permute-start.4 = (f32[16,8,128]{2,1,0:T(8,128)S(1)}, f32[16,8,128]{2,1,0:T(8,128)S(1)}, u32[]{:S(2)}, u32[]{:S(2)}) collective-permute-start(f32[16,8,128]{2,1,0:T(8,128)S(1)} %maximum_maximum_fusion.own.mine), channel_id=1, source_target_pairs={{0,1},{1,2},{2,3},{3,4},{4,5},{5,6},{6,7},{8,9},{9,10},{10,11},{11... | collective-permute-start | bytes 196616 | tf_op jit(solution)/shard_map/ppermute | solution.py:503
  7.3 7.6 %collective-permute-start.2 = (f32[1,8,16,128]{3,2,1,0:T(8,128)}, f32[1,8,16,128]{3,2,1,0:T(8,128)S(1)}, u32[]{:S(2)}, u32[]{:S(2)}) collective-permute-start(f32[1,8,16,128]{3,2,1,0:T(8,128)} %bitcast.41), channel_id=1, source_target_pairs={{0,24},{8,16},{16,8},{24,0},{1,25},{9,17},{17,9},{25,1},{2,26},{10... | collective-permute-start | bytes 196616 | tf_op jit(solution)/shard_map/ppermute | solution.py:90
  8.9 5.9 %collective-permute-start.1 = (f32[1,8,16,128]{3,2,1,0:T(8,128)}, f32[1,8,16,128]{3,2,1,0:T(8,128)S(1)}, u32[]{:S(2)}, u32[]{:S(2)}) collective-permute-start(f32[1,8,16,128]{3,2,1,0:T(8,128)} %bitcast.42), channel_id=1, source_target_pairs={{0,16},{8,24},{16,0},{24,8},{1,17},{9,25},{17,1},{25,9},{2,18},{10... | collective-permute-start | bytes 196616 | tf_op jit(solution)/shard_map/ppermute | solution.py:90
  10.2 5.7 %collective-permute-start = (f32[1,8,16,128]{3,2,1,0:T(8,128)}, f32[1,8,16,128]{3,2,1,0:T(8,128)S(1)}, u32[]{:S(2)}, u32[]{:S(2)}) collective-permute-start(f32[1,8,16,128]{3,2,1,0:T(8,128)} %bitcast.43), channel_id=1, source_target_pairs={{0,8},{8,0},{16,24},{24,16},{1,9},{9,1},{17,25},{25,17},{2,10},{10... | collective-permute-start | bytes 196616 | tf_op jit(solution)/shard_map/ppermute | solution.py:90
  15.8 0.8 copy-start
  16.6 0.8 copy-start.2
  19.9 1.2 %collective-permute-start.3 = (f32[1,40,128]{2,1,0:T(8,128)S(1)}, f32[1,40,128]{2,1,0:T(8,128)S(1)}, u32[]{:S(2)}, u32[]{:S(2)}) collective-permute-start(f32[1,40,128]{2,1,0:T(8,128)S(1)} %bitcast.54), channel_id=1, source_target_pairs={{0,1},{1,0},{2,3},{3,2},{4,5},{5,4},{6,7},{7,6},{8,9},{9,8},{10,11... | collective-permute-start | bytes 61448 | tf_op jit(solution)/shard_map/ppermute | solution.py:90
  21.1 17.1 %collective-permute-start.8 = (f32[2,40,128]{2,1,0:T(8,128)S(1)}, f32[2,40,128]{2,1,0:T(8,128)S(1)}, u32[]{:S(2)}, u32[]{:S(2)}) collective-permute-start(f32[2,40,128]{2,1,0:T(8,128)S(1)} %pad_maximum_fusion.1.refs_0_), channel_id=1, source_target_pairs={{0,6},{1,7},{2,4},{3,5},{4,2},{5,3},{6,0},{7,1},{8,14},{9,15},{10,... | collective-permute-start | bytes 122888 | tf_op jit(solution)/shard_map/ppermute | solution.py:90
  23.0 15.2 %collective-permute-start.7 = (f32[2,40,128]{2,1,0:T(8,128)S(1)}, f32[2,40,128]{2,1,0:T(8,128)S(1)}, u32[]{:S(2)}, u32[]{:S(2)}) collective-permute-start(f32[2,40,128]{2,1,0:T(8,128)S(1)} %pad_maximum_fusion.1.refs_0_), channel_id=1, source_target_pairs={{0,4},{1,5},{2,6},{3,7},{4,0},{5,1},{6,2},{7,3},{8,12},{9,13},{10,... | collective-permute-start | bytes 122888 | tf_op jit(solution)/shard_map/ppermute | solution.py:90
  24.8 13.4 %collective-permute-start.6 = (f32[2,40,128]{2,1,0:T(8,128)S(1)}, f32[2,40,128]{2,1,0:T(8,128)S(1)}, u32[]{:S(2)}, u32[]{:S(2)}) collective-permute-start(f32[2,40,128]{2,1,0:T(8,128)S(1)} %pad_maximum_fusion.1.refs_0_), channel_id=1, source_target_pairs={{0,2},{1,3},{2,0},{3,1},{4,6},{5,7},{6,4},{7,5},{8,10},{9,11},{10,... | collective-permute-start | bytes 122888 | tf_op jit(solution)/shard_map/ppermute | solution.py:90
  25.7 0.7 copy-start.3
  26.4 0.7 copy-start.5
  27.1 33.8 %copy-start.4 = (s32[16,42]{1,0:T(8,128)S(1)}, s32[16,42]{1,0:T(8,128)}, u32[]{:S(2)}) copy-start(s32[16,42]{1,0:T(8,128)} %far.5) | copy-start | bytes 8068
  27.1 33.8 %copy-start.6 = (s32[16,27]{1,0:T(8,128)S(1)}, s32[16,27]{1,0:T(8,128)}, u32[]{:S(2)}) copy-start(s32[16,27]{1,0:T(8,128)} %near.5) | copy-start | bytes 5188
  27.1 33.8 %copy-start.7 = (f32[32]{0:T(128)S(1)}, f32[32]{0:T(128)}, u32[]{:S(2)}) copy-start(f32[32]{0:T(128)} %screening.1) | copy-start | bytes 388
  33.4 27.4 %collective-permute-start.13 = (f32[512,128]{1,0:T(8,128)S(1)}, f32[512,128]{1,0:T(8,128)S(1)}, u32[]{:S(2)}, u32[]{:S(2)}) collective-permute-start(f32[512,128]{1,0:T(8,128)S(1)} %pad_maximum_fusion.mine), channel_id=1, source_target_pairs={{1,0},{2,1},{3,2},{4,3},{5,4},{6,5},{7,6},{9,8},{10,9},{11,10},{12... | collective-permute-start | bytes 786440 | tf_op jit(solution)/shard_map/ppermute | solution.py:527
  36.2 24.7 %collective-permute-start.12 = (f32[512,128]{1,0:T(8,128)S(1)}, f32[512,128]{1,0:T(8,128)S(1)}, u32[]{:S(2)}, u32[]{:S(2)}) collective-permute-start(f32[512,128]{1,0:T(8,128)S(1)} %pad_maximum_fusion.mine), channel_id=1, source_target_pairs={{0,1},{1,2},{2,3},{3,4},{4,5},{5,6},{6,7},{8,9},{9,10},{10,11},{11... | collective-permute-start | bytes 786440 | tf_op jit(solution)/shard_map/ppermute | solution.py:527
  44.6 3.8 %collective-permute-start.11 = (f32[1,5,8,128]{3,2,1,0:T(8,128)S(1)}, f32[1,5,8,128]{3,2,1,0:T(8,128)S(1)}, u32[]{:S(2)}, u32[]{:S(2)}) collective-permute-start(f32[1,5,8,128]{3,2,1,0:T(8,128)S(1)} %bitcast.51), channel_id=1, source_target_pairs={{0,24},{8,16},{16,8},{24,0},{1,25},{9,17},{17,9},{25,1},{2,26},{10... | collective-permute-start | bytes 61448 | tf_op jit(solution)/shard_map/ppermute | solution.py:90
  45.6 4.7 %collective-permute-start.10 = (f32[1,5,8,128]{3,2,1,0:T(8,128)S(1)}, f32[1,5,8,128]{3,2,1,0:T(8,128)S(1)}, u32[]{:S(2)}, u32[]{:S(2)}) collective-permute-start(f32[1,5,8,128]{3,2,1,0:T(8,128)S(1)} %bitcast.52), channel_id=1, source_target_pairs={{0,16},{8,24},{16,0},{24,8},{1,17},{9,25},{17,1},{25,9},{2,18},{10... | collective-permute-start | bytes 61448 | tf_op jit(solution)/shard_map/ppermute | solution.py:90
  47.9 3.8 %collective-permute-start.9 = (f32[1,5,8,128]{3,2,1,0:T(8,128)S(1)}, f32[1,5,8,128]{3,2,1,0:T(8,128)S(1)}, u32[]{:S(2)}, u32[]{:S(2)}) collective-permute-start(f32[1,5,8,128]{3,2,1,0:T(8,128)S(1)} %bitcast.53), channel_id=1, source_target_pairs={{0,8},{8,0},{16,24},{24,16},{1,9},{9,1},{17,25},{25,17},{2,10},{10... | collective-permute-start | bytes 61448 | tf_op jit(solution)/shard_map/ppermute | solution.py:90
  52.9 1.2 collective-permute-start.14
  54.1 4.9 %collective-permute-start.17 = (f32[2,32,128]{2,1,0:T(8,128)S(1)}, f32[2,32,128]{2,1,0:T(8,128)S(1)}, u32[]{:S(2)}, u32[]{:S(2)}) collective-permute-start(f32[2,32,128]{2,1,0:T(8,128)S(1)} %pad_maximum_fusion.2.refs_0_), channel_id=1, source_target_pairs={{0,6},{1,7},{2,4},{3,5},{4,2},{5,3},{6,0},{7,1},{8,14},{9,15},{10,... | collective-permute-start | bytes 98312 | tf_op jit(solution)/shard_map/ppermute | solution.py:90
  54.3 4.9 %collective-permute-start.16 = (f32[2,32,128]{2,1,0:T(8,128)S(1)}, f32[2,32,128]{2,1,0:T(8,128)S(1)}, u32[]{:S(2)}, u32[]{:S(2)}) collective-permute-start(f32[2,32,128]{2,1,0:T(8,128)S(1)} %pad_maximum_fusion.2.refs_0_), channel_id=1, source_target_pairs={{0,4},{1,5},{2,6},{3,7},{4,0},{5,1},{6,2},{7,3},{8,12},{9,13},{10,... | collective-permute-start | bytes 98312 | tf_op jit(solution)/shard_map/ppermute | solution.py:90
  57.0 3.9 %collective-permute-start.15 = (f32[2,32,128]{2,1,0:T(8,128)S(1)}, f32[2,32,128]{2,1,0:T(8,128)S(1)}, u32[]{:S(2)}, u32[]{:S(2)}) collective-permute-start(f32[2,32,128]{2,1,0:T(8,128)S(1)} %pad_maximum_fusion.2.refs_0_), channel_id=1, source_target_pairs={{0,2},{1,3},{2,0},{3,1},{4,6},{5,7},{6,4},{7,5},{8,10},{9,11},{10,... | collective-permute-start | bytes 98312 | tf_op jit(solution)/shard_map/ppermute | solution.py:90
  108.5 6.6 %collective-permute-start.20 = (f32[4,8,128]{2,1,0:T(8,128)S(1)}, f32[4,8,128]{2,1,0:T(8,128)S(1)}, u32[]{:S(2)}, u32[]{:S(2)}) collective-permute-start(f32[4,8,128]{2,1,0:T(8,128)S(1)} %get-tuple-element.16), channel_id=1, source_target_pairs={{0,24},{8,16},{16,8},{24,0},{1,25},{9,17},{17,9},{25,1},{2,26},{10... | collective-permute-start | bytes 49160 | tf_op jit(solution)/shard_map/ppermute | solution.py:576
  110.2 6.7 %collective-permute-start.19 = (f32[4,8,128]{2,1,0:T(8,128)S(1)}, f32[4,8,128]{2,1,0:T(8,128)S(1)}, u32[]{:S(2)}, u32[]{:S(2)}) collective-permute-start(f32[4,8,128]{2,1,0:T(8,128)S(1)} %get-tuple-element.17), channel_id=1, source_target_pairs={{0,16},{8,24},{16,0},{24,8},{1,17},{9,25},{17,1},{25,9},{2,18},{10... | collective-permute-start | bytes 49160 | tf_op jit(solution)/shard_map/ppermute | solution.py:576
  115.1 3.7 %collective-permute-start.18 = (f32[4,8,128]{2,1,0:T(8,128)S(1)}, f32[4,8,128]{2,1,0:T(8,128)S(1)}, u32[]{:S(2)}, u32[]{:S(2)}) collective-permute-start(f32[4,8,128]{2,1,0:T(8,128)S(1)} %get-tuple-element.18), channel_id=1, source_target_pairs={{0,8},{8,0},{16,24},{24,16},{1,9},{9,1},{17,25},{25,17},{2,10},{10... | collective-permute-start | bytes 49160 | tf_op jit(solution)/shard_map/ppermute | solution.py:576

commit v3 on v2

--- a/solution.py
+++ b/solution.py
@@ -80,7 +80,7 @@
     return lax.dot_general(a, b, (((1,), (1,)), ((), ())), precision=highest, preferred_element_type=jnp.float32)
 
 
-def gather_parts(block, axis, pairs, later=()):
+def gather_parts(block, axis, pairs, later=None):
     count = lax.axis_size(axis)
     parts = [block[None]]
     while sum(p.shape[0] for p in parts) < count:
@@ -88,7 +88,7 @@
         have = held.shape[0]
         steps = range(1, 4 if (have > 1 or pairs) and have * 4 <= count else 2)
         parts = [held] + [lax.ppermute(held, axis, [(i, i ^ (have * j)) for i in range(count)]) for j in steps]
-        if later and have == 1:
+        if later is not None and have == 1:
             parts[1], later = lax.optimization_barrier((parts[1], later))
     return parts, later
 
@@ -194,11 +194,18 @@
         tgt[d] = jnp.broadcast_to(pts[PLANE + cell, d : d + 1, :], (LANES, LANES)).T
 
 
-def square(tgt, src, slot, rows):
-    dx = tgt[0, rows, :] - src[slot, 0:1, :]
-    dy = tgt[1, rows, :] - src[slot, 1:2, :]
-    dz = tgt[2, rows, :] - src[slot, 2:3, :]
-    return (dx * dx + dy * dy) + (dz * dz + soften)
+def each_square(tgt, src, first, count, use):
+    sources = [[src[first + u, d : d + 1, :] for d in range(3)] for u in range(count)]
+    for r in range(LANES // ROWS):
+        at = [tgt[d, r * ROWS : (r + 1) * ROWS, :] for d in range(3)]
+        for u in range(count):
+            dx, dy, dz = (a - b for a, b in zip(at, sources[u]))
+            use(r, u, (dx * dx + dy * dy) + (dz * dz + soften))
+
+
+def lay_points(windows, pts):
+    for k, points in enumerate(windows):
+        pts[k * PLANE : (k + 1) * PLANE] = points[...]
 
 
 def cell_fields(message, c, groups, kinds):
@@ -206,40 +213,12 @@
     return jnp.concatenate([message[pl.ds(g * rows + c, kinds, stride=PLANE), :] for g in range(groups)], axis=0)
 
 
-def pairs_kernel(groups, planes, unit, meta, counts, near, far, table, before, mine, after, out, pts, tgt, src):
-    for k, points in enumerate((before, mine, after)):
-        pts[k * PLANE : (k + 1) * PLANE] = points[...]
-    me, group = meta[0], meta[1]
-    low_half = in_low_half()
-
-    def put_near(j, slot):
-        src[j] = pts[slot]
-
-    def put_far(j, first, second, live):
-        src[j] = jnp.where(low_half, table[first], table[second])
-
-    def put_none(j):
-        src[j] = jnp.zeros(src.shape[1:], jnp.float32)
-
-    def per_cell(t, carry):
-        cell = target_cell(group, t, groups)
-        n_blocks = list_blocks(me, cell, counts, near, far, planes, put_near, put_far, put_none, unit)
-        put_targets(pts, cell, tgt)
-
-        def measure(i, x):
-            for u in range(unit):
-                out[t, unit * i + u] = square(tgt, src, unit * i + u, slice(None))
-            return x
-
-        lax.fori_loop(0, (n_blocks + unit - 1) // unit, measure, 0)
-        return carry
-
-    lax.fori_loop(0, PLANE // groups, per_cell, 0)
-
-
-def hartree_kernel(groups, kinds, meta, counts, near, far, cst, marks, own, mine, squares, *refs):
-    parts, (out, every, val, mom, srcv) = refs[:-5], refs[-5:]
+def hartree_kernel(
+    groups, kinds, unroll, meta, counts, near, far, cst, table, marks, points_before, own, points_after, mine, *refs
+):
+    parts, (out, every, pts, tgt, src, val, mom, srcv) = refs[:-8], refs[-8:]
     lay_out(parts, every)
+    lay_points((points_before, own, points_after), pts)
     planes = every.shape[0]
     cells = PLANE // groups
     me, group = meta[0], meta[1]
@@ -256,12 +235,15 @@
     low_half = in_low_half()
 
     def put_near(j, slot):
+        src[j] = pts[slot]
         srcv[j] = val[slot]
 
     def put_far(j, first, second, live):
+        src[j] = jnp.where(low_half, table[first], table[second])
         srcv[j] = jnp.where(low_half, mom[first], mom[second] * live.astype(jnp.float32))
 
     def put_none(j):
+        src[j] = jnp.zeros(src.shape[1:], jnp.float32)
         srcv[j] = jnp.zeros((1, LANES), jnp.float32)
 
     z_low = me.astype(jnp.float32) * cell_side
@@ -269,13 +251,22 @@
     out[0] = jnp.broadcast_to(marks[...], (ROWS, LANES))
     for t in range(cells):
         cell = target_cell(group, t, groups)
-        n_blocks = list_blocks(me, cell, counts, near, far, planes, put_near, put_far, put_none, 2)
-
-        def step(i, acc):
-            parts = [lax.rsqrt(squares[t, 2 * i + u]) * srcv[2 * i + u] for u in range(2)]
-            return acc + (parts[0] + parts[1])
-
-        acc = lax.fori_loop(0, (n_blocks + 1) // 2, step, jnp.zeros((LANES, LANES), jnp.float32))
+        n_blocks = list_blocks(me, cell, counts, near, far, planes, put_near, put_far, put_none, unroll)
+        put_targets(pts, cell, tgt)
+
+        def step(i, accs):
+            accs = list(accs)
+            charges = [srcv[unroll * i + u] for u in range(unroll)]
+
+            def use(r, u, sq):
+                accs[r] = accs[r] + lax.rsqrt(sq) * charges[u]
+
+            each_square(tgt, src, unroll * i, unroll, use)
+            return tuple(accs)
+
+        zero = jnp.zeros((ROWS, LANES), jnp.float32)
+        accs = lax.fori_loop(0, (n_blocks + unroll - 1) // unroll, step, (zero,) * (LANES // ROWS))
+        acc = jnp.concatenate(accs, axis=0)
         row = dot_nt(jnp.ones((ROWS, LANES), jnp.float32), acc)[0:1, :]
         out[0, t : t + 1, :] = row
         point = own[cell]
@@ -306,11 +297,13 @@
 
 
 def orbital_kernel(
-    planes, batch, unit, steps, meta, counts, near, far, levels, screening, cst,
-    points_before, own, points_after, before, mine, after, squares, *refs,
+    planes, batch, unit, steps, meta, counts, near, far, levels, screening, cst, table,
+    points_before, own, points_after, before, mine, after, *refs,
 ):
-    parts, (out, rate, slot_of, every, val, mom, srcv, dist, inv, acc) = refs[:-10], refs[-10:]
+    parts, (out, rate, slot_of, every, pts, tgt, src, val, mom, srcv, dist, inv, acc) = refs[:-13], refs[-13:]
     lay_out(parts, every)
+    lay_points((points_before, own, points_after), pts)
+    low_half = in_low_half()
     groups, cells, kinds, _ = out.shape
     orbs = groups * kinds
     me, group = meta[0], meta[1]
@@ -344,12 +337,12 @@
         return square.T[:, : 2 * orbs].astype(jnp.bfloat16)
 
     for k in range(3):
-        points, message = (points_before, own, points_after)[k], (before, mine, after)[k]
+        message = (before, mine, after)[k]
         there = lax.bitwise_xor(me, jnp.clip(me - 1 + k, 0, planes - 1))
 
         def prepare(c, carry):
             at = k * PLANE + c
-            point = points[c]
+            point = pts[at]
             potential = point[3:4] + every[there, pl.ds(c, 1), :]
             v = cell_fields(message, c, groups, kinds) * (point[4:5] * potential)
             val[at] = flip(v)
@@ -379,13 +372,16 @@
     lax.fori_loop(0, planes, put_plane, 0)
 
     def put_near(j, slot):
+        src[j] = pts[slot]
         srcv[j] = val[slot]
 
     def put_far(j, first, second, live):
+        src[j] = jnp.where(low_half, table[first], table[second])
         srcv[j, :HALF, :] = mom[first]
         srcv[j, HALF:, :] = jnp.where(live, mom[second], jnp.zeros_like(mom[second]))
 
     def put_none(j):
+        src[j] = jnp.zeros(src.shape[1:], jnp.float32)
         srcv[j] = jnp.zeros(srcv.shape[1:], srcv.dtype)
 
     def products(b, first):
@@ -402,12 +398,15 @@
         n_blocks = list_blocks(me, cell, counts, near, far, planes, put_near, put_far, put_none, unit)
         n_units = (n_blocks + unit - 1) // unit
 
+        put_targets(pts, cell, tgt)
+
         def measure(i, x):
-            for u in range(unit):
-                sq = squares[t, unit * i + u]
-                r = lax.rsqrt(sq)
-                inv[unit * i + u] = r
-                dist[unit * i + u] = sq * r
+            def use(r, u, sq):
+                one_over = lax.rsqrt(sq)
+                inv[unit * i + u, r * ROWS : (r + 1) * ROWS, :] = one_over
+                dist[unit * i + u, r * ROWS : (r + 1) * ROWS, :] = sq * one_over
+
+            each_square(tgt, src, unit * i, unit, use)
             return x
 
         lax.fori_loop(0, n_units, measure, 0)
@@ -500,43 +499,36 @@
     counts = jnp.stack(
         [jnp.sum((near_cells >= 0).astype(jnp.int32), 1), jnp.sum((far_cells >= 0).astype(jnp.int32), 1)], axis=1
     )
-    points_before, points_after = lax.ppermute(own, "space", up), lax.ppermute(own, "space", down)
-
     charges = call(
         charge_kernel, "charge", jax.ShapeDtypeStruct((2 * cells + ROWS, LANES), f32), 1, (meta, cst, own, *fields)
     )
-    charges, (points_before, points_after) = gather_parts(charges, "space", False, (points_before, points_after))
+    mine = jnp.concatenate([f.reshape(kinds * cells, LANES) for f in fields], axis=0)
+    charges, (own, mine) = gather_parts(charges, "space", False, (own, mine))
+    points_before, points_after = lax.ppermute(own, "space", up), lax.ppermute(own, "space", down)
+    before, after = lax.ppermute(mine, "space", up), lax.ppermute(mine, "space", down)
 
     batch, unit, steps = 4, 4, 9
     most = near_cells.shape[1]
     blocks = most + (window - most + planes + 1) // 2 + 2 * unit
-    squares = call(
-        functools.partial(pairs_kernel, groups, planes, unit),
-        "pairs",
-        jax.ShapeDtypeStruct((share, blocks, LANES, LANES), f32),
-        4,
-        (meta, counts, near_cells, far_cells, table, points_before, own, points_after),
-        [
-            pltpu.VMEM((window, ROWS, LANES), f32),
-            pltpu.VMEM((3, LANES, LANES), f32),
-            pltpu.VMEM((blocks, ROWS, LANES), f32),
-        ],
-    )
-    mine = jnp.concatenate([f.reshape(kinds * cells, LANES) for f in fields], axis=0)
-    mine, squares = lax.optimization_barrier((mine, squares))
-    before, after = lax.ppermute(mine, "space", up), lax.ppermute(mine, "space", down)
+    geometry = [
+        pltpu.VMEM((window, ROWS, LANES), f32),
+        pltpu.VMEM((3, LANES, LANES), f32),
+        pltpu.VMEM((blocks, ROWS, LANES), f32),
+    ]
     shares = call(
-        functools.partial(hartree_kernel, groups, kinds),
+        functools.partial(hartree_kernel, groups, kinds, unit),
         "hartree",
         jax.ShapeDtypeStruct((1 + groups, ROWS, LANES), f32),
         4,
-        (meta, counts, near_cells, far_cells, cst, marks, own, mine, squares, *charges),
-        [
-            pltpu.VMEM((planes, 2 * cells + ROWS, LANES), f32),
+        (meta, counts, near_cells, far_cells, cst, table, marks, points_before, own, points_after, mine, *charges),
+        [pltpu.VMEM((planes, 2 * cells + ROWS, LANES), f32)]
+        + geometry
+        + [
             pltpu.VMEM((window, 1, LANES), f32),
             pltpu.VMEM((window + planes, 1, LANES), f32),
             pltpu.VMEM((blocks, 1, LANES), f32),
         ],
+        12,
     )
     shares = gather_list(shares, "orb")
     levels = jnp.concatenate([share[0, ROWS - 1, :kinds] for share in shares]).astype(jnp.int32)
@@ -556,12 +548,13 @@
         "orbitals",
         jax.ShapeDtypeStruct((groups, share, kinds, LANES), f32),
         6,
-        (meta, counts, near_cells, far_cells, levels, screening, cst)
-        + (points_before, own, points_after, before, mine, after, squares, *gathered),
+        (meta, counts, near_cells, far_cells, levels, screening, cst, table)
+        + (points_before, own, points_after, before, mine, after, *gathered),
         [
             pltpu.SMEM((screening.shape[0] + 2 * batch,), f32),
             pltpu.SMEM((screening.shape[0],), jnp.int32),
             pltpu.VMEM((planes, cells + orbs // 2, LANES), f32),
+            *geometry,
             pltpu.VMEM((window, LANES, 2 * orbs), bf16),
             pltpu.VMEM((window + planes, HALF, 2 * orbs), bf16),
             pltpu.VMEM((blocks, LANES, 2 * orbs), bf16),

time: 121 us -> 114 us (0.942)
  the two profiles are of different devices: /device:TPU:14 before, /device:TPU:4 now
where the time goes in v3:
time: 114 us; the launch traced here: 113 us
  Pallas kernels  67.3 us (59%)
  starting transfers between devices  30.9 us (27%)
  waiting for transfers between devices  11.7 us (10%)
  other arithmetic  1.6 us (1%)
    pallas_call x5, Pallas kernels, call(): pl.pallas_call(kernel, out_shape=out_shape, in_specs=[smem()] * smems + [...  67.3 us
    ppermute x14, starting transfers between devices, gather_parts(): lax.ppermute(held, axis, [(i, i ^ have * j) for i in range(count)])  15.9 us
    ppermute x14, waiting for transfers between devices, gather_parts(): lax.ppermute(held, axis, [(i, i ^ have * j) for i in range(count)])  9.94 us
    ppermute x3, starting transfers between devices, body(): lax.ppermute(sent[k], 'orb', [(i, i ^ k) for i in range(groups)])  4.44 us
    ppermute x1, starting transfers between devices, body(): lax.ppermute(mine, 'space', down)  4.4 us
  transfers between devices with their start and end apart: 21, of which 10 were waited for; matrix products, arithmetic and copies ran while one was open for 2% of the time, Pallas kernels for 9%

profile of v3, /device:TPU:4, one launch (start us, length us, event | category | flops | bytes accessed | tf_op | source)
XLA Modules:
  0.0 113.3 jit_solution(13553640435199417493)
XLA Ops:
  0.6 3.7 %collective-permute-start.2 = (f32[1,8,16,128]{3,2,1,0:T(8,128)}, f32[1,8,16,128]{3,2,1,0:T(8,128)S(1)}, u32[]{:S(2)}, u32[]{:S(2)}) collective-permute-start(f32[1,8,16,128]{3,2,1,0:T(8,128)} %bitcast.41), channel_id=1, source_target_pairs={{0,24},{8,16},{16,8},{24,0},{1,25},{9,17},{17,9},{25,1},{2,26},{10... | collective-permute-start | bytes 196616 | tf_op jit(solution)/shard_map/ppermute | solution.py:90
  4.3 0.0 collective-permute-start.1
  4.3 0.8 collective-permute-start
  5.1 0.0 copy-start.5
  5.1 0.6 copy-done.8
  5.7 0.1 copy-done.3
  5.8 0.1 convert_reduce_fusion.1
  5.9 0.0 copy-done.2
  5.9 0.1 convert_reduce_fusion
  6.0 0.0 copy-done.7
  6.1 0.0 copy-done.5
  6.1 0.1 pad.20.clone
  6.2 1.1 multiply_add_fusion.table
  7.3 0.0 copy-start.1
  7.3 0.0 copy-start
  7.3 0.1 maximum_maximum_fusion.own
  7.4 0.1 pad_add_fusion.1.meta
  7.5 0.0 collective-permute-done.2
  7.5 2.6 %collective-permute-done.1 = f32[1,8,16,128]{3,2,1,0:T(8,128)S(1)} collective-permute-done((f32[1,8,16,128]{3,2,1,0:T(8,128)}, f32[1,8,16,128]{3,2,1,0:T(8,128)S(1)}, u32[]{:S(2)}, u32[]{:S(2)}) %collective-permute-start.1) | collective-permute-done | bytes 65568 | tf_op jit(solution)/shard_map/ppermute | solution.py:90
  10.1 0.0 collective-permute-done
  10.1 0.0 copy-done.1
  10.1 2.4 %charge.1 = f32[40,128]{1,0:T(8,128)S(1)} custom-call(s32[2]{0:T(128)S(1)} %pad_add_fusion.1.meta, f32[12,8,128]{2,1,0:T(8,128)S(1)} %copy-done, f32[16,8,128]{2,1,0:T(8,128)S(1)} %maximum_maximum_fusion.own, f32[8,16,128]{2,1,0:T(8,128)S(1)} %copy-done.1, f32[8,16,128]{2,1,0:T(8,128)S(1)} %bitcast.49, f32[8,16,128]{2,1,0:T(8,128)S(1)} %bitcast.47, ...), custom_call_target="tpu_custom_call" | custom-call | tf_op jit(solution)/shard_map/charge/pallas_call | solution.py:464
  12.5 0.0 collective-permute-start.3
  12.6 1.2 %collective-permute-done.3 = f32[1,40,128]{2,1,0:T(8,128)S(1)} collective-permute-done((f32[1,40,128]{2,1,0:T(8,128)S(1)}, f32[1,40,128]{2,1,0:T(8,128)S(1)}, u32[]{:S(2)}, u32[]{:S(2)}) %collective-permute-start.3) | collective-permute-done | bytes 20512 | tf_op jit(solution)/shard_map/ppermute | solution.py:90
  13.8 1.4 %collective-permute-start.8 = (f32[2,40,128]{2,1,0:T(8,128)S(1)}, f32[2,40,128]{2,1,0:T(8,128)S(1)}, u32[]{:S(2)}, u32[]{:S(2)}) collective-permute-start(f32[2,40,128]{2,1,0:T(8,128)S(1)} %pad_maximum_fusion.1.refs_0_), channel_id=1, source_target_pairs={{0,6},{1,7},{2,4},{3,5},{4,2},{5,3},{6,0},{7,1},{8,14},{9,15},{10,... | collective-permute-start | bytes 122888 | tf_op jit(solution)/shard_map/ppermute | solution.py:90
  15.2 1.5 %collective-permute-start.7 = (f32[2,40,128]{2,1,0:T(8,128)S(1)}, f32[2,40,128]{2,1,0:T(8,128)S(1)}, u32[]{:S(2)}, u32[]{:S(2)}) collective-permute-start(f32[2,40,128]{2,1,0:T(8,128)S(1)} %pad_maximum_fusion.1.refs_0_), channel_id=1, source_target_pairs={{0,4},{1,5},{2,6},{3,7},{4,0},{5,1},{6,2},{7,3},{8,12},{9,13},{10,... | collective-permute-start | bytes 122888 | tf_op jit(solution)/shard_map/ppermute | solution.py:90
  16.7 0.5 collective-permute-start.6
  17.3 2.3 %collective-permute-start.5 = (f32[16,8,128]{2,1,0:T(8,128)S(1)}, f32[16,8,128]{2,1,0:T(8,128)S(1)}, u32[]{:S(2)}, u32[]{:S(2)}) collective-permute-start(f32[16,8,128]{2,1,0:T(8,128)S(1)} %maximum_maximum_fusion.own), channel_id=1, source_target_pairs={{1,0},{2,1},{3,2},{4,3},{5,4},{6,5},{7,6},{9,8},{10,9},{11,10},{12... | collective-permute-start | bytes 196616 | tf_op jit(solution)/shard_map/ppermute | solution.py:507
  19.5 2.1 %collective-permute-start.4 = (f32[16,8,128]{2,1,0:T(8,128)S(1)}, f32[16,8,128]{2,1,0:T(8,128)S(1)}, u32[]{:S(2)}, u32[]{:S(2)}) collective-permute-start(f32[16,8,128]{2,1,0:T(8,128)S(1)} %maximum_maximum_fusion.own), channel_id=1, source_target_pairs={{0,1},{1,2},{2,3},{3,4},{4,5},{5,6},{6,7},{8,9},{9,10},{10,11},{11... | collective-permute-start | bytes 196616 | tf_op jit(solution)/shard_map/ppermute | solution.py:507
  21.6 0.1 copy.18.counts
  21.7 0.0 collective-permute-done.8.refs_3_
  21.7 4.4 %collective-permute-start.13 = (f32[512,128]{1,0:T(8,128)S(1)}, f32[512,128]{1,0:T(8,128)S(1)}, u32[]{:S(2)}, u32[]{:S(2)}) collective-permute-start(f32[512,128]{1,0:T(8,128)S(1)} %pad_maximum_fusion.mine), channel_id=1, source_target_pairs={{1,0},{2,1},{3,2},{4,3},{5,4},{6,5},{7,6},{9,8},{10,9},{11,10},{12... | collective-permute-start | bytes 786440 | tf_op jit(solution)/shard_map/ppermute | solution.py:508
  26.1 0.0 collective-permute-done.7.refs_2_
  26.1 1.9 %collective-permute-start.12 = (f32[512,128]{1,0:T(8,128)S(1)}, f32[512,128]{1,0:T(8,128)S(1)}, u32[]{:S(2)}, u32[]{:S(2)}) collective-permute-start(f32[512,128]{1,0:T(8,128)S(1)} %pad_maximum_fusion.mine), channel_id=1, source_target_pairs={{0,1},{1,2},{2,3},{3,4},{4,5},{5,6},{6,7},{8,9},{9,10},{10,11},{11... | collective-permute-start | bytes 786440 | tf_op jit(solution)/shard_map/ppermute | solution.py:508
  28.0 0.0 collective-permute-done.6.refs_1_
  28.0 0.0 collective-permute-done.5.points_after
  28.0 0.0 collective-permute-done.4.points_before
  28.1 9.2 %hartree.1.refs_0_ = f32[5,8,128]{2,1,0:T(8,128)S(1)} custom-call(s32[2]{0:T(128)S(1)} %pad_add_fusion.1.meta, s32[16,2]{1,0:T(8,128)S(1)} %copy.18.counts, s32[16,27]{1,0:T(8,128)S(1)} %copy-done.3, s32[16,42]{1,0:T(8,128)S(1)} %copy-done.2, f32[12,8,128]{2,1,0:T(8,128)S(1)} %copy-done, f32[56,8,128]{2,1,0:T(8,128)S(1)} %multiply_add_fusion.table, ...), custom_call_target="tpu_custom_call" | custom-call | tf_op jit(solution)/shard_map/hartree/pallas_call | solution.py:464
  37.3 2.5 %collective-permute-start.11 = (f32[1,5,8,128]{3,2,1,0:T(8,128)S(1)}, f32[1,5,8,128]{3,2,1,0:T(8,128)S(1)}, u32[]{:S(2)}, u32[]{:S(2)}) collective-permute-start(f32[1,5,8,128]{3,2,1,0:T(8,128)S(1)} %bitcast.53), channel_id=1, source_target_pairs={{0,24},{8,16},{16,8},{24,0},{1,25},{9,17},{17,9},{25,1},{2,26},{10... | collective-permute-start | bytes 61448 | tf_op jit(solution)/shard_map/ppermute | solution.py:90
  39.8 0.0 collective-permute-start.10
  39.8 1.9 %collective-permute-start.9 = (f32[1,5,8,128]{3,2,1,0:T(8,128)S(1)}, f32[1,5,8,128]{3,2,1,0:T(8,128)S(1)}, u32[]{:S(2)}, u32[]{:S(2)}) collective-permute-start(f32[1,5,8,128]{3,2,1,0:T(8,128)S(1)} %bitcast.55), channel_id=1, source_target_pairs={{0,8},{8,0},{16,24},{24,16},{1,9},{9,1},{17,25},{25,17},{2,10},{10... | collective-permute-start | bytes 61448 | tf_op jit(solution)/shard_map/ppermute | solution.py:90
  41.7 1.2 %collective-permute-done.11 = f32[1,5,8,128]{3,2,1,0:T(8,128)S(1)} collective-permute-done((f32[1,5,8,128]{3,2,1,0:T(8,128)S(1)}, f32[1,5,8,128]{3,2,1,0:T(8,128)S(1)}, u32[]{:S(2)}, u32[]{:S(2)}) %collective-permute-start.11) | collective-permute-done | bytes 20512 | tf_op jit(solution)/shard_map/ppermute | solution.py:90
  42.9 1.6 %collective-permute-done.10 = f32[1,5,8,128]{3,2,1,0:T(8,128)S(1)} collective-permute-done((f32[1,5,8,128]{3,2,1,0:T(8,128)S(1)}, f32[1,5,8,128]{3,2,1,0:T(8,128)S(1)}, u32[]{:S(2)}, u32[]{:S(2)}) %collective-permute-start.10) | collective-permute-done | bytes 20512 | tf_op jit(solution)/shard_map/ppermute | solution.py:90
  44.5 0.0 collective-permute-done.9
  44.5 1.2 %combine.1 = (f32[16,128]{1,0:T(8,128)}, f32[32,128]{1,0:T(8,128)S(1)}) custom-call(s32[2]{0:T(128)S(1)} %pad_add_fusion.1.meta, f32[5,8,128]{2,1,0:T(8,128)S(1)} %hartree.1.refs_0_, f32[5,8,128]{2,1,0:T(8,128)S(1)} %bitcast.58, f32[5,8,128]{2,1,0:T(8,128)S(1)} %bitcast.61, f32[5,8,128]{2,1,0:T(8,128)S(1)} %bitcast.57), custom_call_target="tpu_custom_call" | custom-call | tf_op jit(solution)/shard_map/combine/pallas_call | solution.py:464
  45.7 0.0 collective-permute-start.14
  45.7 1.2 %collective-permute-done.14 = f32[1,32,128]{2,1,0:T(8,128)S(1)} collective-permute-done((f32[1,32,128]{2,1,0:T(8,128)S(1)}, f32[1,32,128]{2,1,0:T(8,128)S(1)}, u32[]{:S(2)}, u32[]{:S(2)}) %collective-permute-start.14) | collective-permute-done | bytes 16416 | tf_op jit(solution)/shard_map/ppermute | solution.py:90
  46.9 1.5 %collective-permute-start.17 = (f32[2,32,128]{2,1,0:T(8,128)S(1)}, f32[2,32,128]{2,1,0:T(8,128)S(1)}, u32[]{:S(2)}, u32[]{:S(2)}) collective-permute-start(f32[2,32,128]{2,1,0:T(8,128)S(1)} %pad_maximum_fusion.2.refs_0_), channel_id=1, source_target_pairs={{0,6},{1,7},{2,4},{3,5},{4,2},{5,3},{6,0},{7,1},{8,14},{9,15},{10,... | collective-permute-start | bytes 98312 | tf_op jit(solution)/shard_map/ppermute | solution.py:90
  48.3 0.3 collective-permute-start.16
  48.7 1.7 %collective-permute-start.15 = (f32[2,32,128]{2,1,0:T(8,128)S(1)}, f32[2,32,128]{2,1,0:T(8,128)S(1)}, u32[]{:S(2)}, u32[]{:S(2)}) collective-permute-start(f32[2,32,128]{2,1,0:T(8,128)S(1)} %pad_maximum_fusion.2.refs_0_), channel_id=1, source_target_pairs={{0,2},{1,3},{2,0},{3,1},{4,6},{5,7},{6,4},{7,5},{8,10},{9,11},{10,... | collective-permute-start | bytes 98312 | tf_op jit(solution)/shard_map/ppermute | solution.py:90
  50.4 0.1 maximum_convert_fusion.levels
  50.4 1.3 %collective-permute-done.17.refs_3_ = f32[2,32,128]{2,1,0:T(8,128)S(1)} collective-permute-done((f32[2,32,128]{2,1,0:T(8,128)S(1)}, f32[2,32,128]{2,1,0:T(8,128)S(1)}, u32[]{:S(2)}, u32[]{:S(2)}) %collective-permute-start.17) | collective-permute-done | bytes 32800 | tf_op jit(solution)/shard_map/ppermute | solution.py:90
  51.7 0.6 collective-permute-done.16.refs_2_
  52.3 0.3 collective-permute-done.15.refs_1_
  52.6 0.0 collective-permute-done.13.after
  52.6 0.0 collective-permute-done.12.before
  52.6 53.3 %orbitals.1 = f32[4,4,8,128]{3,2,1,0:T(8,128)S(1)} custom-call(s32[2]{0:T(128)S(1)} %pad_add_fusion.1.meta, s32[16,2]{1,0:T(8,128)S(1)} %copy.18.counts, s32[16,27]{1,0:T(8,128)S(1)} %copy-done.3, s32[16,42]{1,0:T(8,128)S(1)} %copy-done.2, s32[32]{0:T(128)S(1)} %maximum_convert_fusion.levels, f32[32]{0:T(128)S(1)} %copy-done.4, f32[12,8,128]{2,1,0:T(8,128)S(1)} %copy-done, ...), custom_call_target="tpu_custom_call" | custom-call | tf_op jit(solution)/shard_map/orbitals/pallas_call | solution.py:464
  105.9 0.1 collective-permute-start.20
  106.0 0.1 collective-permute-start.19
  106.1 4.3 %collective-permute-start.18 = (f32[4,8,128]{2,1,0:T(8,128)S(1)}, f32[4,8,128]{2,1,0:T(8,128)S(1)}, u32[]{:S(2)}, u32[]{:S(2)}) collective-permute-start(f32[4,8,128]{2,1,0:T(8,128)S(1)} %get-tuple-element.14), channel_id=1, source_target_pairs={{0,8},{8,0},{16,24},{24,16},{1,9},{9,1},{17,25},{25,17},{2,10},{10... | collective-permute-start | bytes 49160 | tf_op jit(solution)/shard_map/ppermute | solution.py:569
  110.4 1.1 %collective-permute-done.20.refs_3_ = f32[4,8,128]{2,1,0:T(8,128)S(1)} collective-permute-done((f32[4,8,128]{2,1,0:T(8,128)S(1)}, f32[4,8,128]{2,1,0:T(8,128)S(1)}, u32[]{:S(2)}, u32[]{:S(2)}) %collective-permute-start.20) | collective-permute-done | bytes 16416 | tf_op jit(solution)/shard_map/ppermute | solution.py:569
  111.5 0.0 collective-permute-done.19.refs_2_
  111.5 0.6 collective-permute-done.18.refs_1_
  112.1 1.2 %place.1 = f32[8,16,128]{2,1,0:T(8,128)} custom-call(s32[2]{0:T(128)S(1)} %pad_add_fusion.1.meta, f32[4,8,128]{2,1,0:T(8,128)S(1)} %get-tuple-element.15.refs_0_, f32[4,8,128]{2,1,0:T(8,128)S(1)} %collective-permute-done.18.refs_1_, f32[4,8,128]{2,1,0:T(8,128)S(1)} %collective-permute-done.19.refs_2_, f32[4,8,128]{2,1,0:T(8,128)S(1)} %collective-permute-done.20.refs_3_), custom_call_target="tpu_custom_call" | custom-call | tf_op jit(solution)/shard_map/place/pallas_call | solution.py:464
  (23 shorter events, 0.1 us)
Async XLA Ops:
  0.6 6.8 %collective-permute-start.2 = (f32[1,8,16,128]{3,2,1,0:T(8,128)}, f32[1,8,16,128]{3,2,1,0:T(8,128)S(1)}, u32[]{:S(2)}, u32[]{:S(2)}) collective-permute-start(f32[1,8,16,128]{3,2,1,0:T(8,128)} %bitcast.41), channel_id=1, source_target_pairs={{0,24},{8,16},{16,8},{24,0},{1,25},{9,17},{17,9},{25,1},{2,26},{10... | collective-permute-start | bytes 196616 | tf_op jit(solution)/shard_map/ppermute | solution.py:90
  4.3 5.8 %collective-permute-start.1 = (f32[1,8,16,128]{3,2,1,0:T(8,128)}, f32[1,8,16,128]{3,2,1,0:T(8,128)S(1)}, u32[]{:S(2)}, u32[]{:S(2)}) collective-permute-start(f32[1,8,16,128]{3,2,1,0:T(8,128)} %bitcast.42), channel_id=1, source_target_pairs={{0,16},{8,24},{16,0},{24,8},{1,17},{9,25},{17,1},{25,9},{2,18},{10... | collective-permute-start | bytes 196616 | tf_op jit(solution)/shard_map/ppermute | solution.py:90
  4.3 5.8 %collective-permute-start = (f32[1,8,16,128]{3,2,1,0:T(8,128)}, f32[1,8,16,128]{3,2,1,0:T(8,128)S(1)}, u32[]{:S(2)}, u32[]{:S(2)}) collective-permute-start(f32[1,8,16,128]{3,2,1,0:T(8,128)} %bitcast.43), channel_id=1, source_target_pairs={{0,8},{8,0},{16,24},{24,16},{1,9},{9,1},{17,25},{25,17},{2,10},{10... | collective-permute-start | bytes 196616 | tf_op jit(solution)/shard_map/ppermute | solution.py:90
  5.1 0.7 copy-start.8
  5.1 1.0 copy-start.7
  5.1 0.7 copy-start.3
  5.1 0.8 copy-start.2
  5.1 1.0 copy-start.5
  6.2 1.1 copy-start.6
  7.3 2.8 %copy-start.1 = (f32[8,16,128]{2,1,0:T(8,128)S(1)}, f32[8,16,128]{2,1,0:T(8,128)}, u32[]{:S(2)}) copy-start(f32[8,16,128]{2,1,0:T(8,128)} %refs_0_.1) | copy-start | bytes 196612
  7.3 2.8 %copy-start = (f32[12,8,128]{2,1,0:T(8,128)S(1)}, f32[12,8,128]{2,1,0:T(8,128)}, u32[]{:S(2)}) copy-start(f32[12,8,128]{2,1,0:T(8,128)} %constant.26.clone.cst) | copy-start | bytes 147460
  12.5 1.2 %collective-permute-start.3 = (f32[1,40,128]{2,1,0:T(8,128)S(1)}, f32[1,40,128]{2,1,0:T(8,128)S(1)}, u32[]{:S(2)}, u32[]{:S(2)}) collective-permute-start(f32[1,40,128]{2,1,0:T(8,128)S(1)} %bitcast.51), channel_id=1, source_target_pairs={{0,1},{1,0},{2,3},{3,2},{4,5},{5,4},{6,7},{7,6},{8,9},{9,8},{10,11... | collective-permute-start | bytes 61448 | tf_op jit(solution)/shard_map/ppermute | solution.py:90
  13.8 7.9 %collective-permute-start.8 = (f32[2,40,128]{2,1,0:T(8,128)S(1)}, f32[2,40,128]{2,1,0:T(8,128)S(1)}, u32[]{:S(2)}, u32[]{:S(2)}) collective-permute-start(f32[2,40,128]{2,1,0:T(8,128)S(1)} %pad_maximum_fusion.1.refs_0_), channel_id=1, source_target_pairs={{0,6},{1,7},{2,4},{3,5},{4,2},{5,3},{6,0},{7,1},{8,14},{9,15},{10,... | collective-permute-start | bytes 122888 | tf_op jit(solution)/shard_map/ppermute | solution.py:90
  15.2 10.9 %collective-permute-start.7 = (f32[2,40,128]{2,1,0:T(8,128)S(1)}, f32[2,40,128]{2,1,0:T(8,128)S(1)}, u32[]{:S(2)}, u32[]{:S(2)}) collective-permute-start(f32[2,40,128]{2,1,0:T(8,128)S(1)} %pad_maximum_fusion.1.refs_0_), channel_id=1, source_target_pairs={{0,4},{1,5},{2,6},{3,7},{4,0},{5,1},{6,2},{7,3},{8,12},{9,13},{10,... | collective-permute-start | bytes 122888 | tf_op jit(solution)/shard_map/ppermute | solution.py:90
  16.7 11.3 %collective-permute-start.6 = (f32[2,40,128]{2,1,0:T(8,128)S(1)}, f32[2,40,128]{2,1,0:T(8,128)S(1)}, u32[]{:S(2)}, u32[]{:S(2)}) collective-permute-start(f32[2,40,128]{2,1,0:T(8,128)S(1)} %pad_maximum_fusion.1.refs_0_), channel_id=1, source_target_pairs={{0,2},{1,3},{2,0},{3,1},{4,6},{5,7},{6,4},{7,5},{8,10},{9,11},{10,... | collective-permute-start | bytes 122888 | tf_op jit(solution)/shard_map/ppermute | solution.py:90
  17.3 10.8 %collective-permute-start.5 = (f32[16,8,128]{2,1,0:T(8,128)S(1)}, f32[16,8,128]{2,1,0:T(8,128)S(1)}, u32[]{:S(2)}, u32[]{:S(2)}) collective-permute-start(f32[16,8,128]{2,1,0:T(8,128)S(1)} %maximum_maximum_fusion.own), channel_id=1, source_target_pairs={{1,0},{2,1},{3,2},{4,3},{5,4},{6,5},{7,6},{9,8},{10,9},{11,10},{12... | collective-permute-start | bytes 196616 | tf_op jit(solution)/shard_map/ppermute | solution.py:507
  19.5 8.5 %collective-permute-start.4 = (f32[16,8,128]{2,1,0:T(8,128)S(1)}, f32[16,8,128]{2,1,0:T(8,128)S(1)}, u32[]{:S(2)}, u32[]{:S(2)}) collective-permute-start(f32[16,8,128]{2,1,0:T(8,128)S(1)} %maximum_maximum_fusion.own), channel_id=1, source_target_pairs={{0,1},{1,2},{2,3},{3,4},{4,5},{5,6},{6,7},{8,9},{9,10},{10,11},{11... | collective-permute-start | bytes 196616 | tf_op jit(solution)/shard_map/ppermute | solution.py:507
  21.7 30.9 %collective-permute-start.13 = (f32[512,128]{1,0:T(8,128)S(1)}, f32[512,128]{1,0:T(8,128)S(1)}, u32[]{:S(2)}, u32[]{:S(2)}) collective-permute-start(f32[512,128]{1,0:T(8,128)S(1)} %pad_maximum_fusion.mine), channel_id=1, source_target_pairs={{1,0},{2,1},{3,2},{4,3},{5,4},{6,5},{7,6},{9,8},{10,9},{11,10},{12... | collective-permute-start | bytes 786440 | tf_op jit(solution)/shard_map/ppermute | solution.py:508
  26.1 26.5 %collective-permute-start.12 = (f32[512,128]{1,0:T(8,128)S(1)}, f32[512,128]{1,0:T(8,128)S(1)}, u32[]{:S(2)}, u32[]{:S(2)}) collective-permute-start(f32[512,128]{1,0:T(8,128)S(1)} %pad_maximum_fusion.mine), channel_id=1, source_target_pairs={{0,1},{1,2},{2,3},{3,4},{4,5},{5,6},{6,7},{8,9},{9,10},{10,11},{11... | collective-permute-start | bytes 786440 | tf_op jit(solution)/shard_map/ppermute | solution.py:508
  37.3 5.6 %collective-permute-start.11 = (f32[1,5,8,128]{3,2,1,0:T(8,128)S(1)}, f32[1,5,8,128]{3,2,1,0:T(8,128)S(1)}, u32[]{:S(2)}, u32[]{:S(2)}) collective-permute-start(f32[1,5,8,128]{3,2,1,0:T(8,128)S(1)} %bitcast.53), channel_id=1, source_target_pairs={{0,24},{8,16},{16,8},{24,0},{1,25},{9,17},{17,9},{25,1},{2,26},{10... | collective-permute-start | bytes 61448 | tf_op jit(solution)/shard_map/ppermute | solution.py:90
  39.8 4.7 %collective-permute-start.10 = (f32[1,5,8,128]{3,2,1,0:T(8,128)S(1)}, f32[1,5,8,128]{3,2,1,0:T(8,128)S(1)}, u32[]{:S(2)}, u32[]{:S(2)}) collective-permute-start(f32[1,5,8,128]{3,2,1,0:T(8,128)S(1)} %bitcast.54), channel_id=1, source_target_pairs={{0,16},{8,24},{16,0},{24,8},{1,17},{9,25},{17,1},{25,9},{2,18},{10... | collective-permute-start | bytes 61448 | tf_op jit(solution)/shard_map/ppermute | solution.py:90
  39.8 4.7 %collective-permute-start.9 = (f32[1,5,8,128]{3,2,1,0:T(8,128)S(1)}, f32[1,5,8,128]{3,2,1,0:T(8,128)S(1)}, u32[]{:S(2)}, u32[]{:S(2)}) collective-permute-start(f32[1,5,8,128]{3,2,1,0:T(8,128)S(1)} %bitcast.55), channel_id=1, source_target_pairs={{0,8},{8,0},{16,24},{24,16},{1,9},{9,1},{17,25},{25,17},{2,10},{10... | collective-permute-start | bytes 61448 | tf_op jit(solution)/shard_map/ppermute | solution.py:90
  45.7 1.2 %collective-permute-start.14 = (f32[1,32,128]{2,1,0:T(8,128)S(1)}, f32[1,32,128]{2,1,0:T(8,128)S(1)}, u32[]{:S(2)}, u32[]{:S(2)}) collective-permute-start(f32[1,32,128]{2,1,0:T(8,128)S(1)} %bitcast.62), channel_id=1, source_target_pairs={{0,1},{1,0},{2,3},{3,2},{4,5},{5,4},{6,7},{7,6},{8,9},{9,8},{10,11... | collective-permute-start | bytes 49160 | tf_op jit(solution)/shard_map/ppermute | solution.py:90
  46.9 5.7 %copy-start.4 = (f32[32]{0:T(128)S(1)}, f32[32]{0:T(128)}, u32[]{:S(2)}) copy-start(f32[32]{0:T(128)} %screening.1) | copy-start | bytes 388
  46.9 4.8 %collective-permute-start.17 = (f32[2,32,128]{2,1,0:T(8,128)S(1)}, f32[2,32,128]{2,1,0:T(8,128)S(1)}, u32[]{:S(2)}, u32[]{:S(2)}) collective-permute-start(f32[2,32,128]{2,1,0:T(8,128)S(1)} %pad_maximum_fusion.2.refs_0_), channel_id=1, source_target_pairs={{0,6},{1,7},{2,4},{3,5},{4,2},{5,3},{6,0},{7,1},{8,14},{9,15},{10,... | collective-permute-start | bytes 98312 | tf_op jit(solution)/shard_map/ppermute | solution.py:90
  48.3 3.9 %collective-permute-start.16 = (f32[2,32,128]{2,1,0:T(8,128)S(1)}, f32[2,32,128]{2,1,0:T(8,128)S(1)}, u32[]{:S(2)}, u32[]{:S(2)}) collective-permute-start(f32[2,32,128]{2,1,0:T(8,128)S(1)} %pad_maximum_fusion.2.refs_0_), channel_id=1, source_target_pairs={{0,4},{1,5},{2,6},{3,7},{4,0},{5,1},{6,2},{7,3},{8,12},{9,13},{10,... | collective-permute-start | bytes 98312 | tf_op jit(solution)/shard_map/ppermute | solution.py:90
  48.7 3.9 %collective-permute-start.15 = (f32[2,32,128]{2,1,0:T(8,128)S(1)}, f32[2,32,128]{2,1,0:T(8,128)S(1)}, u32[]{:S(2)}, u32[]{:S(2)}) collective-permute-start(f32[2,32,128]{2,1,0:T(8,128)S(1)} %pad_maximum_fusion.2.refs_0_), channel_id=1, source_target_pairs={{0,2},{1,3},{2,0},{3,1},{4,6},{5,7},{6,4},{7,5},{8,10},{9,11},{10,... | collective-permute-start | bytes 98312 | tf_op jit(solution)/shard_map/ppermute | solution.py:90
  105.9 5.6 %collective-permute-start.20 = (f32[4,8,128]{2,1,0:T(8,128)S(1)}, f32[4,8,128]{2,1,0:T(8,128)S(1)}, u32[]{:S(2)}, u32[]{:S(2)}) collective-permute-start(f32[4,8,128]{2,1,0:T(8,128)S(1)} %get-tuple-element.12), channel_id=1, source_target_pairs={{0,24},{8,16},{16,8},{24,0},{1,25},{9,17},{17,9},{25,1},{2,26},{10... | collective-permute-start | bytes 49160 | tf_op jit(solution)/shard_map/ppermute | solution.py:569
  106.0 5.5 %collective-permute-start.19 = (f32[4,8,128]{2,1,0:T(8,128)S(1)}, f32[4,8,128]{2,1,0:T(8,128)S(1)}, u32[]{:S(2)}, u32[]{:S(2)}) collective-permute-start(f32[4,8,128]{2,1,0:T(8,128)S(1)} %get-tuple-element.13), channel_id=1, source_target_pairs={{0,16},{8,24},{16,0},{24,8},{1,17},{9,25},{17,1},{25,9},{2,18},{10... | collective-permute-start | bytes 49160 | tf_op jit(solution)/shard_map/ppermute | solution.py:569
  106.1 6.0 %collective-permute-start.18 = (f32[4,8,128]{2,1,0:T(8,128)S(1)}, f32[4,8,128]{2,1,0:T(8,128)S(1)}, u32[]{:S(2)}, u32[]{:S(2)}) collective-permute-start(f32[4,8,128]{2,1,0:T(8,128)S(1)} %get-tuple-element.14), channel_id=1, source_target_pairs={{0,8},{8,0},{16,24},{24,16},{1,9},{9,1},{17,25},{25,17},{2,10},{10... | collective-permute-start | bytes 49160 | tf_op jit(solution)/shard_map/ppermute | solution.py:569

commit v4 on v3

--- a/solution.py
+++ b/solution.py
@@ -80,7 +80,7 @@
     return lax.dot_general(a, b, (((1,), (1,)), ((), ())), precision=highest, preferred_element_type=jnp.float32)
 
 
-def gather_parts(block, axis, pairs, later=None):
+def gather_parts(block, axis, pairs):
     count = lax.axis_size(axis)
     parts = [block[None]]
     while sum(p.shape[0] for p in parts) < count:
@@ -88,13 +88,11 @@
         have = held.shape[0]
         steps = range(1, 4 if (have > 1 or pairs) and have * 4 <= count else 2)
         parts = [held] + [lax.ppermute(held, axis, [(i, i ^ (have * j)) for i in range(count)]) for j in steps]
-        if later is not None and have == 1:
-            parts[1], later = lax.optimization_barrier((parts[1], later))
-    return parts, later
+    return parts
 
 
 def gather_list(block, axis):
-    parts, _ = gather_parts(block, axis, True)
+    parts = gather_parts(block, axis, True)
     return [p[k] for p in parts for k in range(p.shape[0])]
 
 
@@ -127,26 +125,34 @@
     return both[:rows] + both[rows:] + dot_bf16(vh, wl)
 
 
+def lane_sums(v):
+    high, low = split(v)
+    ones = jnp.ones((ROWS, 2 * v.shape[1]), jnp.bfloat16)
+    return dot_bf16(ones, jnp.concatenate([high, low], axis=1))[0:1, :]
+
+
 def charge_kernel(meta, cst, own, *refs):
     z_low = meta[0].astype(jnp.float32) * cell_side
-    fields, out = refs[:-1], refs[-1]
-    density = jnp.zeros((PLANE, LANES), jnp.float32)
+    fields, (out, density) = refs[:-2], refs[-2:]
+    total = jnp.zeros((PLANE, LANES), jnp.float32)
     for phi in fields:
         for j in range(phi.shape[0]):
             v = phi[j]
-            density = density + v * v
-    out[:PLANE, :] = density
+            total = total + v * v
+    density[...] = 2.0 * total
     acc = jnp.zeros((HALF, LANES), jnp.float32)
-    ones = jnp.ones((ROWS, LANES), jnp.float32)
     for c in range(PLANE):
-        charge = own[c, 4:5, :] * (2.0 * out[c : c + 1, :])
-        out[c : c + 1, :] = charge
-        x, y, z = own[c, 0:1, :], own[c, 1:2, :], own[c, 2:3, :]
+        point = own[c]
+        charge = point[4:5] * density[c : c + 1, :]
         low = (cell_side * (c % 4), cell_side * (c // 4), z_low)
-        acc = acc + weights(cst, x, y, z, (0.0, 0.0, z_low), (1.0, 1.0, cell_side)) * charge
-        moments = dot_nt(ones, twice(weights(cst, x, y, z, low, (cell_side,) * 3) * charge))
-        out[PLANE + c : PLANE + c + 1, :] = moments[0:1, :]
-    out[2 * PLANE :, :] = dot_nt(ones, twice(acc))
+        acc = acc + weights(cst, point[0:1], point[1:2], point[2:3], (0.0, 0.0, z_low), (1.0, 1.0, cell_side)) * charge
+        moments = lane_sums(weights(cst, point[0:1], point[1:2], point[2:3], low, (cell_side,) * 3) * charge)
+        out[c, :5, :] = point[:5]
+        out[c, 5:6, :] = charge
+        out[c, 6:7, :] = jnp.concatenate([moments, moments], axis=1)
+    moments = lane_sums(acc)
+    for c in range(PLANE):
+        out[c, 7:8, :] = jnp.concatenate([moments, moments], axis=1)
 
 
 def live_planes(me, planes):
@@ -203,79 +209,100 @@
             use(r, u, (dx * dx + dy * dy) + (dz * dz + soften))
 
 
-def lay_points(windows, pts):
-    for k, points in enumerate(windows):
-        pts[k * PLANE : (k + 1) * PLANE] = points[...]
-
-
 def cell_fields(message, c, groups, kinds):
     rows = kinds * PLANE
     return jnp.concatenate([message[pl.ds(g * rows + c, kinds, stride=PLANE), :] for g in range(groups)], axis=0)
 
 
-def hartree_kernel(
-    groups, kinds, unroll, meta, counts, near, far, cst, table, marks, points_before, own, points_after, mine, *refs
-):
-    parts, (out, every, pts, tgt, src, val, mom, srcv) = refs[:-8], refs[-8:]
+def hartree_kernel(groups, kinds, unroll, meta, counts, near, far, cst, table, marks, mine, *refs):
+    parts, (out, pts, src, every, items, tgt) = refs[:-6], refs[-6:]
     lay_out(parts, every)
-    lay_points((points_before, own, points_after), pts)
     planes = every.shape[0]
     cells = PLANE // groups
     me, group = meta[0], meta[1]
+    window = 3 * PLANE
     for k in range(3):
         there = lax.bitwise_xor(me, jnp.clip(me - 1 + k, 0, planes - 1))
-        val[k * PLANE : (k + 1) * PLANE, 0, :] = every[there, :PLANE, :]
-        mom[k * PLANE : (k + 1) * PLANE, 0, :] = every[there, PLANE : 2 * PLANE, :]
+        for c in range(PLANE):
+            pts[k * PLANE + c] = every[there, c]
+    row = lax.broadcasted_iota(jnp.int32, (ROWS, 1), 0)
+
+    def put_cell(c, carry):
+        items[c] = jnp.where(row == 5, pts[c, 6:7, :], table[c])
+        return carry
+
+    lax.fori_loop(0, window, put_cell, 0, unroll=8)
 
     def put_plane(g, c):
-        mom[3 * PLANE + g] = every[lax.bitwise_xor(me, g), 2 * PLANE : 2 * PLANE + 1, :]
+        items[window + g] = jnp.where(row == 5, every[lax.bitwise_xor(me, g), 0, 7:8, :], table[window + g])
         return c
 
     lax.fori_loop(0, planes, put_plane, 0)
+    items[window + planes] = jnp.zeros((ROWS, LANES), jnp.float32)
     low_half = in_low_half()
-
-    def put_near(j, slot):
-        src[j] = pts[slot]
-        srcv[j] = val[slot]
-
-    def put_far(j, first, second, live):
-        src[j] = jnp.where(low_half, table[first], table[second])
-        srcv[j] = jnp.where(low_half, mom[first], mom[second] * live.astype(jnp.float32))
-
-    def put_none(j):
-        src[j] = jnp.zeros(src.shape[1:], jnp.float32)
-        srcv[j] = jnp.zeros((1, LANES), jnp.float32)
-
     z_low = me.astype(jnp.float32) * cell_side
     total = jnp.zeros((groups * kinds, LANES), jnp.float32)
     out[0] = jnp.broadcast_to(marks[...], (ROWS, LANES))
     for t in range(cells):
         cell = target_cell(group, t, groups)
+
+        def put_near(j, slot):
+            src[t, j] = pts[slot]
+
+        def put_far(j, first, second, live):
+            src[t, j] = jnp.where(low_half, items[first], items[jnp.where(live, second, window + planes)])
+
+        def put_none(j):
+            src[t, j] = jnp.zeros((ROWS, LANES), jnp.float32)
+
         n_blocks = list_blocks(me, cell, counts, near, far, planes, put_near, put_far, put_none, unroll)
         put_targets(pts, cell, tgt)
 
         def step(i, accs):
             accs = list(accs)
-            charges = [srcv[unroll * i + u] for u in range(unroll)]
+            charges = [src[t, unroll * i + u, 5:6, :] for u in range(unroll)]
 
             def use(r, u, sq):
                 accs[r] = accs[r] + lax.rsqrt(sq) * charges[u]
 
-            each_square(tgt, src, unroll * i, unroll, use)
+            each_square(tgt, src.at[t], unroll * i, unroll, use)
             return tuple(accs)
 
         zero = jnp.zeros((ROWS, LANES), jnp.float32)
         accs = lax.fori_loop(0, (n_blocks + unroll - 1) // unroll, step, (zero,) * (LANES // ROWS))
-        acc = jnp.concatenate(accs, axis=0)
-        row = dot_nt(jnp.ones((ROWS, LANES), jnp.float32), acc)[0:1, :]
-        out[0, t : t + 1, :] = row
-        point = own[cell]
-        scaled = point[4:5] * (point[3:4] + row)
+        potential = dot_nt(jnp.ones((ROWS, LANES), jnp.float32), jnp.concatenate(accs, axis=0))[0:1, :]
+        out[0, t : t + 1, :] = potential
+        point = pts[PLANE + cell]
+        scaled = point[4:5] * (point[3:4] + potential)
         v = cell_fields(mine, cell, groups, kinds) * scaled
         w = weights(cst, point[0:1], point[1:2], point[2:3], (0.0, 0.0, z_low), (1.0, 1.0, cell_side))
         total = total + dot_split(v, twice(w))
     for k in range(groups):
         out[1 + lax.bitwise_xor(group, k), :kinds, :] = total[k * kinds : (k + 1) * kinds, :]
+
+
+def pairs_kernel(groups, planes, unroll, meta, counts, pts, src, dist, inv, tgt):
+    group = meta[1]
+    _, n_planes = live_planes(meta[0], planes)
+
+    def per_cell(t, carry):
+        cell = target_cell(group, t, groups)
+        put_targets(pts, cell, tgt)
+        n_blocks = counts[cell, 0] + (counts[cell, 1] + n_planes + 1) // 2
+
+        def measure(i, x):
+            def use(r, u, sq):
+                one_over = lax.rsqrt(sq)
+                inv[t, unroll * i + u, r * ROWS : (r + 1) * ROWS, :] = one_over
+                dist[t, unroll * i + u, r * ROWS : (r + 1) * ROWS, :] = sq * one_over
+
+            each_square(tgt, src.at[t], unroll * i, unroll, use)
+            return x
+
+        lax.fori_loop(0, (n_blocks + unroll - 1) // unroll, measure, 0)
+        return carry
+
+    lax.fori_loop(0, PLANE // groups, per_cell, 0)
 
 
 def combine_kernel(kinds, meta, *refs):
@@ -297,13 +324,11 @@
 
 
 def orbital_kernel(
-    planes, batch, unit, steps, meta, counts, near, far, levels, screening, cst, table,
-    points_before, own, points_after, before, mine, after, *refs,
+    planes, batch, unit, steps, meta, counts, near, far, levels, screening, cst,
+    pts, before, mine, after, dist, inv, *refs,
 ):
-    parts, (out, rate, slot_of, every, pts, tgt, src, val, mom, srcv, dist, inv, acc) = refs[:-13], refs[-13:]
+    parts, (out, rate, slot_of, every, val, mom, srcv, acc) = refs[:-8], refs[-8:]
     lay_out(parts, every)
-    lay_points((points_before, own, points_after), pts)
-    low_half = in_low_half()
     groups, cells, kinds, _ = out.shape
     orbs = groups * kinds
     me, group = meta[0], meta[1]
@@ -372,23 +397,20 @@
     lax.fori_loop(0, planes, put_plane, 0)
 
     def put_near(j, slot):
-        src[j] = pts[slot]
         srcv[j] = val[slot]
 
     def put_far(j, first, second, live):
-        src[j] = jnp.where(low_half, table[first], table[second])
         srcv[j, :HALF, :] = mom[first]
         srcv[j, HALF:, :] = jnp.where(live, mom[second], jnp.zeros_like(mom[second]))
 
     def put_none(j):
-        src[j] = jnp.zeros(src.shape[1:], jnp.float32)
         srcv[j] = jnp.zeros(srcv.shape[1:], srcv.dtype)
 
-    def products(b, first):
+    def products(t, b, first):
         rates = [rate[b * batch + q] for q in range(batch)]
         rows = []
         for q in range(batch):
-            tiles = [(jnp.exp2(dist[first + h] * rates[q]) * inv[first + h]).astype(jnp.bfloat16) for h in range(unit)]
+            tiles = [(jnp.exp2(dist[t, first + h] * rates[q]) * inv[t, first + h]).astype(jnp.bfloat16) for h in range(unit)]
             rows.append(jnp.concatenate(tiles, axis=1))
         v = jnp.concatenate([srcv[first + h] for h in range(unit)], axis=0)
         return jnp.dot(jnp.concatenate(rows, axis=0), v, preferred_element_type=jnp.float32)
@@ -398,19 +420,6 @@
         n_blocks = list_blocks(me, cell, counts, near, far, planes, put_near, put_far, put_none, unit)
         n_units = (n_blocks + unit - 1) // unit
 
-        put_targets(pts, cell, tgt)
-
-        def measure(i, x):
-            def use(r, u, sq):
-                one_over = lax.rsqrt(sq)
-                inv[unit * i + u, r * ROWS : (r + 1) * ROWS, :] = one_over
-                dist[unit * i + u, r * ROWS : (r + 1) * ROWS, :] = sq * one_over
-
-            each_square(tgt, src, unit * i, unit, use)
-            return x
-
-        lax.fori_loop(0, n_units, measure, 0)
-
         def clear_acc(b, x):
             acc[b] = jnp.zeros(acc.shape[1:], jnp.float32)
             return x
@@ -420,7 +429,7 @@
         def step(i, at):
             b, u = at
             for _ in range(steps):
-                acc[b] = acc[b] + products(b, unit * u)
+                acc[b] = acc[b] + products(t, b, unit * u)
                 wrap = u + 1 == n_units
                 b, u = jnp.where(wrap, b + 1, b), jnp.where(wrap, 0, u + 1)
             return b, u
@@ -500,36 +509,48 @@
         [jnp.sum((near_cells >= 0).astype(jnp.int32), 1), jnp.sum((far_cells >= 0).astype(jnp.int32), 1)], axis=1
     )
     charges = call(
-        charge_kernel, "charge", jax.ShapeDtypeStruct((2 * cells + ROWS, LANES), f32), 1, (meta, cst, own, *fields)
-    )
+        charge_kernel,
+        "charge",
+        jax.ShapeDtypeStruct((cells, ROWS, LANES), f32),
+        1,
+        (meta, cst, own, *fields),
+        [pltpu.VMEM((cells, LANES), f32)],
+    )
+    charges = gather_parts(charges, "space", False)
     mine = jnp.concatenate([f.reshape(kinds * cells, LANES) for f in fields], axis=0)
-    charges, (own, mine) = gather_parts(charges, "space", False, (own, mine))
-    points_before, points_after = lax.ppermute(own, "space", up), lax.ppermute(own, "space", down)
-    before, after = lax.ppermute(mine, "space", up), lax.ppermute(mine, "space", down)
 
     batch, unit, steps = 4, 4, 9
     most = near_cells.shape[1]
-    blocks = most + (window - most + planes + 1) // 2 + 2 * unit
-    geometry = [
-        pltpu.VMEM((window, ROWS, LANES), f32),
-        pltpu.VMEM((3, LANES, LANES), f32),
-        pltpu.VMEM((blocks, ROWS, LANES), f32),
-    ]
-    shares = call(
+    blocks = most + (window - most + planes + 1) // 2
+    blocks = -(-blocks // unit) * unit + unit
+    shares, pts, src = call(
         functools.partial(hartree_kernel, groups, kinds, unit),
         "hartree",
-        jax.ShapeDtypeStruct((1 + groups, ROWS, LANES), f32),
+        (
+            jax.ShapeDtypeStruct((1 + groups, ROWS, LANES), f32),
+            jax.ShapeDtypeStruct((window, ROWS, LANES), f32),
+            jax.ShapeDtypeStruct((share, blocks, ROWS, LANES), f32),
+        ),
         4,
-        (meta, counts, near_cells, far_cells, cst, table, marks, points_before, own, points_after, mine, *charges),
-        [pltpu.VMEM((planes, 2 * cells + ROWS, LANES), f32)]
-        + geometry
-        + [
-            pltpu.VMEM((window, 1, LANES), f32),
-            pltpu.VMEM((window + planes, 1, LANES), f32),
-            pltpu.VMEM((blocks, 1, LANES), f32),
+        (meta, counts, near_cells, far_cells, cst, table, marks, mine, *charges),
+        [
+            pltpu.VMEM((planes, cells, ROWS, LANES), f32),
+            pltpu.VMEM((window + planes + 1, ROWS, LANES), f32),
+            pltpu.VMEM((3, LANES, LANES), f32),
         ],
         12,
     )
+    dist, inv = call(
+        functools.partial(pairs_kernel, groups, planes, unit),
+        "pairs",
+        (jax.ShapeDtypeStruct((share, blocks, LANES, LANES), f32),) * 2,
+        2,
+        (meta, counts, pts, src),
+        [pltpu.VMEM((3, LANES, LANES), f32)],
+        4,
+    )
+    mine, shares = lax.optimization_barrier((mine, shares))
+    before, after = lax.ppermute(mine, "space", up), lax.ppermute(mine, "space", down)
     shares = gather_list(shares, "orb")
     levels = jnp.concatenate([share[0, ROWS - 1, :kinds] for share in shares]).astype(jnp.int32)
     hartree, combined = call(
@@ -540,7 +561,7 @@
         (meta, *shares),
         [pltpu.VMEM((orbs, LANES), f32)],
     )
-    gathered, _ = gather_parts(combined, "space", False)
+    gathered = gather_parts(combined, "space", False)
 
     levels_at_most = -(-screening.shape[0] // batch) + 1
     sent = call(
@@ -548,21 +569,17 @@
         "orbitals",
         jax.ShapeDtypeStruct((groups, share, kinds, LANES), f32),
         6,
-        (meta, counts, near_cells, far_cells, levels, screening, cst, table)
-        + (points_before, own, points_after, before, mine, after, *gathered),
+        (meta, counts, near_cells, far_cells, levels, screening, cst, pts, before, mine, after, dist, inv, *gathered),
         [
             pltpu.SMEM((screening.shape[0] + 2 * batch,), f32),
             pltpu.SMEM((screening.shape[0],), jnp.int32),
             pltpu.VMEM((planes, cells + orbs // 2, LANES), f32),
-            *geometry,
             pltpu.VMEM((window, LANES, 2 * orbs), bf16),
             pltpu.VMEM((window + planes, HALF, 2 * orbs), bf16),
             pltpu.VMEM((blocks, LANES, 2 * orbs), bf16),
-            pltpu.VMEM((blocks, LANES, LANES), f32),
-            pltpu.VMEM((blocks, LANES, LANES), f32),
             pltpu.VMEM((levels_at_most, batch * LANES, 2 * orbs), f32),
         ],
-        24,
+        14,
     )
     parts = [sent[0]]
     for k in range(1, groups):

time: 114 us -> 117 us (1.026); the launches traced: 113 us -> 115 us
  Pallas kernels: 67.3 us -> 58.9 us
  local copies, waits for them, and re-layouts: 0.94 us -> 7.61 us
  other arithmetic: 1.6 us -> 5.86 us
  starting transfers between devices: 30.9 us -> 26.8 us
  waiting for transfers between devices: 11.7 us -> 15 us
    pallas_call x5 -> x6, Pallas kernels: 67.3 us -> 58.9 us  [call(): pl.pallas_call(kernel, out_shape=out_shape, in_specs=[smem()] * smems + [...]
    unnamed x19, local copies, waits for them, and re-layouts: 0.75 us -> 7.43 us
    ppermute x2 -> x0, starting transfers between devices: 4.31 us -> none  [the longest x1 2.26 us: body(): lax.ppermute(own, 'space', down)]
    ppermute x3, waiting for transfers between devices: 1.71 us -> 5.17 us  [body(): lax.ppermute(sent[k], 'orb', [(i, i ^ k) for i in range(groups)])]
  transfers between devices with their start and end apart: 21 -> 19, of which waited for: 10 -> 9; matrix products, arithmetic and copies ran while one was open for 2% -> 6% of each run, Pallas kernels for 9% -> 5%
where the time goes in v4:
time: 117 us; the launch traced here: 115 us
  Pallas kernels  58.9 us (50%)
  starting transfers between devices  26.8 us (23%)
  waiting for transfers between devices  15 us (13%)
  local copies, waits for them, and re-layouts  7.61 us (7%)
  other arithmetic  5.86 us (5%)
    pallas_call x6, Pallas kernels, call(): pl.pallas_call(kernel, out_shape=out_shape, in_specs=[smem()] * smems + [...  58.9 us
    ppermute x14, starting transfers between devices, gather_parts(): lax.ppermute(held, axis, [(i, i ^ have * j) for i in range(count)])  15.9 us
    ppermute x14, waiting for transfers between devices, gather_parts(): lax.ppermute(held, axis, [(i, i ^ have * j) for i in range(count)])  9.78 us
    unnamed x19, local copies, waits for them, and re-layouts  7.43 us
    ppermute x3, waiting for transfers between devices, body(): lax.ppermute(sent[k], 'orb', [(i, i ^ k) for i in range(groups)])  5.17 us
    ppermute x1, starting transfers between devices, body(): lax.ppermute(mine, 'space', down)  4.54 us
    ppermute x3, starting transfers between devices, body(): lax.ppermute(sent[k], 'orb', [(i, i ^ k) for i in range(groups)])  4.44 us
  transfers between devices with their start and end apart: 19, of which 9 were waited for; matrix products, arithmetic and copies ran while one was open for 6% of the time, Pallas kernels for 5%

profile of v4, /device:TPU:4, one launch (start us, length us, event | category | flops | bytes accessed | tf_op | source)
XLA Modules:
  0.0 114.9 jit_solution(3964492830281219431)
XLA Ops:
  0.6 1.6 %collective-permute-start = (f32[1,8,16,128]{3,2,1,0:T(8,128)}, f32[1,8,16,128]{3,2,1,0:T(8,128)S(1)}, u32[]{:S(2)}, u32[]{:S(2)}) collective-permute-start(f32[1,8,16,128]{3,2,1,0:T(8,128)} %bitcast.43), channel_id=1, source_target_pairs={{0,8},{8,0},{16,24},{24,16},{1,9},{9,1},{17,25},{25,17},{2,10},{10... | collective-permute-start | bytes 196616 | tf_op jit(solution)/shard_map/ppermute | solution.py:90
  2.3 2.6 %collective-permute-start.1 = (f32[1,8,16,128]{3,2,1,0:T(8,128)}, f32[1,8,16,128]{3,2,1,0:T(8,128)S(1)}, u32[]{:S(2)}, u32[]{:S(2)}) collective-permute-start(f32[1,8,16,128]{3,2,1,0:T(8,128)} %bitcast.44), channel_id=1, source_target_pairs={{0,16},{8,24},{16,0},{24,8},{1,17},{9,25},{17,1},{25,9},{2,18},{10... | collective-permute-start | bytes 196616 | tf_op jit(solution)/shard_map/ppermute | solution.py:90
  4.9 0.2 collective-permute-start.2
  5.1 0.8 copy.21
  5.8 0.7 broadcast_multiply_fusion
  6.5 0.8 convert_reduce_fusion.1
  7.3 0.8 convert_reduce_fusion
  8.2 0.7 convert_element_type.20
  8.8 0.1 pad.16.clone
  8.9 1.1 multiply_add_fusion.table
  10.0 0.8 maximum_maximum_fusion.own
  10.8 0.1 pad_add_fusion.1.meta
  10.8 0.0 collective-permute-done
  10.8 0.0 collective-permute-done.1
  10.8 0.3 collective-permute-done.2
  11.2 0.8 copy-done
  12.0 0.8 copy-done.3
  12.8 1.1 charge.1
  13.9 0.0 collective-permute-start.3
  13.9 1.2 %collective-permute-done.3 = f32[1,16,8,128]{3,2,1,0:T(8,128)S(1)} collective-permute-done((f32[1,16,8,128]{3,2,1,0:T(8,128)S(1)}, f32[1,16,8,128]{3,2,1,0:T(8,128)S(1)}, u32[]{:S(2)}, u32[]{:S(2)}) %collective-permute-start.3) | collective-permute-done | bytes 65568 | tf_op jit(solution)/shard_map/ppermute | solution.py:90
  15.2 1.6 %collective-permute-start.4 = (f32[2,16,8,128]{3,2,1,0:T(8,128)S(1)}, f32[2,16,8,128]{3,2,1,0:T(8,128)S(1)}, u32[]{:S(2)}, u32[]{:S(2)}) collective-permute-start(f32[2,16,8,128]{3,2,1,0:T(8,128)S(1)} %pad_maximum_fusion.1.refs_0_), channel_id=1, source_target_pairs={{0,2},{1,3},{2,0},{3,1},{4,6},{5,7},{6,4},{7,5},{8,10},{9,11},{10,... | collective-permute-start | bytes 393224 | tf_op jit(solution)/shard_map/ppermute | solution.py:90
  16.7 0.5 collective-permute-start.5
  17.2 1.5 %collective-permute-start.6 = (f32[2,16,8,128]{3,2,1,0:T(8,128)S(1)}, f32[2,16,8,128]{3,2,1,0:T(8,128)S(1)}, u32[]{:S(2)}, u32[]{:S(2)}) collective-permute-start(f32[2,16,8,128]{3,2,1,0:T(8,128)S(1)} %pad_maximum_fusion.1.refs_0_), channel_id=1, source_target_pairs={{0,6},{1,7},{2,4},{3,5},{4,2},{5,3},{6,0},{7,1},{8,14},{9,15},{10,... | collective-permute-start | bytes 393224 | tf_op jit(solution)/shard_map/ppermute | solution.py:90
  18.7 0.1 copy.19.counts
  18.8 0.9 pad_maximum_fusion.mine
  19.7 1.5 %collective-permute-done.4.refs_1_ = f32[2,16,8,128]{3,2,1,0:T(8,128)S(1)} collective-permute-done((f32[2,16,8,128]{3,2,1,0:T(8,128)S(1)}, f32[2,16,8,128]{3,2,1,0:T(8,128)S(1)}, u32[]{:S(2)}, u32[]{:S(2)}) %collective-permute-start.4) | collective-permute-done | bytes 131104 | tf_op jit(solution)/shard_map/ppermute | solution.py:90
  21.1 3.7 %collective-permute-done.5.refs_2_ = f32[2,16,8,128]{3,2,1,0:T(8,128)S(1)} collective-permute-done((f32[2,16,8,128]{3,2,1,0:T(8,128)S(1)}, f32[2,16,8,128]{3,2,1,0:T(8,128)S(1)}, u32[]{:S(2)}, u32[]{:S(2)}) %collective-permute-start.5) | collective-permute-done | bytes 131104 | tf_op jit(solution)/shard_map/ppermute | solution.py:90
  24.8 0.0 collective-permute-done.6.refs_3_
  24.8 0.8 copy-done.1
  25.6 0.7 copy-done.4
  26.3 0.7 copy-done.6
  27.0 8.9 %hartree.1 = (f32[5,8,128]{2,1,0:T(8,128)S(1)}, f32[48,8,128]{2,1,0:T(8,128)S(1)}, f32[4,48,8,128]{3,2,1,0:T(8,128)S(1)}) custom-call(s32[2]{0:T(128)S(1)} %pad_add_fusion.1.meta, s32[16,2]{1,0:T(8,128)S(1)} %copy.19.counts, s32[16,27]{1,0:T(8,128)S(1)} %copy-done.6, s32[16,42]{1,0:T(8,128)S(1)} %copy-done.4, f32[12,8,128]{2,1,0:T(8,128)S(1)} %copy-done.1, ...), custom_call_target="tpu_custom_call" | custom-call | tf_op jit(solution)/shard_map/hartree/pallas_call | solution.py:473
  35.9 0.3 collective-permute-start.7
  36.2 3.6 %collective-permute-start.8 = (f32[1,5,8,128]{3,2,1,0:T(8,128)S(1)}, f32[1,5,8,128]{3,2,1,0:T(8,128)S(1)}, u32[]{:S(2)}, u32[]{:S(2)}) collective-permute-start(f32[1,5,8,128]{3,2,1,0:T(8,128)S(1)} %bitcast.54), channel_id=1, source_target_pairs={{0,16},{8,24},{16,0},{24,8},{1,17},{9,25},{17,1},{25,9},{2,18},{10... | collective-permute-start | bytes 61448 | tf_op jit(solution)/shard_map/ppermute | solution.py:90
  39.8 0.6 collective-permute-start.9
  40.4 1.9 %collective-permute-start.10 = (f32[512,128]{1,0:T(8,128)S(1)}, f32[512,128]{1,0:T(8,128)S(1)}, u32[]{:S(2)}, u32[]{:S(2)}) collective-permute-start(f32[512,128]{1,0:T(8,128)S(1)} %pad_maximum_fusion.mine), channel_id=1, source_target_pairs={{0,1},{1,2},{2,3},{3,4},{4,5},{5,6},{6,7},{8,9},{9,10},{10,11},{11... | collective-permute-start | bytes 786440 | tf_op jit(solution)/shard_map/ppermute | solution.py:553
  42.3 4.5 %collective-permute-start.11 = (f32[512,128]{1,0:T(8,128)S(1)}, f32[512,128]{1,0:T(8,128)S(1)}, u32[]{:S(2)}, u32[]{:S(2)}) collective-permute-start(f32[512,128]{1,0:T(8,128)S(1)} %pad_maximum_fusion.mine), channel_id=1, source_target_pairs={{1,0},{2,1},{3,2},{4,3},{5,4},{6,5},{7,6},{9,8},{10,9},{11,10},{12... | collective-permute-start | bytes 786440 | tf_op jit(solution)/shard_map/ppermute | solution.py:553
  46.8 4.9 %pairs.1 = (f32[4,48,128,128]{3,2,1,0:T(8,128)S(1)}, f32[4,48,128,128]{3,2,1,0:T(8,128)S(1)}) custom-call(s32[2]{0:T(128)S(1)} %pad_add_fusion.1.meta, s32[16,2]{1,0:T(8,128)S(1)} %copy.19.counts, f32[48,8,128]{2,1,0:T(8,128)S(1)} %get-tuple-element.13.pts, f32[4,48,8,128]{3,2,1,0:T(8,128)S(1)} %get-tuple-element.15.src), custom_call_target="tpu_custom_call" | custom-call | tf_op jit(solution)/shard_map/pairs/pallas_call | solution.py:473
  51.7 0.0 collective-permute-done.9
  51.7 0.0 collective-permute-done.8
  51.8 0.0 collective-permute-done.7
  51.8 1.2 %combine.1 = (f32[16,128]{1,0:T(8,128)}, f32[32,128]{1,0:T(8,128)S(1)}) custom-call(s32[2]{0:T(128)S(1)} %pad_add_fusion.1.meta, f32[5,8,128]{2,1,0:T(8,128)S(1)} %get-tuple-element.12.refs_0_, f32[5,8,128]{2,1,0:T(8,128)S(1)} %bitcast.56, f32[5,8,128]{2,1,0:T(8,128)S(1)} %bitcast.59, f32[5,8,128]{2,1,0:T(8,128)S(1)} %bitcast.61), custom_call_target="tpu_custom_call" | custom-call | tf_op jit(solution)/shard_map/combine/pallas_call | solution.py:473
  52.9 0.0 collective-permute-start.12
  52.9 1.2 %collective-permute-done.12 = f32[1,32,128]{2,1,0:T(8,128)S(1)} collective-permute-done((f32[1,32,128]{2,1,0:T(8,128)S(1)}, f32[1,32,128]{2,1,0:T(8,128)S(1)}, u32[]{:S(2)}, u32[]{:S(2)}) %collective-permute-start.12) | collective-permute-done | bytes 16416 | tf_op jit(solution)/shard_map/ppermute | solution.py:90
  54.1 0.0 collective-permute-start.13
  54.1 0.6 collective-permute-start.14
  54.7 2.9 %collective-permute-start.15 = (f32[2,32,128]{2,1,0:T(8,128)S(1)}, f32[2,32,128]{2,1,0:T(8,128)S(1)}, u32[]{:S(2)}, u32[]{:S(2)}) collective-permute-start(f32[2,32,128]{2,1,0:T(8,128)S(1)} %pad_maximum_fusion.2.refs_0_), channel_id=1, source_target_pairs={{0,6},{1,7},{2,4},{3,5},{4,2},{5,3},{6,0},{7,1},{8,14},{9,15},{10,... | collective-permute-start | bytes 98312 | tf_op jit(solution)/shard_map/ppermute | solution.py:90
  57.6 0.1 maximum_convert_fusion.levels
  57.7 0.3 collective-permute-done.13.refs_1_
  58.0 0.0 collective-permute-done.14.refs_2_
  58.0 1.5 %collective-permute-done.15.refs_3_ = f32[2,32,128]{2,1,0:T(8,128)S(1)} collective-permute-done((f32[2,32,128]{2,1,0:T(8,128)S(1)}, f32[2,32,128]{2,1,0:T(8,128)S(1)}, u32[]{:S(2)}, u32[]{:S(2)}) %collective-permute-start.15) | collective-permute-done | bytes 32800 | tf_op jit(solution)/shard_map/ppermute | solution.py:90
  59.6 0.0 collective-permute-done.10.before
  59.6 0.8 copy-done.2
  60.4 0.7 copy-done.5
  61.1 0.7 copy-done.7
  61.8 0.7 copy-done.8
  62.4 41.6 %orbitals.1 = f32[4,4,8,128]{3,2,1,0:T(8,128)S(1)} custom-call(s32[2]{0:T(128)S(1)} %pad_add_fusion.1.meta, s32[16,2]{1,0:T(8,128)S(1)} %copy.19.counts, s32[16,27]{1,0:T(8,128)S(1)} %copy-done.7, s32[16,42]{1,0:T(8,128)S(1)} %copy-done.5, s32[32]{0:T(128)S(1)} %maximum_convert_fusion.levels, f32[32]{0:T(128)S(1)} %copy-done.8, f32[12,8,128]{2,1,0:T(8,128)S(1)} %copy-done.2, ...), custom_call_target="tpu_custom_call" | custom-call | tf_op jit(solution)/shard_map/orbitals/pallas_call | solution.py:473
  104.0 0.1 collective-permute-start.16
  104.1 4.0 %collective-permute-start.17 = (f32[4,8,128]{2,1,0:T(8,128)S(1)}, f32[4,8,128]{2,1,0:T(8,128)S(1)}, u32[]{:S(2)}, u32[]{:S(2)}) collective-permute-start(f32[4,8,128]{2,1,0:T(8,128)S(1)} %get-tuple-element.21), channel_id=1, source_target_pairs={{0,16},{8,24},{16,0},{24,8},{1,17},{9,25},{17,1},{25,9},{2,18},{10... | collective-permute-start | bytes 49160 | tf_op jit(solution)/shard_map/ppermute | solution.py:586
  108.1 0.4 collective-permute-start.18
  108.5 0.0 collective-permute-done.16.refs_1_
  108.5 1.4 %collective-permute-done.17.refs_2_ = f32[4,8,128]{2,1,0:T(8,128)S(1)} collective-permute-done((f32[4,8,128]{2,1,0:T(8,128)S(1)}, f32[4,8,128]{2,1,0:T(8,128)S(1)}, u32[]{:S(2)}, u32[]{:S(2)}) %collective-permute-start.17) | collective-permute-done | bytes 16416 | tf_op jit(solution)/shard_map/ppermute | solution.py:586
  109.8 3.8 %collective-permute-done.18.refs_3_ = f32[4,8,128]{2,1,0:T(8,128)S(1)} collective-permute-done((f32[4,8,128]{2,1,0:T(8,128)S(1)}, f32[4,8,128]{2,1,0:T(8,128)S(1)}, u32[]{:S(2)}, u32[]{:S(2)}) %collective-permute-start.18) | collective-permute-done | bytes 16416 | tf_op jit(solution)/shard_map/ppermute | solution.py:586
  113.7 1.2 %place.1 = f32[8,16,128]{2,1,0:T(8,128)} custom-call(s32[2]{0:T(128)S(1)} %pad_add_fusion.1.meta, f32[4,8,128]{2,1,0:T(8,128)S(1)} %get-tuple-element.23.refs_0_, f32[4,8,128]{2,1,0:T(8,128)S(1)} %collective-permute-done.16.refs_1_, f32[4,8,128]{2,1,0:T(8,128)S(1)} %collective-permute-done.17.refs_2_, f32[4,8,128]{2,1,0:T(8,128)S(1)} %collective-permute-done.18.refs_3_), custom_call_target="tpu_custom_call" | custom-call | tf_op jit(solution)/shard_map/place/pallas_call | solution.py:473
  (20 shorter events, 0.1 us)
Async XLA Ops:
  0.6 10.2 %collective-permute-start = (f32[1,8,16,128]{3,2,1,0:T(8,128)}, f32[1,8,16,128]{3,2,1,0:T(8,128)S(1)}, u32[]{:S(2)}, u32[]{:S(2)}) collective-permute-start(f32[1,8,16,128]{3,2,1,0:T(8,128)} %bitcast.43), channel_id=1, source_target_pairs={{0,8},{8,0},{16,24},{24,16},{1,9},{9,1},{17,25},{25,17},{2,10},{10... | collective-permute-start | bytes 196616 | tf_op jit(solution)/shard_map/ppermute | solution.py:90
  2.3 8.6 %collective-permute-start.1 = (f32[1,8,16,128]{3,2,1,0:T(8,128)}, f32[1,8,16,128]{3,2,1,0:T(8,128)S(1)}, u32[]{:S(2)}, u32[]{:S(2)}) collective-permute-start(f32[1,8,16,128]{3,2,1,0:T(8,128)} %bitcast.44), channel_id=1, source_target_pairs={{0,16},{8,24},{16,0},{24,8},{1,17},{9,25},{17,1},{25,9},{2,18},{10... | collective-permute-start | bytes 196616 | tf_op jit(solution)/shard_map/ppermute | solution.py:90
  4.9 6.3 %collective-permute-start.2 = (f32[1,8,16,128]{3,2,1,0:T(8,128)}, f32[1,8,16,128]{3,2,1,0:T(8,128)S(1)}, u32[]{:S(2)}, u32[]{:S(2)}) collective-permute-start(f32[1,8,16,128]{3,2,1,0:T(8,128)} %bitcast.45), channel_id=1, source_target_pairs={{0,24},{8,16},{16,8},{24,0},{1,25},{9,17},{17,9},{25,1},{2,26},{10... | collective-permute-start | bytes 196616 | tf_op jit(solution)/shard_map/ppermute | solution.py:90
  11.2 0.8 copy-start
  12.0 0.8 copy-start.3
  13.9 1.3 %collective-permute-start.3 = (f32[1,16,8,128]{3,2,1,0:T(8,128)S(1)}, f32[1,16,8,128]{3,2,1,0:T(8,128)S(1)}, u32[]{:S(2)}, u32[]{:S(2)}) collective-permute-start(f32[1,16,8,128]{3,2,1,0:T(8,128)S(1)} %bitcast.41), channel_id=1, source_target_pairs={{0,1},{1,0},{2,3},{3,2},{4,5},{5,4},{6,7},{7,6},{8,9},{9,8},{10,11... | collective-permute-start | bytes 196616 | tf_op jit(solution)/shard_map/ppermute | solution.py:90
  15.2 6.0 %collective-permute-start.4 = (f32[2,16,8,128]{3,2,1,0:T(8,128)S(1)}, f32[2,16,8,128]{3,2,1,0:T(8,128)S(1)}, u32[]{:S(2)}, u32[]{:S(2)}) collective-permute-start(f32[2,16,8,128]{3,2,1,0:T(8,128)S(1)} %pad_maximum_fusion.1.refs_0_), channel_id=1, source_target_pairs={{0,2},{1,3},{2,0},{3,1},{4,6},{5,7},{6,4},{7,5},{8,10},{9,11},{10,... | collective-permute-start | bytes 393224 | tf_op jit(solution)/shard_map/ppermute | solution.py:90
  16.7 8.1 %collective-permute-start.5 = (f32[2,16,8,128]{3,2,1,0:T(8,128)S(1)}, f32[2,16,8,128]{3,2,1,0:T(8,128)S(1)}, u32[]{:S(2)}, u32[]{:S(2)}) collective-permute-start(f32[2,16,8,128]{3,2,1,0:T(8,128)S(1)} %pad_maximum_fusion.1.refs_0_), channel_id=1, source_target_pairs={{0,4},{1,5},{2,6},{3,7},{4,0},{5,1},{6,2},{7,3},{8,12},{9,13},{10,... | collective-permute-start | bytes 393224 | tf_op jit(solution)/shard_map/ppermute | solution.py:90
  17.2 7.6 %collective-permute-start.6 = (f32[2,16,8,128]{3,2,1,0:T(8,128)S(1)}, f32[2,16,8,128]{3,2,1,0:T(8,128)S(1)}, u32[]{:S(2)}, u32[]{:S(2)}) collective-permute-start(f32[2,16,8,128]{3,2,1,0:T(8,128)S(1)} %pad_maximum_fusion.1.refs_0_), channel_id=1, source_target_pairs={{0,6},{1,7},{2,4},{3,5},{4,2},{5,3},{6,0},{7,1},{8,14},{9,15},{10,... | collective-permute-start | bytes 393224 | tf_op jit(solution)/shard_map/ppermute | solution.py:90
  24.8 0.8 copy-start.1
  25.6 0.7 copy-start.4
  26.3 0.7 copy-start.6
  35.9 15.8 %collective-permute-start.7 = (f32[1,5,8,128]{3,2,1,0:T(8,128)S(1)}, f32[1,5,8,128]{3,2,1,0:T(8,128)S(1)}, u32[]{:S(2)}, u32[]{:S(2)}) collective-permute-start(f32[1,5,8,128]{3,2,1,0:T(8,128)S(1)} %bitcast.53), channel_id=1, source_target_pairs={{0,8},{8,0},{16,24},{24,16},{1,9},{9,1},{17,25},{25,17},{2,10},{10... | collective-permute-start | bytes 61448 | tf_op jit(solution)/shard_map/ppermute | solution.py:90
  36.2 15.5 %collective-permute-start.8 = (f32[1,5,8,128]{3,2,1,0:T(8,128)S(1)}, f32[1,5,8,128]{3,2,1,0:T(8,128)S(1)}, u32[]{:S(2)}, u32[]{:S(2)}) collective-permute-start(f32[1,5,8,128]{3,2,1,0:T(8,128)S(1)} %bitcast.54), channel_id=1, source_target_pairs={{0,16},{8,24},{16,0},{24,8},{1,17},{9,25},{17,1},{25,9},{2,18},{10... | collective-permute-start | bytes 61448 | tf_op jit(solution)/shard_map/ppermute | solution.py:90
  39.8 11.9 %collective-permute-start.9 = (f32[1,5,8,128]{3,2,1,0:T(8,128)S(1)}, f32[1,5,8,128]{3,2,1,0:T(8,128)S(1)}, u32[]{:S(2)}, u32[]{:S(2)}) collective-permute-start(f32[1,5,8,128]{3,2,1,0:T(8,128)S(1)} %bitcast.55), channel_id=1, source_target_pairs={{0,24},{8,16},{16,8},{24,0},{1,25},{9,17},{17,9},{25,1},{2,26},{10... | collective-permute-start | bytes 61448 | tf_op jit(solution)/shard_map/ppermute | solution.py:90
  40.4 19.2 %collective-permute-start.10 = (f32[512,128]{1,0:T(8,128)S(1)}, f32[512,128]{1,0:T(8,128)S(1)}, u32[]{:S(2)}, u32[]{:S(2)}) collective-permute-start(f32[512,128]{1,0:T(8,128)S(1)} %pad_maximum_fusion.mine), channel_id=1, source_target_pairs={{0,1},{1,2},{2,3},{3,4},{4,5},{5,6},{6,7},{8,9},{9,10},{10,11},{11... | collective-permute-start | bytes 786440 | tf_op jit(solution)/shard_map/ppermute | solution.py:553
  42.3 17.3 %collective-permute-start.11 = (f32[512,128]{1,0:T(8,128)S(1)}, f32[512,128]{1,0:T(8,128)S(1)}, u32[]{:S(2)}, u32[]{:S(2)}) collective-permute-start(f32[512,128]{1,0:T(8,128)S(1)} %pad_maximum_fusion.mine), channel_id=1, source_target_pairs={{1,0},{2,1},{3,2},{4,3},{5,4},{6,5},{7,6},{9,8},{10,9},{11,10},{12... | collective-permute-start | bytes 786440 | tf_op jit(solution)/shard_map/ppermute | solution.py:553
  52.9 1.2 %collective-permute-start.12 = (f32[1,32,128]{2,1,0:T(8,128)S(1)}, f32[1,32,128]{2,1,0:T(8,128)S(1)}, u32[]{:S(2)}, u32[]{:S(2)}) collective-permute-start(f32[1,32,128]{2,1,0:T(8,128)S(1)} %bitcast.62), channel_id=1, source_target_pairs={{0,1},{1,0},{2,3},{3,2},{4,5},{5,4},{6,7},{7,6},{8,9},{9,8},{10,11... | collective-permute-start | bytes 49160 | tf_op jit(solution)/shard_map/ppermute | solution.py:90
  54.1 3.9 %collective-permute-start.13 = (f32[2,32,128]{2,1,0:T(8,128)S(1)}, f32[2,32,128]{2,1,0:T(8,128)S(1)}, u32[]{:S(2)}, u32[]{:S(2)}) collective-permute-start(f32[2,32,128]{2,1,0:T(8,128)S(1)} %pad_maximum_fusion.2.refs_0_), channel_id=1, source_target_pairs={{0,2},{1,3},{2,0},{3,1},{4,6},{5,7},{6,4},{7,5},{8,10},{9,11},{10,... | collective-permute-start | bytes 98312 | tf_op jit(solution)/shard_map/ppermute | solution.py:90
  54.1 3.9 %collective-permute-start.14 = (f32[2,32,128]{2,1,0:T(8,128)S(1)}, f32[2,32,128]{2,1,0:T(8,128)S(1)}, u32[]{:S(2)}, u32[]{:S(2)}) collective-permute-start(f32[2,32,128]{2,1,0:T(8,128)S(1)} %pad_maximum_fusion.2.refs_0_), channel_id=1, source_target_pairs={{0,4},{1,5},{2,6},{3,7},{4,0},{5,1},{6,2},{7,3},{8,12},{9,13},{10,... | collective-permute-start | bytes 98312 | tf_op jit(solution)/shard_map/ppermute | solution.py:90
  54.7 4.8 %collective-permute-start.15 = (f32[2,32,128]{2,1,0:T(8,128)S(1)}, f32[2,32,128]{2,1,0:T(8,128)S(1)}, u32[]{:S(2)}, u32[]{:S(2)}) collective-permute-start(f32[2,32,128]{2,1,0:T(8,128)S(1)} %pad_maximum_fusion.2.refs_0_), channel_id=1, source_target_pairs={{0,6},{1,7},{2,4},{3,5},{4,2},{5,3},{6,0},{7,1},{8,14},{9,15},{10,... | collective-permute-start | bytes 98312 | tf_op jit(solution)/shard_map/ppermute | solution.py:90
  59.6 0.8 copy-start.2
  60.4 0.7 copy-start.5
  61.1 0.7 copy-start.7
  61.8 0.7 copy-start.8
  104.0 4.5 %collective-permute-start.16 = (f32[4,8,128]{2,1,0:T(8,128)S(1)}, f32[4,8,128]{2,1,0:T(8,128)S(1)}, u32[]{:S(2)}, u32[]{:S(2)}) collective-permute-start(f32[4,8,128]{2,1,0:T(8,128)S(1)} %get-tuple-element.22), channel_id=1, source_target_pairs={{0,8},{8,0},{16,24},{24,16},{1,9},{9,1},{17,25},{25,17},{2,10},{10... | collective-permute-start | bytes 49160 | tf_op jit(solution)/shard_map/ppermute | solution.py:586
  104.1 5.7 %collective-permute-start.17 = (f32[4,8,128]{2,1,0:T(8,128)S(1)}, f32[4,8,128]{2,1,0:T(8,128)S(1)}, u32[]{:S(2)}, u32[]{:S(2)}) collective-permute-start(f32[4,8,128]{2,1,0:T(8,128)S(1)} %get-tuple-element.21), channel_id=1, source_target_pairs={{0,16},{8,24},{16,0},{24,8},{1,17},{9,25},{17,1},{25,9},{2,18},{10... | collective-permute-start | bytes 49160 | tf_op jit(solution)/shard_map/ppermute | solution.py:586
  108.1 5.5 %collective-permute-start.18 = (f32[4,8,128]{2,1,0:T(8,128)S(1)}, f32[4,8,128]{2,1,0:T(8,128)S(1)}, u32[]{:S(2)}, u32[]{:S(2)}) collective-permute-start(f32[4,8,128]{2,1,0:T(8,128)S(1)} %get-tuple-element.20), channel_id=1, source_target_pairs={{0,24},{8,16},{16,8},{24,0},{1,25},{9,17},{17,9},{25,1},{2,26},{10... | collective-permute-start | bytes 49160 | tf_op jit(solution)/shard_map/ppermute | solution.py:586

commit v5 on v4

--- a/solution.py
+++ b/solution.py
@@ -27,13 +27,16 @@
 
 
 def basis_rows():
-    row = np.arange(ROWS)
+    row = lax.broadcasted_iota(jnp.int32, (ROWS, LANES), 0)
     out = []
     for pick in (row // 4, 2 + row // 4, row % 4):
-        for k in range(NODES - 1):
-            out.append([roots[a][k] for a in pick])
-        out.append([scales[a] for a in pick])
-    return np.broadcast_to(np.array(out, np.float32)[:, :, None], (12, ROWS, LANES)).copy()
+        for k in range(NODES):
+            values = [float(scales[a] if k == NODES - 1 else roots[a][k]) for a in range(NODES)]
+            made = jnp.full((ROWS, LANES), values[0], jnp.float32)
+            for a in range(1, NODES):
+                made = jnp.where(pick == a, values[a], made)
+            out.append(made)
+    return out
 
 
 def proxy_table(planes, window):
@@ -80,7 +83,7 @@
     return lax.dot_general(a, b, (((1,), (1,)), ((), ())), precision=highest, preferred_element_type=jnp.float32)
 
 
-def gather_parts(block, axis, pairs):
+def gather_parts(block, axis, pairs, later=None):
     count = lax.axis_size(axis)
     parts = [block[None]]
     while sum(p.shape[0] for p in parts) < count:
@@ -88,11 +91,13 @@
         have = held.shape[0]
         steps = range(1, 4 if (have > 1 or pairs) and have * 4 <= count else 2)
         parts = [held] + [lax.ppermute(held, axis, [(i, i ^ (have * j)) for i in range(count)]) for j in steps]
-    return parts
+        if later is not None and have == 1:
+            parts[1], later = lax.optimization_barrier((parts[1], later))
+    return parts, later
 
 
 def gather_list(block, axis):
-    parts = gather_parts(block, axis, True)
+    parts, _ = gather_parts(block, axis, True)
     return [p[k] for p in parts for k in range(p.shape[0])]
 
 
@@ -131,10 +136,11 @@
     return dot_bf16(ones, jnp.concatenate([high, low], axis=1))[0:1, :]
 
 
-def charge_kernel(meta, cst, own, *refs):
+def charge_kernel(meta, own, partial, *refs):
     z_low = meta[0].astype(jnp.float32) * cell_side
     fields, (out, density) = refs[:-2], refs[-2:]
-    total = jnp.zeros((PLANE, LANES), jnp.float32)
+    cst = basis_rows()
+    total = partial[...]
     for phi in fields:
         for j in range(phi.shape[0]):
             v = phi[j]
@@ -160,16 +166,21 @@
     return below, below + jnp.maximum(planes - 2 - me, 0)
 
 
-def list_blocks(me, cell, counts, near, far, planes, put_near, put_far, put_none, multiple):
+def list_lengths(lists, cell, slots):
+    return lists[cell, sum(slots)], lists[cell, sum(slots) + 1]
+
+
+def list_blocks(me, cell, lists, slots, planes, put_near, put_far, put_none, multiple):
     window = 3 * PLANE
     base = (me - 1) * PLANE
     below, n_planes = live_planes(me, planes)
-    n_near, n_far = counts[cell, 0], counts[cell, 1]
+    near_slots, far_slots = slots
+    n_near, n_far = list_lengths(lists, cell, slots)
     n_items = n_far + n_planes
     n_pairs = (n_items + 1) // 2
 
     def near_step(j, c):
-        put_near(j, near[cell, j] - base)
+        put_near(j, lists[cell, j] - base)
         return c
 
     lax.fori_loop(0, n_near, near_step, 0)
@@ -178,7 +189,7 @@
         j = jnp.minimum(j, n_items - 1)
         p = j - n_far
         level = jnp.where(p < below, p, p + (me + 2 - below))
-        slot = far[cell, jnp.minimum(j, far.shape[1] - 1)] - base
+        slot = lists[cell, near_slots + jnp.minimum(j, far_slots - 1)] - base
         return jnp.where(j < n_far, slot, window + level)
 
     def far_step(j, c):
@@ -214,13 +225,14 @@
     return jnp.concatenate([message[pl.ds(g * rows + c, kinds, stride=PLANE), :] for g in range(groups)], axis=0)
 
 
-def hartree_kernel(groups, kinds, unroll, meta, counts, near, far, cst, table, marks, mine, *refs):
+def hartree_kernel(groups, kinds, unroll, slots, meta, lists, table, marks, mine, *refs):
     parts, (out, pts, src, every, items, tgt) = refs[:-6], refs[-6:]
     lay_out(parts, every)
     planes = every.shape[0]
     cells = PLANE // groups
     me, group = meta[0], meta[1]
     window = 3 * PLANE
+    cst = basis_rows()
     for k in range(3):
         there = lax.bitwise_xor(me, jnp.clip(me - 1 + k, 0, planes - 1))
         for c in range(PLANE):
@@ -255,7 +267,7 @@
         def put_none(j):
             src[t, j] = jnp.zeros((ROWS, LANES), jnp.float32)
 
-        n_blocks = list_blocks(me, cell, counts, near, far, planes, put_near, put_far, put_none, unroll)
+        n_blocks = list_blocks(me, cell, lists, slots, planes, put_near, put_far, put_none, unroll)
         put_targets(pts, cell, tgt)
 
         def step(i, accs):
@@ -281,14 +293,15 @@
         out[1 + lax.bitwise_xor(group, k), :kinds, :] = total[k * kinds : (k + 1) * kinds, :]
 
 
-def pairs_kernel(groups, planes, unroll, meta, counts, pts, src, dist, inv, tgt):
+def pairs_kernel(groups, planes, unroll, slots, meta, lists, pts, src, dist, inv, tgt):
     group = meta[1]
     _, n_planes = live_planes(meta[0], planes)
 
     def per_cell(t, carry):
         cell = target_cell(group, t, groups)
         put_targets(pts, cell, tgt)
-        n_blocks = counts[cell, 0] + (counts[cell, 1] + n_planes + 1) // 2
+        n_near, n_far = list_lengths(lists, cell, slots)
+        n_blocks = n_near + (n_far + n_planes + 1) // 2
 
         def measure(i, x):
             def use(r, u, sq):
@@ -324,7 +337,7 @@
 
 
 def orbital_kernel(
-    planes, batch, unit, steps, meta, counts, near, far, levels, screening, cst,
+    planes, batch, unit, steps, slots, meta, lists, levels, rates_of,
     pts, before, mine, after, dist, inv, *refs,
 ):
     parts, (out, rate, slot_of, every, val, mom, srcv, acc) = refs[:-8], refs[-8:]
@@ -338,9 +351,9 @@
         rate[i] = 0.0
         return c
 
-    lax.fori_loop(0, screening.shape[0], clear, 0)
+    lax.fori_loop(0, rates_of.shape[0], clear, 0)
     for q in range(2 * batch):
-        rate[screening.shape[0] + q] = 0.0
+        rate[rates_of.shape[0] + q] = 0.0
     lane = lax.broadcasted_iota(jnp.int32, (1, LANES), 1) % orbs
 
     def rank(i, carry):
@@ -349,12 +362,13 @@
         known = slot_of[level]
         slot = jnp.where(known < 0, found, known)
         slot_of[level] = slot
-        rate[slot] = screening[level] * (-log2e)
+        rate[slot] = rates_of[level]
         return found + (known < 0).astype(jnp.int32), jnp.where(lane == i, slot, lane_slot)
 
     n_levels, lane_slot = lax.fori_loop(0, orbs, rank, (jnp.int32(0), jnp.zeros((1, LANES), jnp.int32)))
     n_batches = (n_levels + batch - 1) // batch
     first_half = lax.broadcasted_iota(jnp.int32, (1, 2 * orbs), 1) < orbs
+    cst = basis_rows()
 
     def flip(v):
         high = v.astype(jnp.bfloat16).astype(jnp.float32)
@@ -417,7 +431,7 @@
 
     def per_cell(t, carry):
         cell = target_cell(group, t, groups)
-        n_blocks = list_blocks(me, cell, counts, near, far, planes, put_near, put_far, put_none, unit)
+        n_blocks = list_blocks(me, cell, lists, slots, planes, put_near, put_far, put_none, unit)
         n_units = (n_blocks + unit - 1) // unit
 
         def clear_acc(b, x):
@@ -500,39 +514,49 @@
     ends = planes - 1
     up = [(i, i + 1) for i in range(ends)]
     down = [(i + 1, i) for i in range(ends)]
-    cst = jnp.asarray(basis_rows())
     base_table = proxy_table(planes, window)
     shift = np.zeros(base_table.shape, np.float32)
     shift[:window, 2] = cell_side
     table = jnp.asarray(base_table) + jnp.asarray(shift) * (me - 1).astype(f32)
-    counts = jnp.stack(
-        [jnp.sum((near_cells >= 0).astype(jnp.int32), 1), jnp.sum((far_cells >= 0).astype(jnp.int32), 1)], axis=1
-    )
+    slots = (near_cells.shape[1], far_cells.shape[1])
+    lists = jnp.concatenate(
+        [
+            near_cells,
+            far_cells,
+            jnp.sum((near_cells >= 0).astype(jnp.int32), axis=1, keepdims=True),
+            jnp.sum((far_cells >= 0).astype(jnp.int32), axis=1, keepdims=True),
+        ],
+        axis=1,
+    )
+    rates_of = screening * (-log2e)
+    partial = jnp.sum(orbitals * orbitals, axis=0)
+
     charges = call(
         charge_kernel,
         "charge",
         jax.ShapeDtypeStruct((cells, ROWS, LANES), f32),
         1,
-        (meta, cst, own, *fields),
+        (meta, own, partial, *fields[1:]),
         [pltpu.VMEM((cells, LANES), f32)],
     )
-    charges = gather_parts(charges, "space", False)
     mine = jnp.concatenate([f.reshape(kinds * cells, LANES) for f in fields], axis=0)
+    charges, mine = gather_parts(charges, "space", False, mine)
+    before, after = lax.ppermute(mine, "space", up), lax.ppermute(mine, "space", down)
 
     batch, unit, steps = 4, 4, 9
     most = near_cells.shape[1]
     blocks = most + (window - most + planes + 1) // 2
     blocks = -(-blocks // unit) * unit + unit
     shares, pts, src = call(
-        functools.partial(hartree_kernel, groups, kinds, unit),
+        functools.partial(hartree_kernel, groups, kinds, unit, slots),
         "hartree",
         (
             jax.ShapeDtypeStruct((1 + groups, ROWS, LANES), f32),
             jax.ShapeDtypeStruct((window, ROWS, LANES), f32),
             jax.ShapeDtypeStruct((share, blocks, ROWS, LANES), f32),
         ),
-        4,
-        (meta, counts, near_cells, far_cells, cst, table, marks, mine, *charges),
+        2,
+        (meta, lists, table, marks, mine, *charges),
         [
             pltpu.VMEM((planes, cells, ROWS, LANES), f32),
             pltpu.VMEM((window + planes + 1, ROWS, LANES), f32),
@@ -541,16 +565,14 @@
         12,
     )
     dist, inv = call(
-        functools.partial(pairs_kernel, groups, planes, unit),
+        functools.partial(pairs_kernel, groups, planes, unit, slots),
         "pairs",
         (jax.ShapeDtypeStruct((share, blocks, LANES, LANES), f32),) * 2,
         2,
-        (meta, counts, pts, src),
+        (meta, lists, pts, src),
         [pltpu.VMEM((3, LANES, LANES), f32)],
         4,
     )
-    mine, shares = lax.optimization_barrier((mine, shares))
-    before, after = lax.ppermute(mine, "space", up), lax.ppermute(mine, "space", down)
     shares = gather_list(shares, "orb")
     levels = jnp.concatenate([share[0, ROWS - 1, :kinds] for share in shares]).astype(jnp.int32)
     hartree, combined = call(
@@ -561,15 +583,15 @@
         (meta, *shares),
         [pltpu.VMEM((orbs, LANES), f32)],
     )
-    gathered = gather_parts(combined, "space", False)
+    gathered, _ = gather_parts(combined, "space", False)
 
     levels_at_most = -(-screening.shape[0] // batch) + 1
     sent = call(
-        functools.partial(orbital_kernel, planes, batch, unit, steps),
+        functools.partial(orbital_kernel, planes, batch, unit, steps, slots),
         "orbitals",
         jax.ShapeDtypeStruct((groups, share, kinds, LANES), f32),
-        6,
-        (meta, counts, near_cells, far_cells, levels, screening, cst, pts, before, mine, after, dist, inv, *gathered),
+        4,
+        (meta, lists, levels, rates_of, pts, before, mine, after, dist, inv, *gathered),
         [
             pltpu.SMEM((screening.shape[0] + 2 * batch,), f32),
             pltpu.SMEM((screening.shape[0],), jnp.int32),

time: 117 us -> 116 us (level)
  Pallas kernels: 58.9 us -> 68.6 us
  local copies, waits for them, and re-layouts: 7.61 us -> 1.02 us
  waiting for transfers between devices: 15 us -> 8.68 us
  other arithmetic: 5.86 us -> 8.19 us
    pallas_call x6, Pallas kernels: 58.9 us -> 68.6 us  [call(): pl.pallas_call(kernel, out_shape=out_shape, in_specs=[smem()] * smems + [...]
    unnamed x19 -> x1, local copies, waits for them, and re-layouts: 7.43 us -> 0.75 us
    ppermute x14, waiting for transfers between devices: 9.78 us -> 3.96 us  [gather_parts(): lax.ppermute(held, axis, [(i, i ^ have * j) for i in range(count)])]
    reduce_sum x2 -> x3, other arithmetic: 1.62 us -> 2.51 us  [the longest x1 0.88 us: body(): partial = jnp.sum(orbitals * orbitals, axis=0)]
  transfers between devices with their start and end apart: 19 -> 19, of which waited for: 9 -> 7; matrix products, arithmetic and copies ran while one was open for 6% -> 8% of each run, Pallas kernels for 5% -> 13%
where the time goes in v5:
time: 116 us; the launch traced here: 114 us
  Pallas kernels  68.6 us (59%)
  starting transfers between devices  26.7 us (23%)
  waiting for transfers between devices  8.68 us (7%)
  other arithmetic  8.19 us (7%)
    pallas_call x6, Pallas kernels, call(): pl.pallas_call(kernel, out_shape=out_shape, in_specs=[smem()] * smems + [...  68.6 us
    ppermute x14, starting transfers between devices, gather_parts(): lax.ppermute(held, axis, [(i, i ^ have * j) for i in range(count)])  15.8 us
    ppermute x3, waiting for transfers between devices, body(): lax.ppermute(sent[k], 'orb', [(i, i ^ k) for i in range(groups)])  4.71 us
    ppermute x1, starting transfers between devices, body(): lax.ppermute(mine, 'space', down)  4.54 us
    ppermute x3, starting transfers between devices, body(): lax.ppermute(sent[k], 'orb', [(i, i ^ k) for i in range(groups)])  4.45 us
    ppermute x14, waiting for transfers between devices, gather_parts(): lax.ppermute(held, axis, [(i, i ^ have * j) for i in range(count)])  3.96 us
  transfers between devices with their start and end apart: 19, of which 7 were waited for; matrix products, arithmetic and copies ran while one was open for 8% of the time, Pallas kernels for 13%

profile of v5, /device:TPU:4, one launch (start us, length us, event | category | flops | bytes accessed | tf_op | source)
XLA Modules:
  0.0 114.0 jit_solution(15264296417207773726)
XLA Ops:
  0.6 2.7 %collective-permute-start.1 = (f32[1,8,16,128]{3,2,1,0:T(8,128)}, f32[1,8,16,128]{3,2,1,0:T(8,128)S(1)}, u32[]{:S(2)}, u32[]{:S(2)}) collective-permute-start(f32[1,8,16,128]{3,2,1,0:T(8,128)} %bitcast.60), channel_id=1, source_target_pairs={{0,16},{8,24},{16,0},{24,8},{1,17},{9,25},{17,1},{25,9},{2,18},{10... | collective-permute-start | bytes 196616 | tf_op jit(solution)/shard_map/ppermute | solution.py:93
  3.3 1.3 %collective-permute-start.2 = (f32[1,8,16,128]{3,2,1,0:T(8,128)}, f32[1,8,16,128]{3,2,1,0:T(8,128)S(1)}, u32[]{:S(2)}, u32[]{:S(2)}) collective-permute-start(f32[1,8,16,128]{3,2,1,0:T(8,128)} %bitcast.61), channel_id=1, source_target_pairs={{0,24},{8,16},{16,8},{24,0},{1,25},{9,17},{17,9},{25,1},{2,26},{10... | collective-permute-start | bytes 196616 | tf_op jit(solution)/shard_map/ppermute | solution.py:93
  4.6 0.2 collective-permute-start
  4.9 0.9 multiply_reduce_fusion.partial
  5.7 0.8 copy.16
  6.5 0.7 broadcast_multiply_fusion
  7.2 0.8 convert_reduce_fusion.1
  8.0 0.8 convert_reduce_fusion
  8.8 0.7 convert_element_type.20
  9.5 0.7 broadcast_multiply_fusion.1.rates_of
  10.1 0.1 pad.20.clone
  10.2 1.1 multiply_add_fusion.table
  11.3 0.8 maximum_maximum_fusion.own
  12.1 0.1 pad_add_fusion.1.meta
  12.2 0.0 collective-permute-done.1
  12.2 0.0 collective-permute-done.2
  12.2 0.0 collective-permute-done
  12.2 1.1 charge.1
  13.3 0.0 collective-permute-start.3
  13.3 0.9 pad_maximum_fusion.mine
  14.1 0.4 collective-permute-done.3
  14.5 1.6 %collective-permute-start.4 = (f32[2,16,8,128]{3,2,1,0:T(8,128)S(1)}, f32[2,16,8,128]{3,2,1,0:T(8,128)S(1)}, u32[]{:S(2)}, u32[]{:S(2)}) collective-permute-start(f32[2,16,8,128]{3,2,1,0:T(8,128)S(1)} %pad_maximum_fusion.1.refs_0_), channel_id=1, source_target_pairs={{0,2},{1,3},{2,0},{3,1},{4,6},{5,7},{6,4},{7,5},{8,10},{9,11},{10,... | collective-permute-start | bytes 393224 | tf_op jit(solution)/shard_map/ppermute | solution.py:93
  16.1 0.5 collective-permute-start.5
  16.6 1.5 %collective-permute-start.6 = (f32[2,16,8,128]{3,2,1,0:T(8,128)S(1)}, f32[2,16,8,128]{3,2,1,0:T(8,128)S(1)}, u32[]{:S(2)}, u32[]{:S(2)}) collective-permute-start(f32[2,16,8,128]{3,2,1,0:T(8,128)S(1)} %pad_maximum_fusion.1.refs_0_), channel_id=1, source_target_pairs={{0,6},{1,7},{2,4},{3,5},{4,2},{5,3},{6,0},{7,1},{8,14},{9,15},{10,... | collective-permute-start | bytes 393224 | tf_op jit(solution)/shard_map/ppermute | solution.py:93
  18.1 0.1 copy.12
  18.2 0.1 copy.13
  18.2 0.8 pad_add_fusion.lists
  19.0 1.9 %collective-permute-start.10 = (f32[512,128]{1,0:T(8,128)S(1)}, f32[512,128]{1,0:T(8,128)S(1)}, u32[]{:S(2)}, u32[]{:S(2)}) collective-permute-start(f32[512,128]{1,0:T(8,128)S(1)} %pad_maximum_fusion.mine), channel_id=1, source_target_pairs={{0,1},{1,2},{2,3},{3,4},{4,5},{5,6},{6,7},{8,9},{9,10},{10,11},{11... | collective-permute-start | bytes 786440 | tf_op jit(solution)/shard_map/ppermute | solution.py:544
  21.0 4.5 %collective-permute-start.11 = (f32[512,128]{1,0:T(8,128)S(1)}, f32[512,128]{1,0:T(8,128)S(1)}, u32[]{:S(2)}, u32[]{:S(2)}) collective-permute-start(f32[512,128]{1,0:T(8,128)S(1)} %pad_maximum_fusion.mine), channel_id=1, source_target_pairs={{1,0},{2,1},{3,2},{4,3},{5,4},{6,5},{7,6},{9,8},{10,9},{11,10},{12... | collective-permute-start | bytes 786440 | tf_op jit(solution)/shard_map/ppermute | solution.py:544
  25.5 0.0 collective-permute-done.4.refs_1_
  25.5 0.0 collective-permute-done.5.refs_2_
  25.5 0.0 collective-permute-done.6.refs_3_
  25.5 8.6 %hartree.1 = (f32[5,8,128]{2,1,0:T(8,128)S(1)}, f32[48,8,128]{2,1,0:T(8,128)S(1)}, f32[4,48,8,128]{3,2,1,0:T(8,128)S(1)}) custom-call(s32[2]{0:T(128)S(1)} %pad_add_fusion.1.meta, s32[16,71]{1,0:T(8,128)S(1)} %pad_add_fusion.lists, f32[56,8,128]{2,1,0:T(8,128)S(1)} %multiply_add_fusion.table, f32[1,128]{1,0:T(1,128)S(1)} %pad_bitcast_fusion.marks, ...), custom_call_target="tpu_custom_call" | custom-call | tf_op jit(solution)/shard_map/hartree/pallas_call | solution.py:487
  34.2 2.0 %collective-permute-start.7 = (f32[1,5,8,128]{3,2,1,0:T(8,128)S(1)}, f32[1,5,8,128]{3,2,1,0:T(8,128)S(1)}, u32[]{:S(2)}, u32[]{:S(2)}) collective-permute-start(f32[1,5,8,128]{3,2,1,0:T(8,128)S(1)} %bitcast.49), channel_id=1, source_target_pairs={{0,8},{8,0},{16,24},{24,16},{1,9},{9,1},{17,25},{25,17},{2,10},{10... | collective-permute-start | bytes 61448 | tf_op jit(solution)/shard_map/ppermute | solution.py:93
  36.2 1.5 %collective-permute-start.8 = (f32[1,5,8,128]{3,2,1,0:T(8,128)S(1)}, f32[1,5,8,128]{3,2,1,0:T(8,128)S(1)}, u32[]{:S(2)}, u32[]{:S(2)}) collective-permute-start(f32[1,5,8,128]{3,2,1,0:T(8,128)S(1)} %bitcast.50), channel_id=1, source_target_pairs={{0,16},{8,24},{16,0},{24,8},{1,17},{9,25},{17,1},{25,9},{2,18},{10... | collective-permute-start | bytes 61448 | tf_op jit(solution)/shard_map/ppermute | solution.py:93
  37.7 1.0 collective-permute-start.9
  38.7 4.8 %pairs.1 = (f32[4,48,128,128]{3,2,1,0:T(8,128)S(1)}, f32[4,48,128,128]{3,2,1,0:T(8,128)S(1)}) custom-call(s32[2]{0:T(128)S(1)} %pad_add_fusion.1.meta, s32[16,71]{1,0:T(8,128)S(1)} %pad_add_fusion.lists, f32[48,8,128]{2,1,0:T(8,128)S(1)} %get-tuple-element.14.pts, f32[4,48,8,128]{3,2,1,0:T(8,128)S(1)} %get-tuple-element.15.src), custom_call_target="tpu_custom_call" | custom-call | tf_op jit(solution)/shard_map/pairs/pallas_call | solution.py:487
  43.5 0.0 collective-permute-done.9
  43.5 0.0 collective-permute-done.8
  43.5 0.0 collective-permute-done.7
  43.5 1.2 %combine.1 = (f32[16,128]{1,0:T(8,128)}, f32[32,128]{1,0:T(8,128)S(1)}) custom-call(s32[2]{0:T(128)S(1)} %pad_add_fusion.1.meta, f32[5,8,128]{2,1,0:T(8,128)S(1)} %get-tuple-element.13.refs_0_, f32[5,8,128]{2,1,0:T(8,128)S(1)} %bitcast.52, f32[5,8,128]{2,1,0:T(8,128)S(1)} %bitcast.55, f32[5,8,128]{2,1,0:T(8,128)S(1)} %bitcast.57), custom_call_target="tpu_custom_call" | custom-call | tf_op jit(solution)/shard_map/combine/pallas_call | solution.py:487
  44.7 0.0 collective-permute-start.12
  44.7 1.2 %collective-permute-done.12 = f32[1,32,128]{2,1,0:T(8,128)S(1)} collective-permute-done((f32[1,32,128]{2,1,0:T(8,128)S(1)}, f32[1,32,128]{2,1,0:T(8,128)S(1)}, u32[]{:S(2)}, u32[]{:S(2)}) %collective-permute-start.12) | collective-permute-done | bytes 16416 | tf_op jit(solution)/shard_map/ppermute | solution.py:93
  45.9 0.5 collective-permute-start.13
  46.4 0.6 collective-permute-start.14
  47.0 2.4 %collective-permute-start.15 = (f32[2,32,128]{2,1,0:T(8,128)S(1)}, f32[2,32,128]{2,1,0:T(8,128)S(1)}, u32[]{:S(2)}, u32[]{:S(2)}) collective-permute-start(f32[2,32,128]{2,1,0:T(8,128)S(1)} %pad_maximum_fusion.2.refs_0_), channel_id=1, source_target_pairs={{0,6},{1,7},{2,4},{3,5},{4,2},{5,3},{6,0},{7,1},{8,14},{9,15},{10,... | collective-permute-start | bytes 98312 | tf_op jit(solution)/shard_map/ppermute | solution.py:93
  49.4 0.1 maximum_convert_fusion.levels
  49.4 0.3 collective-permute-done.13.refs_1_
  49.8 0.8 collective-permute-done.14.refs_2_
  50.6 1.2 %collective-permute-done.15.refs_3_ = f32[2,32,128]{2,1,0:T(8,128)S(1)} collective-permute-done((f32[2,32,128]{2,1,0:T(8,128)S(1)}, f32[2,32,128]{2,1,0:T(8,128)S(1)}, u32[]{:S(2)}, u32[]{:S(2)}) %collective-permute-start.15) | collective-permute-done | bytes 32800 | tf_op jit(solution)/shard_map/ppermute | solution.py:93
  51.8 0.0 collective-permute-done.10.before
  51.8 0.0 collective-permute-done.11.after
  51.8 51.7 %orbitals.1 = f32[4,4,8,128]{3,2,1,0:T(8,128)S(1)} custom-call(s32[2]{0:T(128)S(1)} %pad_add_fusion.1.meta, s32[16,71]{1,0:T(8,128)S(1)} %pad_add_fusion.lists, s32[32]{0:T(128)S(1)} %maximum_convert_fusion.levels, f32[32]{0:T(128)S(1)} %broadcast_multiply_fusion.1.rates_of, f32[48,8,128]{2,1,0:T(8,128)S(1)} %get-tuple-element.14.pts, ...), custom_call_target="tpu_custom_call" | custom-call | tf_op jit(solution)/shard_map/orbitals/pallas_call | solution.py:487
  103.6 1.3 %collective-permute-start.16 = (f32[4,8,128]{2,1,0:T(8,128)S(1)}, f32[4,8,128]{2,1,0:T(8,128)S(1)}, u32[]{:S(2)}, u32[]{:S(2)}) collective-permute-start(f32[4,8,128]{2,1,0:T(8,128)S(1)} %get-tuple-element.22), channel_id=1, source_target_pairs={{0,8},{8,0},{16,24},{24,16},{1,9},{9,1},{17,25},{25,17},{2,10},{10... | collective-permute-start | bytes 49160 | tf_op jit(solution)/shard_map/ppermute | solution.py:608
  104.8 2.4 %collective-permute-start.17 = (f32[4,8,128]{2,1,0:T(8,128)S(1)}, f32[4,8,128]{2,1,0:T(8,128)S(1)}, u32[]{:S(2)}, u32[]{:S(2)}) collective-permute-start(f32[4,8,128]{2,1,0:T(8,128)S(1)} %get-tuple-element.21), channel_id=1, source_target_pairs={{0,16},{8,24},{16,0},{24,8},{1,17},{9,25},{17,1},{25,9},{2,18},{10... | collective-permute-start | bytes 49160 | tf_op jit(solution)/shard_map/ppermute | solution.py:608
  107.2 0.8 collective-permute-start.18
  108.0 0.0 collective-permute-done.16.refs_1_
  108.0 1.4 %collective-permute-done.17.refs_2_ = f32[4,8,128]{2,1,0:T(8,128)S(1)} collective-permute-done((f32[4,8,128]{2,1,0:T(8,128)S(1)}, f32[4,8,128]{2,1,0:T(8,128)S(1)}, u32[]{:S(2)}, u32[]{:S(2)}) %collective-permute-start.17) | collective-permute-done | bytes 16416 | tf_op jit(solution)/shard_map/ppermute | solution.py:608
  109.5 3.3 %collective-permute-done.18.refs_3_ = f32[4,8,128]{2,1,0:T(8,128)S(1)} collective-permute-done((f32[4,8,128]{2,1,0:T(8,128)S(1)}, f32[4,8,128]{2,1,0:T(8,128)S(1)}, u32[]{:S(2)}, u32[]{:S(2)}) %collective-permute-start.18) | collective-permute-done | bytes 16416 | tf_op jit(solution)/shard_map/ppermute | solution.py:608
  112.8 1.2 %place.1 = f32[8,16,128]{2,1,0:T(8,128)} custom-call(s32[2]{0:T(128)S(1)} %pad_add_fusion.1.meta, f32[4,8,128]{2,1,0:T(8,128)S(1)} %get-tuple-element.23.refs_0_, f32[4,8,128]{2,1,0:T(8,128)S(1)} %collective-permute-done.16.refs_1_, f32[4,8,128]{2,1,0:T(8,128)S(1)} %collective-permute-done.17.refs_2_, f32[4,8,128]{2,1,0:T(8,128)S(1)} %collective-permute-done.18.refs_3_), custom_call_target="tpu_custom_call" | custom-call | tf_op jit(solution)/shard_map/place/pallas_call | solution.py:487
  (9 shorter events, 0.0 us)
Async XLA Ops:
  0.6 11.5 %collective-permute-start.1 = (f32[1,8,16,128]{3,2,1,0:T(8,128)}, f32[1,8,16,128]{3,2,1,0:T(8,128)S(1)}, u32[]{:S(2)}, u32[]{:S(2)}) collective-permute-start(f32[1,8,16,128]{3,2,1,0:T(8,128)} %bitcast.60), channel_id=1, source_target_pairs={{0,16},{8,24},{16,0},{24,8},{1,17},{9,25},{17,1},{25,9},{2,18},{10... | collective-permute-start | bytes 196616 | tf_op jit(solution)/shard_map/ppermute | solution.py:93
  3.3 8.9 %collective-permute-start.2 = (f32[1,8,16,128]{3,2,1,0:T(8,128)}, f32[1,8,16,128]{3,2,1,0:T(8,128)S(1)}, u32[]{:S(2)}, u32[]{:S(2)}) collective-permute-start(f32[1,8,16,128]{3,2,1,0:T(8,128)} %bitcast.61), channel_id=1, source_target_pairs={{0,24},{8,16},{16,8},{24,0},{1,25},{9,17},{17,9},{25,1},{2,26},{10... | collective-permute-start | bytes 196616 | tf_op jit(solution)/shard_map/ppermute | solution.py:93
  4.6 7.5 %collective-permute-start = (f32[1,8,16,128]{3,2,1,0:T(8,128)}, f32[1,8,16,128]{3,2,1,0:T(8,128)S(1)}, u32[]{:S(2)}, u32[]{:S(2)}) collective-permute-start(f32[1,8,16,128]{3,2,1,0:T(8,128)} %bitcast.62), channel_id=1, source_target_pairs={{0,8},{8,0},{16,24},{24,16},{1,9},{9,1},{17,25},{25,17},{2,10},{10... | collective-permute-start | bytes 196616 | tf_op jit(solution)/shard_map/ppermute | solution.py:93
  13.3 1.3 %collective-permute-start.3 = (f32[1,16,8,128]{3,2,1,0:T(8,128)S(1)}, f32[1,16,8,128]{3,2,1,0:T(8,128)S(1)}, u32[]{:S(2)}, u32[]{:S(2)}) collective-permute-start(f32[1,16,8,128]{3,2,1,0:T(8,128)S(1)} %bitcast.41), channel_id=1, source_target_pairs={{0,1},{1,0},{2,3},{3,2},{4,5},{5,4},{6,7},{7,6},{8,9},{9,8},{10,11... | collective-permute-start | bytes 196616 | tf_op jit(solution)/shard_map/ppermute | solution.py:93
  14.5 11.0 %collective-permute-start.4 = (f32[2,16,8,128]{3,2,1,0:T(8,128)S(1)}, f32[2,16,8,128]{3,2,1,0:T(8,128)S(1)}, u32[]{:S(2)}, u32[]{:S(2)}) collective-permute-start(f32[2,16,8,128]{3,2,1,0:T(8,128)S(1)} %pad_maximum_fusion.1.refs_0_), channel_id=1, source_target_pairs={{0,2},{1,3},{2,0},{3,1},{4,6},{5,7},{6,4},{7,5},{8,10},{9,11},{10,... | collective-permute-start | bytes 393224 | tf_op jit(solution)/shard_map/ppermute | solution.py:93
  16.1 9.4 %collective-permute-start.5 = (f32[2,16,8,128]{3,2,1,0:T(8,128)S(1)}, f32[2,16,8,128]{3,2,1,0:T(8,128)S(1)}, u32[]{:S(2)}, u32[]{:S(2)}) collective-permute-start(f32[2,16,8,128]{3,2,1,0:T(8,128)S(1)} %pad_maximum_fusion.1.refs_0_), channel_id=1, source_target_pairs={{0,4},{1,5},{2,6},{3,7},{4,0},{5,1},{6,2},{7,3},{8,12},{9,13},{10,... | collective-permute-start | bytes 393224 | tf_op jit(solution)/shard_map/ppermute | solution.py:93
  16.6 8.9 %collective-permute-start.6 = (f32[2,16,8,128]{3,2,1,0:T(8,128)S(1)}, f32[2,16,8,128]{3,2,1,0:T(8,128)S(1)}, u32[]{:S(2)}, u32[]{:S(2)}) collective-permute-start(f32[2,16,8,128]{3,2,1,0:T(8,128)S(1)} %pad_maximum_fusion.1.refs_0_), channel_id=1, source_target_pairs={{0,6},{1,7},{2,4},{3,5},{4,2},{5,3},{6,0},{7,1},{8,14},{9,15},{10,... | collective-permute-start | bytes 393224 | tf_op jit(solution)/shard_map/ppermute | solution.py:93
  19.0 32.8 %collective-permute-start.10 = (f32[512,128]{1,0:T(8,128)S(1)}, f32[512,128]{1,0:T(8,128)S(1)}, u32[]{:S(2)}, u32[]{:S(2)}) collective-permute-start(f32[512,128]{1,0:T(8,128)S(1)} %pad_maximum_fusion.mine), channel_id=1, source_target_pairs={{0,1},{1,2},{2,3},{3,4},{4,5},{5,6},{6,7},{8,9},{9,10},{10,11},{11... | collective-permute-start | bytes 786440 | tf_op jit(solution)/shard_map/ppermute | solution.py:544
  21.0 30.9 %collective-permute-start.11 = (f32[512,128]{1,0:T(8,128)S(1)}, f32[512,128]{1,0:T(8,128)S(1)}, u32[]{:S(2)}, u32[]{:S(2)}) collective-permute-start(f32[512,128]{1,0:T(8,128)S(1)} %pad_maximum_fusion.mine), channel_id=1, source_target_pairs={{1,0},{2,1},{3,2},{4,3},{5,4},{6,5},{7,6},{9,8},{10,9},{11,10},{12... | collective-permute-start | bytes 786440 | tf_op jit(solution)/shard_map/ppermute | solution.py:544
  34.2 9.3 %collective-permute-start.7 = (f32[1,5,8,128]{3,2,1,0:T(8,128)S(1)}, f32[1,5,8,128]{3,2,1,0:T(8,128)S(1)}, u32[]{:S(2)}, u32[]{:S(2)}) collective-permute-start(f32[1,5,8,128]{3,2,1,0:T(8,128)S(1)} %bitcast.49), channel_id=1, source_target_pairs={{0,8},{8,0},{16,24},{24,16},{1,9},{9,1},{17,25},{25,17},{2,10},{10... | collective-permute-start | bytes 61448 | tf_op jit(solution)/shard_map/ppermute | solution.py:93
  36.2 7.3 %collective-permute-start.8 = (f32[1,5,8,128]{3,2,1,0:T(8,128)S(1)}, f32[1,5,8,128]{3,2,1,0:T(8,128)S(1)}, u32[]{:S(2)}, u32[]{:S(2)}) collective-permute-start(f32[1,5,8,128]{3,2,1,0:T(8,128)S(1)} %bitcast.50), channel_id=1, source_target_pairs={{0,16},{8,24},{16,0},{24,8},{1,17},{9,25},{17,1},{25,9},{2,18},{10... | collective-permute-start | bytes 61448 | tf_op jit(solution)/shard_map/ppermute | solution.py:93
  37.7 5.8 %collective-permute-start.9 = (f32[1,5,8,128]{3,2,1,0:T(8,128)S(1)}, f32[1,5,8,128]{3,2,1,0:T(8,128)S(1)}, u32[]{:S(2)}, u32[]{:S(2)}) collective-permute-start(f32[1,5,8,128]{3,2,1,0:T(8,128)S(1)} %bitcast.51), channel_id=1, source_target_pairs={{0,24},{8,16},{16,8},{24,0},{1,25},{9,17},{17,9},{25,1},{2,26},{10... | collective-permute-start | bytes 61448 | tf_op jit(solution)/shard_map/ppermute | solution.py:93
  44.7 1.2 %collective-permute-start.12 = (f32[1,32,128]{2,1,0:T(8,128)S(1)}, f32[1,32,128]{2,1,0:T(8,128)S(1)}, u32[]{:S(2)}, u32[]{:S(2)}) collective-permute-start(f32[1,32,128]{2,1,0:T(8,128)S(1)} %bitcast.58), channel_id=1, source_target_pairs={{0,1},{1,0},{2,3},{3,2},{4,5},{5,4},{6,7},{7,6},{8,9},{9,8},{10,11... | collective-permute-start | bytes 49160 | tf_op jit(solution)/shard_map/ppermute | solution.py:93
  45.9 3.9 %collective-permute-start.13 = (f32[2,32,128]{2,1,0:T(8,128)S(1)}, f32[2,32,128]{2,1,0:T(8,128)S(1)}, u32[]{:S(2)}, u32[]{:S(2)}) collective-permute-start(f32[2,32,128]{2,1,0:T(8,128)S(1)} %pad_maximum_fusion.2.refs_0_), channel_id=1, source_target_pairs={{0,2},{1,3},{2,0},{3,1},{4,6},{5,7},{6,4},{7,5},{8,10},{9,11},{10,... | collective-permute-start | bytes 98312 | tf_op jit(solution)/shard_map/ppermute | solution.py:93
  46.4 4.3 %collective-permute-start.14 = (f32[2,32,128]{2,1,0:T(8,128)S(1)}, f32[2,32,128]{2,1,0:T(8,128)S(1)}, u32[]{:S(2)}, u32[]{:S(2)}) collective-permute-start(f32[2,32,128]{2,1,0:T(8,128)S(1)} %pad_maximum_fusion.2.refs_0_), channel_id=1, source_target_pairs={{0,4},{1,5},{2,6},{3,7},{4,0},{5,1},{6,2},{7,3},{8,12},{9,13},{10,... | collective-permute-start | bytes 98312 | tf_op jit(solution)/shard_map/ppermute | solution.py:93
  47.0 4.8 %collective-permute-start.15 = (f32[2,32,128]{2,1,0:T(8,128)S(1)}, f32[2,32,128]{2,1,0:T(8,128)S(1)}, u32[]{:S(2)}, u32[]{:S(2)}) collective-permute-start(f32[2,32,128]{2,1,0:T(8,128)S(1)} %pad_maximum_fusion.2.refs_0_), channel_id=1, source_target_pairs={{0,6},{1,7},{2,4},{3,5},{4,2},{5,3},{6,0},{7,1},{8,14},{9,15},{10,... | collective-permute-start | bytes 98312 | tf_op jit(solution)/shard_map/ppermute | solution.py:93
  103.6 4.5 %collective-permute-start.16 = (f32[4,8,128]{2,1,0:T(8,128)S(1)}, f32[4,8,128]{2,1,0:T(8,128)S(1)}, u32[]{:S(2)}, u32[]{:S(2)}) collective-permute-start(f32[4,8,128]{2,1,0:T(8,128)S(1)} %get-tuple-element.22), channel_id=1, source_target_pairs={{0,8},{8,0},{16,24},{24,16},{1,9},{9,1},{17,25},{25,17},{2,10},{10... | collective-permute-start | bytes 49160 | tf_op jit(solution)/shard_map/ppermute | solution.py:608
  104.8 4.6 %collective-permute-start.17 = (f32[4,8,128]{2,1,0:T(8,128)S(1)}, f32[4,8,128]{2,1,0:T(8,128)S(1)}, u32[]{:S(2)}, u32[]{:S(2)}) collective-permute-start(f32[4,8,128]{2,1,0:T(8,128)S(1)} %get-tuple-element.21), channel_id=1, source_target_pairs={{0,16},{8,24},{16,0},{24,8},{1,17},{9,25},{17,1},{25,9},{2,18},{10... | collective-permute-start | bytes 49160 | tf_op jit(solution)/shard_map/ppermute | solution.py:608
  107.2 5.5 %collective-permute-start.18 = (f32[4,8,128]{2,1,0:T(8,128)S(1)}, f32[4,8,128]{2,1,0:T(8,128)S(1)}, u32[]{:S(2)}, u32[]{:S(2)}) collective-permute-start(f32[4,8,128]{2,1,0:T(8,128)S(1)} %get-tuple-element.20), channel_id=1, source_target_pairs={{0,24},{8,16},{16,8},{24,0},{1,25},{9,17},{17,9},{25,1},{2,26},{10... | collective-permute-start | bytes 49160 | tf_op jit(solution)/shard_map/ppermute | solution.py:608

commit v6 on v5

--- a/solution.py
+++ b/solution.py
@@ -26,32 +26,26 @@
 scales = [1.0 / np.prod([node_set[a] - r for r in roots[a]]) for a in range(NODES)]
 
 
-def basis_rows():
+def put_basis(cst):
     row = lax.broadcasted_iota(jnp.int32, (ROWS, LANES), 0)
-    out = []
-    for pick in (row // 4, 2 + row // 4, row % 4):
+    for i, pick in enumerate((row // 4, 2 + row // 4, row % 4)):
         for k in range(NODES):
             values = [float(scales[a] if k == NODES - 1 else roots[a][k]) for a in range(NODES)]
             made = jnp.full((ROWS, LANES), values[0], jnp.float32)
             for a in range(1, NODES):
                 made = jnp.where(pick == a, values[a], made)
-            out.append(made)
+            cst[NODES * i + k] = made
+
+
+def node_offsets():
+    lane = lax.broadcasted_iota(jnp.int32, (1, LANES), 1) % HALF
+    out = []
+    for pick in (lane // 16, lane // 4 % 4, lane % 4):
+        made = jnp.full((1, LANES), 0.5 * (node_set[0] + 1.0), jnp.float32)
+        for a in range(1, NODES):
+            made = jnp.where(pick == a, float(0.5 * (node_set[a] + 1.0)), made)
+        out.append(made)
     return out
-
-
-def proxy_table(planes, window):
-    offset = 0.5 * (node_set + 1.0)
-    p = np.arange(LANES) % HALF
-    offs = np.stack([offset[p // 16], offset[p // 4 % 4], offset[p % 4]])
-    cells = np.arange(window)
-    lows = np.stack([cells % 4, cells // 4 % 4, cells // 16]) * cell_side
-    near = lows[:, :, None] + offs[:, None, :] * cell_side
-    levels = np.arange(planes)
-    lows = np.stack([0 * levels, 0 * levels, levels]) * cell_side
-    far = lows[:, :, None] + offs[:, None, :] * np.array([1.0, 1.0, cell_side])[:, None, None]
-    table = np.zeros((window + planes, ROWS, LANES), np.float32)
-    table[:, :3] = np.moveaxis(np.concatenate([near, far], 1), 0, 1)
-    return table
 
 
 def poly(u, r0, r1, r2, scale):
@@ -138,8 +132,8 @@
 
 def charge_kernel(meta, own, partial, *refs):
     z_low = meta[0].astype(jnp.float32) * cell_side
-    fields, (out, density) = refs[:-2], refs[-2:]
-    cst = basis_rows()
+    fields, (out, density, cst) = refs[:-3], refs[-3:]
+    put_basis(cst)
     total = partial[...]
     for phi in fields:
         for j in range(phi.shape[0]):
@@ -148,7 +142,7 @@
     density[...] = 2.0 * total
     acc = jnp.zeros((HALF, LANES), jnp.float32)
     for c in range(PLANE):
-        point = own[c]
+        point = own[:, c, :]
         charge = point[4:5] * density[c : c + 1, :]
         low = (cell_side * (c % 4), cell_side * (c // 4), z_low)
         acc = acc + weights(cst, point[0:1], point[1:2], point[2:3], (0.0, 0.0, z_low), (1.0, 1.0, cell_side)) * charge
@@ -166,8 +160,15 @@
     return below, below + jnp.maximum(planes - 2 - me, 0)
 
 
-def list_lengths(lists, cell, slots):
-    return lists[cell, sum(slots)], lists[cell, sum(slots) + 1]
+def list_lengths(lists, cell, slots, me, planes):
+    low, high = jnp.int32(0), jnp.int32(slots[0])
+    for _ in range(slots[0].bit_length()):
+        mid = (low + high) // 2
+        live = (low < high) & (lists[cell, jnp.minimum(mid, slots[0] - 1)] >= 0)
+        high = jnp.where(live | (low >= high), high, mid)
+        low = jnp.where(live, mid + 1, low)
+    around = 1 + (me > 0).astype(jnp.int32) + (me + 1 < planes).astype(jnp.int32)
+    return low, around * PLANE - low
 
 
 def list_blocks(me, cell, lists, slots, planes, put_near, put_far, put_none, multiple):
@@ -175,7 +176,7 @@
     base = (me - 1) * PLANE
     below, n_planes = live_planes(me, planes)
     near_slots, far_slots = slots
-    n_near, n_far = list_lengths(lists, cell, slots)
+    n_near, n_far = list_lengths(lists, cell, slots, me, planes)
     n_items = n_far + n_planes
     n_pairs = (n_items + 1) // 2
 
@@ -225,28 +226,38 @@
     return jnp.concatenate([message[pl.ds(g * rows + c, kinds, stride=PLANE), :] for g in range(groups)], axis=0)
 
 
-def hartree_kernel(groups, kinds, unroll, slots, meta, lists, table, marks, mine, *refs):
-    parts, (out, pts, src, every, items, tgt) = refs[:-6], refs[-6:]
+def hartree_kernel(groups, kinds, unroll, slots, meta, lists, marks, mine, *refs):
+    parts, (out, pts, src, every, items, tgt, cst) = refs[:-7], refs[-7:]
     lay_out(parts, every)
     planes = every.shape[0]
     cells = PLANE // groups
     me, group = meta[0], meta[1]
     window = 3 * PLANE
-    cst = basis_rows()
+    put_basis(cst)
     for k in range(3):
         there = lax.bitwise_xor(me, jnp.clip(me - 1 + k, 0, planes - 1))
         for c in range(PLANE):
             pts[k * PLANE + c] = every[there, c]
     row = lax.broadcasted_iota(jnp.int32, (ROWS, 1), 0)
 
+    offsets = node_offsets()
+
+    def item_of(lows, sides, moments):
+        made = jnp.where(row == 5, moments, 0.0)
+        for d in range(3):
+            made = jnp.where(row == d, lows[d] + offsets[d] * sides[d], made)
+        return made
+
     def put_cell(c, carry):
-        items[c] = jnp.where(row == 5, pts[c, 6:7, :], table[c])
+        lows = (*cell_low(c), (me - 1 + c // PLANE).astype(jnp.float32) * cell_side)
+        items[c] = item_of(lows, (cell_side,) * 3, pts[c, 6:7, :])
         return carry
 
     lax.fori_loop(0, window, put_cell, 0, unroll=8)
 
     def put_plane(g, c):
-        items[window + g] = jnp.where(row == 5, every[lax.bitwise_xor(me, g), 0, 7:8, :], table[window + g])
+        lows = (0.0, 0.0, g.astype(jnp.float32) * cell_side)
+        items[window + g] = item_of(lows, (1.0, 1.0, cell_side), every[lax.bitwise_xor(me, g), 0, 7:8, :])
         return c
 
     lax.fori_loop(0, planes, put_plane, 0)
@@ -300,7 +311,7 @@
     def per_cell(t, carry):
         cell = target_cell(group, t, groups)
         put_targets(pts, cell, tgt)
-        n_near, n_far = list_lengths(lists, cell, slots)
+        n_near, n_far = list_lengths(lists, cell, slots, meta[0], planes)
         n_blocks = n_near + (n_far + n_planes + 1) // 2
 
         def measure(i, x):
@@ -337,13 +348,14 @@
 
 
 def orbital_kernel(
-    planes, batch, unit, steps, slots, meta, lists, levels, rates_of,
+    planes, batch, unit, steps, slots, meta, lists, table,
     pts, before, mine, after, dist, inv, *refs,
 ):
-    parts, (out, rate, slot_of, every, val, mom, srcv, acc) = refs[:-8], refs[-8:]
+    parts, (out, rate, slot_of, every, val, mom, srcv, acc, cst) = refs[:-9], refs[-9:]
     lay_out(parts, every)
     groups, cells, kinds, _ = out.shape
     orbs = groups * kinds
+    n_rates = table.shape[0] - orbs
     me, group = meta[0], meta[1]
 
     def clear(i, c):
@@ -351,24 +363,24 @@
         rate[i] = 0.0
         return c
 
-    lax.fori_loop(0, rates_of.shape[0], clear, 0)
+    lax.fori_loop(0, n_rates, clear, 0)
     for q in range(2 * batch):
-        rate[rates_of.shape[0] + q] = 0.0
+        rate[n_rates + q] = 0.0
     lane = lax.broadcasted_iota(jnp.int32, (1, LANES), 1) % orbs
 
     def rank(i, carry):
         found, lane_slot = carry
-        level = levels[i]
+        level = table[i].astype(jnp.int32)
         known = slot_of[level]
         slot = jnp.where(known < 0, found, known)
         slot_of[level] = slot
-        rate[slot] = rates_of[level]
+        rate[slot] = table[orbs + level] * (-log2e)
         return found + (known < 0).astype(jnp.int32), jnp.where(lane == i, slot, lane_slot)
 
     n_levels, lane_slot = lax.fori_loop(0, orbs, rank, (jnp.int32(0), jnp.zeros((1, LANES), jnp.int32)))
     n_batches = (n_levels + batch - 1) // batch
     first_half = lax.broadcasted_iota(jnp.int32, (1, 2 * orbs), 1) < orbs
-    cst = basis_rows()
+    put_basis(cst)
 
     def flip(v):
         high = v.astype(jnp.bfloat16).astype(jnp.float32)
@@ -507,29 +519,15 @@
 
     fields = gather_list(orbitals, "orb")
     weight = quad_weight * (cell_side**3 / point_count)
-    own = jnp.concatenate(
-        [jnp.transpose(points, (1, 0, 2)), external[:, None], weight[:, None], jnp.zeros((cells, 3, LANES), f32)], axis=1
-    )
+    own = jnp.concatenate([points, external[None], weight[None], jnp.zeros((3, cells, LANES), f32)], axis=0)
     marks = jnp.pad(level_index.astype(f32), (0, LANES - kinds))[None]
     ends = planes - 1
     up = [(i, i + 1) for i in range(ends)]
     down = [(i + 1, i) for i in range(ends)]
-    base_table = proxy_table(planes, window)
-    shift = np.zeros(base_table.shape, np.float32)
-    shift[:window, 2] = cell_side
-    table = jnp.asarray(base_table) + jnp.asarray(shift) * (me - 1).astype(f32)
     slots = (near_cells.shape[1], far_cells.shape[1])
-    lists = jnp.concatenate(
-        [
-            near_cells,
-            far_cells,
-            jnp.sum((near_cells >= 0).astype(jnp.int32), axis=1, keepdims=True),
-            jnp.sum((far_cells >= 0).astype(jnp.int32), axis=1, keepdims=True),
-        ],
-        axis=1,
-    )
-    rates_of = screening * (-log2e)
+    lists = jnp.concatenate([near_cells, far_cells], axis=1)
     partial = jnp.sum(orbitals * orbitals, axis=0)
+    basis = pltpu.VMEM((3 * NODES, ROWS, LANES), f32)
 
     charges = call(
         charge_kernel,
@@ -537,11 +535,11 @@
         jax.ShapeDtypeStruct((cells, ROWS, LANES), f32),
         1,
         (meta, own, partial, *fields[1:]),
-        [pltpu.VMEM((cells, LANES), f32)],
+        [pltpu.VMEM((cells, LANES), f32), basis],
     )
     mine = jnp.concatenate([f.reshape(kinds * cells, LANES) for f in fields], axis=0)
     charges, mine = gather_parts(charges, "space", False, mine)
-    before, after = lax.ppermute(mine, "space", up), lax.ppermute(mine, "space", down)
+    before = lax.ppermute(mine, "space", up)
 
     batch, unit, steps = 4, 4, 9
     most = near_cells.shape[1]
@@ -556,14 +554,17 @@
             jax.ShapeDtypeStruct((share, blocks, ROWS, LANES), f32),
         ),
         2,
-        (meta, lists, table, marks, mine, *charges),
+        (meta, lists, marks, mine, *charges),
         [
             pltpu.VMEM((planes, cells, ROWS, LANES), f32),
             pltpu.VMEM((window + planes + 1, ROWS, LANES), f32),
             pltpu.VMEM((3, LANES, LANES), f32),
+            basis,
         ],
         12,
     )
+    mine, shares = lax.optimization_barrier((mine, shares))
+    after = lax.ppermute(mine, "space", down)
     dist, inv = call(
         functools.partial(pairs_kernel, groups, planes, unit, slots),
         "pairs",
@@ -574,7 +575,7 @@
         4,
     )
     shares = gather_list(shares, "orb")
-    levels = jnp.concatenate([share[0, ROWS - 1, :kinds] for share in shares]).astype(jnp.int32)
+    levels = jnp.concatenate([share[0, ROWS - 1, :kinds] for share in shares] + [screening])
     hartree, combined = call(
         functools.partial(combine_kernel, kinds),
         "combine",
@@ -590,8 +591,8 @@
         functools.partial(orbital_kernel, planes, batch, unit, steps, slots),
         "orbitals",
         jax.ShapeDtypeStruct((groups, share, kinds, LANES), f32),
-        4,
-        (meta, lists, levels, rates_of, pts, before, mine, after, dist, inv, *gathered),
+        3,
+        (meta, lists, levels, pts, before, mine, after, dist, inv, *gathered),
         [
             pltpu.SMEM((screening.shape[0] + 2 * batch,), f32),
             pltpu.SMEM((screening.shape[0],), jnp.int32),
@@ -600,6 +601,7 @@
             pltpu.VMEM((window + planes, HALF, 2 * orbs), bf16),
             pltpu.VMEM((blocks, LANES, 2 * orbs), bf16),
             pltpu.VMEM((levels_at_most, batch * LANES, 2 * orbs), f32),
+            basis,
         ],
         14,
     )

time: 116 us -> 132 us (1.14)
  local copies, waits for them, and re-layouts: 1.02 us -> 19 us
  other arithmetic: 8.19 us -> 4.05 us
  waiting for transfers between devices: 8.68 us -> 12.4 us
  starting transfers between devices: 26.7 us -> 24.7 us
    unnamed x1 -> x8, local copies, waits for them, and re-layouts: 0.75 us -> 18.2 us
    ppermute x14, waiting for transfers between devices: 3.96 us -> 10.6 us  [gather_parts(): lax.ppermute(held, axis, [(i, i ^ have * j) for i in range(count)])]
    ppermute x3, waiting for transfers between devices: 4.71 us -> 1.89 us  [body(): lax.ppermute(sent[k], 'orb', [(i, i ^ k) for i in range(groups)])]
    ppermute x2, starting transfers between devices: 6.45 us -> 3.82 us  [the longest x1 1.91 us: body(): before = lax.ppermute(mine, 'space', up)]
    reduce_sum x3 -> x0, other arithmetic: 2.51 us -> none  [the longest x1 0.88 us: body(): partial = jnp.sum(orbitals * orbitals, axis=0)]
    mul x2 -> x0, other arithmetic: 1.36 us -> none  [the longest x1 0.7 us: body(): weight = quad_weight * (cell_side ** 3 / point_count)]
  transfers between devices with their start and end apart: 19 -> 19, of which waited for: 7 -> 9; matrix products, arithmetic and copies ran while one was open for 8% -> 4% of each run, Pallas kernels for 13% -> 12%
where the time goes in v6:
time: 132 us; the launch traced here: 129 us
  Pallas kernels  68.4 us (52%)
  starting transfers between devices  24.7 us (19%)
  local copies, waits for them, and re-layouts  19 us (14%)
  waiting for transfers between devices  12.4 us (9%)
  other arithmetic  4.05 us (3%)
    pallas_call x6, Pallas kernels, call(): pl.pallas_call(kernel, out_shape=out_shape, in_specs=[smem()] * smems + [...  68.4 us
    unnamed x8, local copies, waits for them, and re-layouts  18.2 us
    ppermute x14, starting transfers between devices, gather_parts(): lax.ppermute(held, axis, [(i, i ^ have * j) for i in range(count)])  16.4 us
    ppermute x14, waiting for transfers between devices, gather_parts(): lax.ppermute(held, axis, [(i, i ^ have * j) for i in range(count)])  10.6 us
    ppermute x3, starting transfers between devices, body(): lax.ppermute(sent[k], 'orb', [(i, i ^ k) for i in range(groups)])  4.44 us
  transfers between devices with their start and end apart: 19, of which 9 were waited for; matrix products, arithmetic and copies ran while one was open for 4% of the time, Pallas kernels for 12%

profile of v6, /device:TPU:4, one launch (start us, length us, event | category | flops | bytes accessed | tf_op | source)
XLA Modules:
  0.0 129.4 jit_solution(7755823622182642174)
XLA Ops:
  0.6 1.6 %collective-permute-start = (f32[1,8,16,128]{3,2,1,0:T(8,128)}, f32[1,8,16,128]{3,2,1,0:T(8,128)S(1)}, u32[]{:S(2)}, u32[]{:S(2)}) collective-permute-start(f32[1,8,16,128]{3,2,1,0:T(8,128)} %bitcast.56), channel_id=1, source_target_pairs={{0,8},{8,0},{16,24},{24,16},{1,9},{9,1},{17,25},{25,17},{2,10},{10... | collective-permute-start | bytes 196616 | tf_op jit(solution)/shard_map/ppermute | solution.py:87
  2.3 2.6 %collective-permute-start.1 = (f32[1,8,16,128]{3,2,1,0:T(8,128)}, f32[1,8,16,128]{3,2,1,0:T(8,128)S(1)}, u32[]{:S(2)}, u32[]{:S(2)}) collective-permute-start(f32[1,8,16,128]{3,2,1,0:T(8,128)} %bitcast.57), channel_id=1, source_target_pairs={{0,16},{8,24},{16,0},{24,8},{1,17},{9,25},{17,1},{25,9},{2,18},{10... | collective-permute-start | bytes 196616 | tf_op jit(solution)/shard_map/ppermute | solution.py:87
  4.9 0.2 collective-permute-start.2
  5.1 0.7 multiply_bitcast_fusion
  5.8 0.7 convert_element_type.5
  6.4 0.1 pad.16.clone
  6.5 1.0 maximum_maximum_fusion
  7.5 0.1 pad_add_fusion.1.meta
  7.5 0.0 collective-permute-done
  7.5 2.2 %collective-permute-done.1 = f32[1,8,16,128]{3,2,1,0:T(8,128)S(1)} collective-permute-done((f32[1,8,16,128]{3,2,1,0:T(8,128)}, f32[1,8,16,128]{3,2,1,0:T(8,128)S(1)}, u32[]{:S(2)}, u32[]{:S(2)}) %collective-permute-start.1) | collective-permute-done | bytes 65568 | tf_op jit(solution)/shard_map/ppermute | solution.py:87
  9.8 1.4 %collective-permute-done.2 = f32[1,8,16,128]{3,2,1,0:T(8,128)S(1)} collective-permute-done((f32[1,8,16,128]{3,2,1,0:T(8,128)}, f32[1,8,16,128]{3,2,1,0:T(8,128)S(1)}, u32[]{:S(2)}, u32[]{:S(2)}) %collective-permute-start.2) | collective-permute-done | bytes 65568 | tf_op jit(solution)/shard_map/ppermute | solution.py:87
  11.2 1.1 charge.1
  12.3 0.0 collective-permute-start.3
  12.3 0.9 pad_maximum_fusion.mine
  13.1 0.4 collective-permute-done.3
  13.5 1.6 %collective-permute-start.4 = (f32[2,16,8,128]{3,2,1,0:T(8,128)S(1)}, f32[2,16,8,128]{3,2,1,0:T(8,128)S(1)}, u32[]{:S(2)}, u32[]{:S(2)}) collective-permute-start(f32[2,16,8,128]{3,2,1,0:T(8,128)S(1)} %pad_maximum_fusion.1.refs_0_), channel_id=1, source_target_pairs={{0,2},{1,3},{2,0},{3,1},{4,6},{5,7},{6,4},{7,5},{8,10},{9,11},{10,... | collective-permute-start | bytes 393224 | tf_op jit(solution)/shard_map/ppermute | solution.py:87
  15.1 0.5 collective-permute-start.5
  15.6 1.5 %collective-permute-start.6 = (f32[2,16,8,128]{3,2,1,0:T(8,128)S(1)}, f32[2,16,8,128]{3,2,1,0:T(8,128)S(1)}, u32[]{:S(2)}, u32[]{:S(2)}) collective-permute-start(f32[2,16,8,128]{3,2,1,0:T(8,128)S(1)} %pad_maximum_fusion.1.refs_0_), channel_id=1, source_target_pairs={{0,6},{1,7},{2,4},{3,5},{4,2},{5,3},{6,0},{7,1},{8,14},{9,15},{10,... | collective-permute-start | bytes 393224 | tf_op jit(solution)/shard_map/ppermute | solution.py:87
  17.1 0.8 pad_add_fusion.lists
  17.9 1.9 %collective-permute-start.10 = (f32[512,128]{1,0:T(8,128)S(1)}, f32[512,128]{1,0:T(8,128)S(1)}, u32[]{:S(2)}, u32[]{:S(2)}) collective-permute-start(f32[512,128]{1,0:T(8,128)S(1)} %pad_maximum_fusion.mine), channel_id=1, source_target_pairs={{0,1},{1,2},{2,3},{3,4},{4,5},{5,6},{6,7},{8,9},{9,10},{10,11},{11... | collective-permute-start | bytes 786440 | tf_op jit(solution)/shard_map/ppermute | solution.py:542
  19.8 0.0 collective-permute-done.4.refs_1_
  19.8 3.4 %collective-permute-done.5.refs_2_ = f32[2,16,8,128]{3,2,1,0:T(8,128)S(1)} collective-permute-done((f32[2,16,8,128]{3,2,1,0:T(8,128)S(1)}, f32[2,16,8,128]{3,2,1,0:T(8,128)S(1)}, u32[]{:S(2)}, u32[]{:S(2)}) %collective-permute-start.5) | collective-permute-done | bytes 131104 | tf_op jit(solution)/shard_map/ppermute | solution.py:87
  23.2 0.0 collective-permute-done.6.refs_3_
  23.2 9.4 %hartree.1 = (f32[5,8,128]{2,1,0:T(8,128)S(1)}, f32[48,8,128]{2,1,0:T(8,128)S(1)}, f32[4,48,8,128]{3,2,1,0:T(8,128)S(1)}) custom-call(s32[2]{0:T(128)S(1)} %pad_add_fusion.1.meta, s32[16,69]{1,0:T(8,128)S(1)} %pad_add_fusion.lists, f32[1,128]{1,0:T(1,128)S(1)} %pad_bitcast_fusion.marks, f32[512,128]{1,0:T(8,128)S(1)} %pad_maximum_fusion.mine, ...), custom_call_target="tpu_custom_call" | custom-call | tf_op jit(solution)/shard_map/hartree/pallas_call | solution.py:499
  32.6 0.0 collective-permute-start.7
  32.6 2.2 %collective-permute-start.8 = (f32[1,5,8,128]{3,2,1,0:T(8,128)S(1)}, f32[1,5,8,128]{3,2,1,0:T(8,128)S(1)}, u32[]{:S(2)}, u32[]{:S(2)}) collective-permute-start(f32[1,5,8,128]{3,2,1,0:T(8,128)S(1)} %bitcast.48), channel_id=1, source_target_pairs={{0,16},{8,24},{16,0},{24,8},{1,17},{9,25},{17,1},{25,9},{2,18},{10... | collective-permute-start | bytes 61448 | tf_op jit(solution)/shard_map/ppermute | solution.py:87
  34.8 2.2 %collective-permute-start.9 = (f32[1,5,8,128]{3,2,1,0:T(8,128)S(1)}, f32[1,5,8,128]{3,2,1,0:T(8,128)S(1)}, u32[]{:S(2)}, u32[]{:S(2)}) collective-permute-start(f32[1,5,8,128]{3,2,1,0:T(8,128)S(1)} %bitcast.49), channel_id=1, source_target_pairs={{0,24},{8,16},{16,8},{24,0},{1,25},{9,17},{17,9},{25,1},{2,26},{10... | collective-permute-start | bytes 61448 | tf_op jit(solution)/shard_map/ppermute | solution.py:87
  37.0 1.9 %collective-permute-start.11 = (f32[512,128]{1,0:T(8,128)S(1)}, f32[512,128]{1,0:T(8,128)S(1)}, u32[]{:S(2)}, u32[]{:S(2)}) collective-permute-start(f32[512,128]{1,0:T(8,128)S(1)} %pad_maximum_fusion.mine), channel_id=1, source_target_pairs={{1,0},{2,1},{3,2},{4,3},{5,4},{6,5},{7,6},{9,8},{10,9},{11,10},{12... | collective-permute-start | bytes 786440 | tf_op jit(solution)/shard_map/ppermute | solution.py:567
  38.9 4.9 %pairs.1 = (f32[4,48,128,128]{3,2,1,0:T(8,128)S(1)}, f32[4,48,128,128]{3,2,1,0:T(8,128)S(1)}) custom-call(s32[2]{0:T(128)S(1)} %pad_add_fusion.1.meta, s32[16,69]{1,0:T(8,128)S(1)} %pad_add_fusion.lists, f32[48,8,128]{2,1,0:T(8,128)S(1)} %get-tuple-element.17.pts, f32[4,48,8,128]{3,2,1,0:T(8,128)S(1)} %get-tuple-element.19.src), custom_call_target="tpu_custom_call" | custom-call | tf_op jit(solution)/shard_map/pairs/pallas_call | solution.py:499
  43.8 0.0 copy-start
  43.8 4.5 %copy-done = f32[4,48,128,128]{3,2,1,0:T(8,128)} copy-done((f32[4,48,128,128]{3,2,1,0:T(8,128)}, f32[4,48,128,128]{3,2,1,0:T(8,128)S(1)}, u32[]{:S(2)}) %copy-start) | copy-done | bytes 12582936
  48.3 0.0 copy-start.2
  48.3 4.5 %copy-done.2 = f32[4,48,128,128]{3,2,1,0:T(8,128)} copy-done((f32[4,48,128,128]{3,2,1,0:T(8,128)}, f32[4,48,128,128]{3,2,1,0:T(8,128)S(1)}, u32[]{:S(2)}) %copy-start.2) | copy-done | bytes 12582936
  52.8 0.0 collective-permute-done.9
  52.8 0.0 collective-permute-done.7
  52.8 0.0 collective-permute-done.8
  52.8 1.2 combine.1
  54.0 0.5 collective-permute-start.12
  54.5 0.8 collective-permute-done.12
  55.3 0.4 collective-permute-start.13
  55.7 1.4 %collective-permute-start.14 = (f32[2,32,128]{2,1,0:T(8,128)S(1)}, f32[2,32,128]{2,1,0:T(8,128)S(1)}, u32[]{:S(2)}, u32[]{:S(2)}) collective-permute-start(f32[2,32,128]{2,1,0:T(8,128)S(1)} %pad_maximum_fusion.2.refs_0_), channel_id=1, source_target_pairs={{0,4},{1,5},{2,6},{3,7},{4,0},{5,1},{6,2},{7,3},{8,12},{9,13},{10,... | collective-permute-start | bytes 98312 | tf_op jit(solution)/shard_map/ppermute | solution.py:87
  57.1 1.7 %collective-permute-start.15 = (f32[2,32,128]{2,1,0:T(8,128)S(1)}, f32[2,32,128]{2,1,0:T(8,128)S(1)}, u32[]{:S(2)}, u32[]{:S(2)}) collective-permute-start(f32[2,32,128]{2,1,0:T(8,128)S(1)} %pad_maximum_fusion.2.refs_0_), channel_id=1, source_target_pairs={{0,6},{1,7},{2,4},{3,5},{4,2},{5,3},{6,0},{7,1},{8,14},{9,15},{10,... | collective-permute-start | bytes 98312 | tf_op jit(solution)/shard_map/ppermute | solution.py:87
  58.8 0.7 concatenate.22.table
  59.5 0.0 collective-permute-done.13.refs_1_
  59.5 0.1 collective-permute-done.14.refs_2_
  59.6 2.3 %collective-permute-done.15.refs_3_ = f32[2,32,128]{2,1,0:T(8,128)S(1)} collective-permute-done((f32[2,32,128]{2,1,0:T(8,128)S(1)}, f32[2,32,128]{2,1,0:T(8,128)S(1)}, u32[]{:S(2)}, u32[]{:S(2)}) %collective-permute-start.15) | collective-permute-done | bytes 32800 | tf_op jit(solution)/shard_map/ppermute | solution.py:87
  61.9 0.0 collective-permute-done.10.before
  61.9 0.0 collective-permute-done.11.after
  61.9 0.0 copy-start.1
  61.9 4.6 %copy-done.1 = f32[4,48,128,128]{3,2,1,0:T(8,128)S(1)} copy-done((f32[4,48,128,128]{3,2,1,0:T(8,128)S(1)}, f32[4,48,128,128]{3,2,1,0:T(8,128)}, u32[]{:S(2)}) %copy-start.1) | copy-done | bytes 12582936
  66.5 0.0 copy-start.3
  66.5 4.6 %copy-done.3 = f32[4,48,128,128]{3,2,1,0:T(8,128)S(1)} copy-done((f32[4,48,128,128]{3,2,1,0:T(8,128)S(1)}, f32[4,48,128,128]{3,2,1,0:T(8,128)}, u32[]{:S(2)}) %copy-start.3) | copy-done | bytes 12582936
  71.0 50.7 %orbitals.1 = f32[4,4,8,128]{3,2,1,0:T(8,128)S(1)} custom-call(s32[2]{0:T(128)S(1)} %pad_add_fusion.1.meta, s32[16,69]{1,0:T(8,128)S(1)} %pad_add_fusion.lists, f32[64]{0:T(128)S(1)} %concatenate.22.table, f32[48,8,128]{2,1,0:T(8,128)S(1)} %get-tuple-element.17.pts, f32[512,128]{1,0:T(8,128)S(1)} %collective-permute-done.10.before, ...), custom_call_target="tpu_custom_call" | custom-call | tf_op jit(solution)/shard_map/orbitals/pallas_call | solution.py:499
  121.8 0.1 collective-permute-start.16
  121.9 0.7 collective-permute-start.17
  122.6 3.7 %collective-permute-start.18 = (f32[4,8,128]{2,1,0:T(8,128)S(1)}, f32[4,8,128]{2,1,0:T(8,128)S(1)}, u32[]{:S(2)}, u32[]{:S(2)}) collective-permute-start(f32[4,8,128]{2,1,0:T(8,128)S(1)} %get-tuple-element.24), channel_id=1, source_target_pairs={{0,24},{8,16},{16,8},{24,0},{1,25},{9,17},{17,9},{25,1},{2,26},{10... | collective-permute-start | bytes 49160 | tf_op jit(solution)/shard_map/ppermute | solution.py:610
  126.2 0.0 collective-permute-done.16.refs_1_
  126.2 0.3 collective-permute-done.17.refs_2_
  126.6 1.6 %collective-permute-done.18.refs_3_ = f32[4,8,128]{2,1,0:T(8,128)S(1)} collective-permute-done((f32[4,8,128]{2,1,0:T(8,128)S(1)}, f32[4,8,128]{2,1,0:T(8,128)S(1)}, u32[]{:S(2)}, u32[]{:S(2)}) %collective-permute-start.18) | collective-permute-done | bytes 16416 | tf_op jit(solution)/shard_map/ppermute | solution.py:610
  128.1 1.2 place.1
  (9 shorter events, 0.0 us)
Async XLA Ops:
  0.6 6.9 %collective-permute-start = (f32[1,8,16,128]{3,2,1,0:T(8,128)}, f32[1,8,16,128]{3,2,1,0:T(8,128)S(1)}, u32[]{:S(2)}, u32[]{:S(2)}) collective-permute-start(f32[1,8,16,128]{3,2,1,0:T(8,128)} %bitcast.56), channel_id=1, source_target_pairs={{0,8},{8,0},{16,24},{24,16},{1,9},{9,1},{17,25},{25,17},{2,10},{10... | collective-permute-start | bytes 196616 | tf_op jit(solution)/shard_map/ppermute | solution.py:87
  2.3 7.5 %collective-permute-start.1 = (f32[1,8,16,128]{3,2,1,0:T(8,128)}, f32[1,8,16,128]{3,2,1,0:T(8,128)S(1)}, u32[]{:S(2)}, u32[]{:S(2)}) collective-permute-start(f32[1,8,16,128]{3,2,1,0:T(8,128)} %bitcast.57), channel_id=1, source_target_pairs={{0,16},{8,24},{16,0},{24,8},{1,17},{9,25},{17,1},{25,9},{2,18},{10... | collective-permute-start | bytes 196616 | tf_op jit(solution)/shard_map/ppermute | solution.py:87
  4.9 6.3 %collective-permute-start.2 = (f32[1,8,16,128]{3,2,1,0:T(8,128)}, f32[1,8,16,128]{3,2,1,0:T(8,128)S(1)}, u32[]{:S(2)}, u32[]{:S(2)}) collective-permute-start(f32[1,8,16,128]{3,2,1,0:T(8,128)} %bitcast.58), channel_id=1, source_target_pairs={{0,24},{8,16},{16,8},{24,0},{1,25},{9,17},{17,9},{25,1},{2,26},{10... | collective-permute-start | bytes 196616 | tf_op jit(solution)/shard_map/ppermute | solution.py:87
  12.3 1.3 collective-permute-start.3
  13.5 6.3 %collective-permute-start.4 = (f32[2,16,8,128]{3,2,1,0:T(8,128)S(1)}, f32[2,16,8,128]{3,2,1,0:T(8,128)S(1)}, u32[]{:S(2)}, u32[]{:S(2)}) collective-permute-start(f32[2,16,8,128]{3,2,1,0:T(8,128)S(1)} %pad_maximum_fusion.1.refs_0_), channel_id=1, source_target_pairs={{0,2},{1,3},{2,0},{3,1},{4,6},{5,7},{6,4},{7,5},{8,10},{9,11},{10,... | collective-permute-start | bytes 393224 | tf_op jit(solution)/shard_map/ppermute | solution.py:87
  15.1 8.1 %collective-permute-start.5 = (f32[2,16,8,128]{3,2,1,0:T(8,128)S(1)}, f32[2,16,8,128]{3,2,1,0:T(8,128)S(1)}, u32[]{:S(2)}, u32[]{:S(2)}) collective-permute-start(f32[2,16,8,128]{3,2,1,0:T(8,128)S(1)} %pad_maximum_fusion.1.refs_0_), channel_id=1, source_target_pairs={{0,4},{1,5},{2,6},{3,7},{4,0},{5,1},{6,2},{7,3},{8,12},{9,13},{10,... | collective-permute-start | bytes 393224 | tf_op jit(solution)/shard_map/ppermute | solution.py:87
  15.6 7.6 %collective-permute-start.6 = (f32[2,16,8,128]{3,2,1,0:T(8,128)S(1)}, f32[2,16,8,128]{3,2,1,0:T(8,128)S(1)}, u32[]{:S(2)}, u32[]{:S(2)}) collective-permute-start(f32[2,16,8,128]{3,2,1,0:T(8,128)S(1)} %pad_maximum_fusion.1.refs_0_), channel_id=1, source_target_pairs={{0,6},{1,7},{2,4},{3,5},{4,2},{5,3},{6,0},{7,1},{8,14},{9,15},{10,... | collective-permute-start | bytes 393224 | tf_op jit(solution)/shard_map/ppermute | solution.py:87
  17.9 44.0 %collective-permute-start.10 = (f32[512,128]{1,0:T(8,128)S(1)}, f32[512,128]{1,0:T(8,128)S(1)}, u32[]{:S(2)}, u32[]{:S(2)}) collective-permute-start(f32[512,128]{1,0:T(8,128)S(1)} %pad_maximum_fusion.mine), channel_id=1, source_target_pairs={{0,1},{1,2},{2,3},{3,4},{4,5},{5,6},{6,7},{8,9},{9,10},{10,11},{11... | collective-permute-start | bytes 786440 | tf_op jit(solution)/shard_map/ppermute | solution.py:542
  32.6 20.3 %collective-permute-start.7 = (f32[1,5,8,128]{3,2,1,0:T(8,128)S(1)}, f32[1,5,8,128]{3,2,1,0:T(8,128)S(1)}, u32[]{:S(2)}, u32[]{:S(2)}) collective-permute-start(f32[1,5,8,128]{3,2,1,0:T(8,128)S(1)} %bitcast.47), channel_id=1, source_target_pairs={{0,8},{8,0},{16,24},{24,16},{1,9},{9,1},{17,25},{25,17},{2,10},{10... | collective-permute-start | bytes 61448 | tf_op jit(solution)/shard_map/ppermute | solution.py:87
  32.6 20.3 %collective-permute-start.8 = (f32[1,5,8,128]{3,2,1,0:T(8,128)S(1)}, f32[1,5,8,128]{3,2,1,0:T(8,128)S(1)}, u32[]{:S(2)}, u32[]{:S(2)}) collective-permute-start(f32[1,5,8,128]{3,2,1,0:T(8,128)S(1)} %bitcast.48), channel_id=1, source_target_pairs={{0,16},{8,24},{16,0},{24,8},{1,17},{9,25},{17,1},{25,9},{2,18},{10... | collective-permute-start | bytes 61448 | tf_op jit(solution)/shard_map/ppermute | solution.py:87
  34.8 18.0 %collective-permute-start.9 = (f32[1,5,8,128]{3,2,1,0:T(8,128)S(1)}, f32[1,5,8,128]{3,2,1,0:T(8,128)S(1)}, u32[]{:S(2)}, u32[]{:S(2)}) collective-permute-start(f32[1,5,8,128]{3,2,1,0:T(8,128)S(1)} %bitcast.49), channel_id=1, source_target_pairs={{0,24},{8,16},{16,8},{24,0},{1,25},{9,17},{17,9},{25,1},{2,26},{10... | collective-permute-start | bytes 61448 | tf_op jit(solution)/shard_map/ppermute | solution.py:87
  37.0 24.9 %collective-permute-start.11 = (f32[512,128]{1,0:T(8,128)S(1)}, f32[512,128]{1,0:T(8,128)S(1)}, u32[]{:S(2)}, u32[]{:S(2)}) collective-permute-start(f32[512,128]{1,0:T(8,128)S(1)} %pad_maximum_fusion.mine), channel_id=1, source_target_pairs={{1,0},{2,1},{3,2},{4,3},{5,4},{6,5},{7,6},{9,8},{10,9},{11,10},{12... | collective-permute-start | bytes 786440 | tf_op jit(solution)/shard_map/ppermute | solution.py:567
  43.8 4.5 %copy-start = (f32[4,48,128,128]{3,2,1,0:T(8,128)}, f32[4,48,128,128]{3,2,1,0:T(8,128)S(1)}, u32[]{:S(2)}) copy-start(f32[4,48,128,128]{3,2,1,0:T(8,128)S(1)} %get-tuple-element.20.dist) | copy-start | bytes 37748740
  48.3 4.5 %copy-start.2 = (f32[4,48,128,128]{3,2,1,0:T(8,128)}, f32[4,48,128,128]{3,2,1,0:T(8,128)S(1)}, u32[]{:S(2)}) copy-start(f32[4,48,128,128]{3,2,1,0:T(8,128)S(1)} %get-tuple-element.21.inv) | copy-start | bytes 37748740
  54.0 1.3 %collective-permute-start.12 = (f32[1,32,128]{2,1,0:T(8,128)S(1)}, f32[1,32,128]{2,1,0:T(8,128)S(1)}, u32[]{:S(2)}, u32[]{:S(2)}) collective-permute-start(f32[1,32,128]{2,1,0:T(8,128)S(1)} %bitcast.54), channel_id=1, source_target_pairs={{0,1},{1,0},{2,3},{3,2},{4,5},{5,4},{6,7},{7,6},{8,9},{9,8},{10,11... | collective-permute-start | bytes 49160 | tf_op jit(solution)/shard_map/ppermute | solution.py:87
  55.3 4.2 %collective-permute-start.13 = (f32[2,32,128]{2,1,0:T(8,128)S(1)}, f32[2,32,128]{2,1,0:T(8,128)S(1)}, u32[]{:S(2)}, u32[]{:S(2)}) collective-permute-start(f32[2,32,128]{2,1,0:T(8,128)S(1)} %pad_maximum_fusion.2.refs_0_), channel_id=1, source_target_pairs={{0,2},{1,3},{2,0},{3,1},{4,6},{5,7},{6,4},{7,5},{8,10},{9,11},{10,... | collective-permute-start | bytes 98312 | tf_op jit(solution)/shard_map/ppermute | solution.py:87
  55.7 3.9 %collective-permute-start.14 = (f32[2,32,128]{2,1,0:T(8,128)S(1)}, f32[2,32,128]{2,1,0:T(8,128)S(1)}, u32[]{:S(2)}, u32[]{:S(2)}) collective-permute-start(f32[2,32,128]{2,1,0:T(8,128)S(1)} %pad_maximum_fusion.2.refs_0_), channel_id=1, source_target_pairs={{0,4},{1,5},{2,6},{3,7},{4,0},{5,1},{6,2},{7,3},{8,12},{9,13},{10,... | collective-permute-start | bytes 98312 | tf_op jit(solution)/shard_map/ppermute | solution.py:87
  57.1 4.8 %collective-permute-start.15 = (f32[2,32,128]{2,1,0:T(8,128)S(1)}, f32[2,32,128]{2,1,0:T(8,128)S(1)}, u32[]{:S(2)}, u32[]{:S(2)}) collective-permute-start(f32[2,32,128]{2,1,0:T(8,128)S(1)} %pad_maximum_fusion.2.refs_0_), channel_id=1, source_target_pairs={{0,6},{1,7},{2,4},{3,5},{4,2},{5,3},{6,0},{7,1},{8,14},{9,15},{10,... | collective-permute-start | bytes 98312 | tf_op jit(solution)/shard_map/ppermute | solution.py:87
  61.9 4.6 %copy-start.1 = (f32[4,48,128,128]{3,2,1,0:T(8,128)S(1)}, f32[4,48,128,128]{3,2,1,0:T(8,128)}, u32[]{:S(2)}) copy-start(f32[4,48,128,128]{3,2,1,0:T(8,128)} %copy-done) | copy-start | bytes 37748740
  66.5 4.6 %copy-start.3 = (f32[4,48,128,128]{3,2,1,0:T(8,128)S(1)}, f32[4,48,128,128]{3,2,1,0:T(8,128)}, u32[]{:S(2)}) copy-start(f32[4,48,128,128]{3,2,1,0:T(8,128)} %copy-done.2) | copy-start | bytes 37748740
  121.8 4.5 %collective-permute-start.16 = (f32[4,8,128]{2,1,0:T(8,128)S(1)}, f32[4,8,128]{2,1,0:T(8,128)S(1)}, u32[]{:S(2)}, u32[]{:S(2)}) collective-permute-start(f32[4,8,128]{2,1,0:T(8,128)S(1)} %get-tuple-element.26), channel_id=1, source_target_pairs={{0,8},{8,0},{16,24},{24,16},{1,9},{9,1},{17,25},{25,17},{2,10},{10... | collective-permute-start | bytes 49160 | tf_op jit(solution)/shard_map/ppermute | solution.py:610
  121.9 4.7 %collective-permute-start.17 = (f32[4,8,128]{2,1,0:T(8,128)S(1)}, f32[4,8,128]{2,1,0:T(8,128)S(1)}, u32[]{:S(2)}, u32[]{:S(2)}) collective-permute-start(f32[4,8,128]{2,1,0:T(8,128)S(1)} %get-tuple-element.25), channel_id=1, source_target_pairs={{0,16},{8,24},{16,0},{24,8},{1,17},{9,25},{17,1},{25,9},{2,18},{10... | collective-permute-start | bytes 49160 | tf_op jit(solution)/shard_map/ppermute | solution.py:610
  122.6 5.6 %collective-permute-start.18 = (f32[4,8,128]{2,1,0:T(8,128)S(1)}, f32[4,8,128]{2,1,0:T(8,128)S(1)}, u32[]{:S(2)}, u32[]{:S(2)}) collective-permute-start(f32[4,8,128]{2,1,0:T(8,128)S(1)} %get-tuple-element.24), channel_id=1, source_target_pairs={{0,24},{8,16},{16,8},{24,0},{1,25},{9,17},{17,9},{25,1},{2,26},{10... | collective-permute-start | bytes 49160 | tf_op jit(solution)/shard_map/ppermute | solution.py:610
